TPU v7x, 256 devices: a whole 4x4x8 slice. The times are simulated.
256 devices in a mesh: orient: 16 (over y_lo, x, core), dom: 16 (over y_hi, z).
Axes of the slice: x: 4, y: 4 (y_hi: 2, y_lo: 2; y = y_hi * 2 + y_lo), z: 8, core: 2. Of those that a mesh axis runs over, the one named last changes fastest.
Arguments:
- images: bfloat16 [1536, 32768], P('dom'), may hold values from -256 to 256
- shifts: int32 [1536, 2], P('dom'), may hold values from -8 to 8
- slices: bfloat16 [4096, 32768], P('orient', 'dom'), may hold values from -1 to 1
- class_of: int32 [4096], P('orient'), may hold values from 0 to 7
- log_prior: float32 [8], replicated, may hold values from -3 to 0
Outputs:
- backprojected: float32 [4096, 32768], P('orient', 'dom')
- log_norm: float32 [1536], P('dom')
All inputs are finite; a program needn't handle non-finite values.
Results may differ from a plain program's by a relative error of at most 0.011.
Values may be sent and summed in bfloat16 or wider, within the bound.
No kernel may reach another device: no remote copies, remote signals or barrier semaphores. Data moves between devices by JAX's collectives and lax.ppermute only.
A program may use at most 128 MiB of HBM per device.

v0:
```python
import math

import jax
import jax.numpy as jnp
from jax import lax
from jax.sharding import PartitionSpec as P

BOX = 256


def shift_images(images, shifts):
    npix = images.shape[1] // 2
    coeff = jnp.arange(npix, dtype=jnp.int32)
    freq_x = coeff % 128
    freq_y = coeff // 128 - npix // 256
    turn = (freq_x[None, :] * shifts[:, 0:1] + freq_y[None, :] * shifts[:, 1:2]) % BOX
    angle = turn.astype(jnp.float32) * (2.0 * math.pi / BOX)
    cosine = jnp.cos(angle)
    sine = jnp.sin(angle)
    real_part = images[:, :npix].astype(jnp.float32)
    imag_part = images[:, npix:].astype(jnp.float32)
    new_real = real_part * cosine + imag_part * sine
    new_imag = imag_part * cosine - real_part * sine
    return jnp.concatenate([new_real, new_imag], axis=1).astype(jnp.bfloat16)


def normalize(score):
    local_peak = jnp.max(score, axis=1)
    peak = lax.pmax(local_peak, "orient")
    row_total = lax.psum(jnp.sum(jnp.exp(score - peak[:, None]), axis=1), "orient")
    weights = (jnp.exp(score - peak[:, None]) / row_total[:, None]).astype(jnp.bfloat16)
    return (weights, peak + jnp.log(row_total))


def on_device(images, shifts, slices, class_of, log_prior):
    shifted = shift_images(images, shifts)
    class_onehot = (
        class_of[:, None] == jnp.arange(log_prior.shape[0], dtype=jnp.int32)[None, :]
    ).astype(jnp.float32)
    prior = jnp.sum(class_onehot * log_prior[None, :], axis=1)
    contract_last = (((1,), (1,)), ((), ()))
    contract_first = (((0,), (0,)), ((), ()))
    columns = lax.all_to_all(shifted, "dom", split_axis=1, concat_axis=0, tiled=True)
    slice_float = slices.astype(jnp.float32)
    norm_part = jnp.sum(slice_float * slice_float, axis=1)
    image_rows = columns
    product = lax.dot_general(image_rows, slices, contract_last, preferred_element_type=jnp.float32)
    totals = lax.psum_scatter(
        product - 0.5 * norm_part[None, :], "dom", scatter_dimension=0, tiled=True
    )
    score = totals + prior[None, :]
    weights, log_norm = normalize(score)
    image_rows = columns
    projected = lax.dot_general(
        lax.all_gather(weights, "dom", axis=0, tiled=True),
        image_rows,
        contract_first,
        preferred_element_type=jnp.float32,
    )
    return (projected, log_norm)


def solution(mesh):
    placed = (P("dom", None), P("dom", None), P("orient", "dom"), P("orient"), P())
    return jax.shard_map(
        on_device,
        mesh=mesh,
        in_specs=placed,
        out_specs=(P("orient", "dom"), P("dom")),
        check_vma=False,
    )
```

profile of v0, /device:TPU:2, one launch (start us, length us, event | category | flops | bytes accessed | tf_op | source)
XLA Modules:
  0.0 522.9 jit_solution(242299288742540207)
XLA Ops:
  7.2 0.8 slice_bitcast_fusion.1
  7.9 28.8 %fusion.1 = (bf16[96,16384]{1,0:T(8,128)(2,1)S(1)}, bf16[96,16384]{1,0:T(8,128)(2,1)S(1)}) fusion(s32[96]{0:T(128)S(1)} %get-tuple-element.5, s32[16384]{0:T(1024)S(1)} %get-tuple-element.7, s32[96]{0:T(128)S(1)} %get-tuple-element.4, s32[16384]{0:T(1024)S(1)} %get-tuple-element.6, bf16[96,32768]{1,0:T(8,128)(2,1)} %param.5), kind=kLoop, calls=%fused_computation.8 | loop fusion | flops 40894464 | bytes 12714752 | tf_op jit(solution)/shard_map/convert.3
  36.8 2.0 copy.10
  38.7 2.0 copy.11
  40.7 1.1 pad_maximum_fusion
  41.8 6.1 %copy.9 = bf16[96,16,2048]{2,0,1:T(8,128)(2,1)} copy(bf16[96,16,2048]{2,1,0:T(8,128)(2,1)S(1)} %pad_maximum_fusion) | data formatting | bytes 12582912 | tf_op jit(solution)/shard_map/concatenate | solution.py:24
  47.9 0.0 copy-start
  47.9 11.4 %all-to-all-start = ((bf16[96,16,2048]{2,0,1:T(8,128)(2,1)}), bf16[96,16,2048]{2,0,1:T(8,128)(2,1)}, u32[]{:S(2)}, u32[]{:S(2)}) async-start(bf16[96,16,2048]{2,0,1:T(8,128)(2,1)} %copy.9), calls=%async_computation | async-start | bytes 12582912 | tf_op jit(solution)/shard_map/all_to_all | solution.py:43
  59.3 0.0 reduce-scatter.2.cloned.1.call-start
  59.4 0.0 copy-done
  59.4 0.3 multiply_reduce_fusion
  59.7 141.3 %all-to-all-done = bf16[96,16,2048]{2,0,1:T(8,128)(2,1)} async-done(((bf16[96,16,2048]{2,0,1:T(8,128)(2,1)}), bf16[96,16,2048]{2,0,1:T(8,128)(2,1)}, u32[]{:S(2)}, u32[]{:S(2)}) %all-to-all-start) | async-done | bytes 6291488 | tf_op jit(solution)/shard_map/all_to_all | solution.py:43
  201.0 0.0 copy-start.1
  201.0 0.0 copy-start.2
  201.0 5.8 %convolution_subtract_fusion = f32[1536,256]{1,0:T(8,128)} fusion(bf16[1536,2048]{1,0:T(8,128)(2,1)} %bitcast.3, bf16[256,2048]{1,0:T(8,128)(2,1)S(1)} %copy-done, f32[256]{0:T(256)S(1)} %broadcast_multiply_fusion), kind=kOutput, calls=%fused_computation.17 | convolution fusion | flops 1611005952 | bytes 8913920 | tf_op jit(solution)/shard_map/dot_general | solution.py:47
  206.8 0.0 reduce-scatter.2.cloned.1.call-update
  206.8 0.0 copy-done.1
  206.8 0.0 copy-done.2
  206.8 0.1 select_reduce_fusion
  206.9 206.6 %reduce-scatter.2.cloned.1.call-done = f32[96,256]{1,0:T(8,128)} async-done(((f32[1536,256]{1,0:T(8,128)}), f32[96,256]{1,0:T(8,128)}) %reduce-scatter.2.cloned.1.call-update) | async-done | bytes 98320 | tf_op jit(solution)/shard_map/reduce_scatter | solution.py:48
  413.5 1.0 add_reduce_fusion
  414.5 23.3 %pmax.7 = f32[96]{0:T(128)S(1)} all-reduce(f32[96]{0:T(128)S(1)} %add_reduce_fusion), channel_id=1, replica_groups=mesh['orient'=16,'dom'=16] {'orient'}, use_global_device_ids=true, to_apply=%region_4.5 | all-reduce | flops 96 | bytes 768 | tf_op jit(solution)/shard_map/pmax | solution.py:29
  437.9 1.1 fusion.9
  439.0 27.1 %psum.7 = f32[96]{0:T(128)S(1)} all-reduce(f32[96]{0:T(128)S(1)} %fusion.9), channel_id=1, replica_groups=mesh['orient'=16,'dom'=16] {'orient'}, use_global_device_ids=true, to_apply=%region_6.7 | all-reduce | flops 96 | bytes 768 | tf_op jit(solution)/shard_map/psum | solution.py:30
  466.1 0.5 log_add_fusion
  466.6 1.0 divide_convert_fusion
  467.6 42.5 %all_gather.3 = bf16[1536,256]{1,0:T(8,128)(2,1)S(1)} all-gather(bf16[96,256]{1,0:T(8,128)(2,1)S(1)} %divide_convert_fusion), channel_id=1, replica_groups=mesh['orient'=16,'dom'=16] {'dom'}, dimensions={0}, use_global_device_ids=true | all-gather | bytes 835584 | tf_op jit(solution)/shard_map/all_gather | solution.py:55
  510.1 5.9 %fusion.16 = f32[256,2048]{1,0:T(8,128)} fusion(bf16[1536,256]{1,0:T(8,128)(2,1)S(1)} %all_gather.3, bf16[1536,2048]{1,0:T(8,128)(2,1)} %bitcast.3), kind=kOutput, calls=%fused_computation.40 | convolution fusion | flops 1610612736 | bytes 9175040 | tf_op jit(solution)/shard_map/dot_general | solution.py:54
  (2 shorter events, 0.0 us)
Async XLA Ops:
  47.9 11.4 %copy-start = (bf16[256,2048]{1,0:T(8,128)(2,1)S(1)}, bf16[256,2048]{1,0:T(8,128)(2,1)}, u32[]{:S(2)}) copy-start(bf16[256,2048]{1,0:T(8,128)(2,1)} %param.7) | copy-start | bytes 3145732
  47.9 153.0 %all-to-all-start = ((bf16[96,16,2048]{2,0,1:T(8,128)(2,1)}), bf16[96,16,2048]{2,0,1:T(8,128)(2,1)}, u32[]{:S(2)}, u32[]{:S(2)}) async-start(bf16[96,16,2048]{2,0,1:T(8,128)(2,1)} %copy.9), calls=%async_computation | async-start | bytes 12582912 | tf_op jit(solution)/shard_map/all_to_all | solution.py:43
  59.3 354.2 %reduce-scatter.2.cloned.1.call-start = ((), (), s32[]{:S(2)}) async-start(), calls=%async_computation.2 | async-start | bytes 1671168 | tf_op jit(solution)/shard_map/reduce_scatter | solution.py:48
  201.0 5.8 %copy-start.1 = (s32[256]{0:T(256)S(1)}, s32[256]{0:T(256)}, u32[]{:S(2)}) copy-start(s32[256]{0:T(256)} %param.8) | copy-start | bytes 3076
  201.0 5.8 %copy-start.2 = (f32[8]{0:T(128)S(1)}, f32[8]{0:T(128)}, u32[]{:S(2)}) copy-start(f32[8]{0:T(128)} %param.9) | copy-start | bytes 100
Sparse Core Ops, SparseCore 0:
  206.9 206.5 reduce-scatter.1
where the time goes:
time: 526 us; the launch traced here: 523 us
  waiting for transfers between devices  348 us (66%)
  blocking collectives  93 us (18%)
  other arithmetic  33.9 us (6%)
  between operations  14.1 us (3%)
  matrix products  11.7 us (2%)
  starting transfers between devices  11.4 us (2%)
  local copies, waits for them, and re-layouts  10.8 us (2%)
    reduce_scatter x1, waiting for transfers between devices, on_device(): lax.psum_scatter(product - 0.5 * norm_part[None, :], 'dom', scatter_dimen...  207 us
    all_to_all x1, waiting for transfers between devices, on_device(): lax.all_to_all(shifted, 'dom', split_axis=1, concat_axis=0, tiled=True)  141 us
    all_gather x1, blocking collectives, on_device(): lax.all_gather(weights, 'dom', axis=0, tiled=True)  42.5 us
    another operation x1, other arithmetic  28.8 us
    psum x1, blocking collectives, normalize(): lax.psum(jnp.sum(jnp.exp(score - peak[:, None]), axis=1), 'orient')  27.1 us
    pmax x1, blocking collectives, normalize(): peak = lax.pmax(local_peak, 'orient')  23.3 us
    all_to_all x1, starting transfers between devices, on_device(): lax.all_to_all(shifted, 'dom', split_axis=1, concat_axis=0, tiled=True)  11.4 us
  transfers between devices with their start and end apart: 2, of which 2 were waited for; matrix products, arithmetic and copies ran while one was open for 0% of the time, Pallas kernels for 0%

commit v1 on v0

v1 whole, which is shorter than its diff:
```python
import functools
import math

import jax
import jax.numpy as jnp
from jax import lax
from jax.experimental import pallas as pl
from jax.experimental.pallas import tpu as pltpu
from jax.sharding import PartitionSpec as P

BOX = 256
LANES = 128
MIB = 1 << 20


def shift_kernel(parts, first, shifts, real, imag, out, cos_x, sin_x, cos_y, sin_y):
    step = pl.program_id(0)
    rows = real.shape[0]

    @pl.when(step == 0)
    def _():
        lane = lax.broadcasted_iota(jnp.int32, (rows, LANES), 1)
        turn_x = (lane * shifts[:, 0:1]) & (BOX - 1)
        turn_y = ((lane * parts + first[0] - first[1]) * shifts[:, 1:2]) & (BOX - 1)
        angle_x = turn_x.astype(jnp.float32) * (2.0 * math.pi / BOX)
        angle_y = turn_y.astype(jnp.float32) * (2.0 * math.pi / BOX)
        cos_x[...] = jnp.cos(angle_x)
        sin_x[...] = jnp.sin(angle_x)
        cos_y[...] = jnp.cos(angle_y)
        sin_y[...] = jnp.sin(angle_y)

    lane = lax.broadcasted_iota(jnp.int32, (rows, LANES), 1)
    cy = jnp.sum(jnp.where(lane == step, cos_y[...], 0.0), axis=1, keepdims=True)
    sy = jnp.sum(jnp.where(lane == step, sin_y[...], 0.0), axis=1, keepdims=True)
    cx = cos_x[...]
    sx = sin_x[...]
    cosine = cx * cy - sx * sy
    sine = sx * cy + cx * sy
    re = real[...].astype(jnp.float32)
    im = imag[...].astype(jnp.float32)
    out[0, 0] = (re * cosine + im * sine).astype(jnp.bfloat16)
    out[1, 0] = (im * cosine - re * sine).astype(jnp.bfloat16)


def shift_part(images, shifts, index, doms, parts):
    rows, width = images.shape
    half = doms // 2
    first = jnp.stack([index, jnp.int32(width // 2 // 256)]).astype(jnp.int32)
    out = pl.pallas_call(
        functools.partial(shift_kernel, parts),
        out_shape=jax.ShapeDtypeStruct((2, half, rows, LANES), jnp.bfloat16),
        grid_spec=pltpu.PrefetchScalarGridSpec(
            num_scalar_prefetch=1,
            grid=(half,),
            in_specs=[
                pl.BlockSpec((rows, 2), lambda i, first: (0, 0)),
                pl.BlockSpec((rows, LANES), lambda i, first: (0, i * parts + first[0])),
                pl.BlockSpec((rows, LANES), lambda i, first: (0, (i + half) * parts + first[0])),
            ],
            out_specs=pl.BlockSpec((2, 1, rows, LANES), lambda i, first: (0, i, 0, 0)),
            scratch_shapes=[pltpu.VMEM((rows, LANES), jnp.float32)] * 4,
        ),
        name="shift",
    )(first, shifts, images, images)
    return out.reshape(doms, rows, LANES)


def score_kernel(columns, slices, bias, out):
    block = jnp.concatenate([columns[p] for p in range(columns.shape[0])], axis=1)
    product = lax.dot_general(block, slices[...], (((1,), (1,)), ((), ())), preferred_element_type=jnp.float32)
    out[...] = product + bias[...]


def partial_score(columns, slices, bias, steps=4):
    parts, images, lanes = columns.shape
    rows = images // steps
    oris = slices.shape[0]
    return pl.pallas_call(
        score_kernel,
        out_shape=jax.ShapeDtypeStruct((images, oris), jnp.float32),
        grid=(steps,),
        in_specs=[
            pl.BlockSpec((parts, rows, lanes), lambda i: (0, i, 0)),
            pl.BlockSpec(slices.shape, lambda i: (0, 0)),
            pl.BlockSpec((1, oris), lambda i: (0, 0)),
        ],
        out_specs=pl.BlockSpec((rows, oris), lambda i: (i, 0)),
        compiler_params=pltpu.CompilerParams(vmem_limit_bytes=32 * MIB),
        name="score",
    )(columns, slices, bias)


def to_row(column):
    rows = column.shape[0]
    wide = jnp.broadcast_to(column, (rows, LANES))
    square = jnp.concatenate([wide, jnp.zeros((LANES - rows, LANES), jnp.float32)], axis=0)
    return jnp.transpose(square)[0:1]


def to_column(row, rows):
    return jnp.transpose(jnp.broadcast_to(row, (LANES, LANES)))[:rows, 0:1]


def total_kernel(pieces, score, stats):
    total = pieces[0]
    for d in range(1, pieces.shape[0]):
        total = total + pieces[d]
    score[...] = total
    peak = jnp.max(total, axis=1, keepdims=True)
    mass = jnp.sum(jnp.exp(total - peak), axis=1, keepdims=True)
    both = jnp.concatenate([to_row(peak), to_row(mass), jnp.zeros((6, LANES), jnp.float32)], axis=0)
    stats[...] = jnp.broadcast_to(both[None], stats.shape)


def total_score(pieces, parts):
    doms, rows, oris = pieces.shape
    return pl.pallas_call(
        total_kernel,
        out_shape=(
            jax.ShapeDtypeStruct((rows, oris), jnp.float32),
            jax.ShapeDtypeStruct((parts, 8, LANES), jnp.float32),
        ),
        compiler_params=pltpu.CompilerParams(vmem_limit_bytes=32 * MIB),
        name="total",
    )(pieces)


def weight_kernel(score, stats, weights, log_norm):
    rows = score.shape[0]
    peaks = stats[:, 0, :]
    masses = stats[:, 1, :]
    peak = jnp.max(peaks, axis=0, keepdims=True)
    total = jnp.sum(masses * jnp.exp(peaks - peak), axis=0, keepdims=True)
    used = lax.broadcasted_iota(jnp.int32, total.shape, 1) < rows
    total = jnp.where(used, total, 1.0)
    log_norm[...] = peak + jnp.log(total)
    chosen = jnp.exp(score[...] - to_column(peak, rows)) / to_column(total, rows)
    weights[...] = jnp.broadcast_to(chosen.astype(jnp.bfloat16)[None], weights.shape)


def weigh(score, stats, doms):
    rows, oris = score.shape
    return pl.pallas_call(
        weight_kernel,
        out_shape=(
            jax.ShapeDtypeStruct((doms, rows, oris), jnp.bfloat16),
            jax.ShapeDtypeStruct((1, LANES), jnp.float32),
        ),
        compiler_params=pltpu.CompilerParams(vmem_limit_bytes=32 * MIB),
        name="weigh",
    )(score, stats)


def project_kernel(weights, columns, out):
    block = jnp.concatenate([columns[p] for p in range(columns.shape[0])], axis=1)
    out[...] = lax.dot_general(
        weights[...], block, (((0,), (0,)), ((), ())), preferred_element_type=jnp.float32
    )


def project(weights, columns, steps=4):
    parts, images, lanes = columns.shape
    oris = weights.shape[1]
    take = parts // steps
    return pl.pallas_call(
        project_kernel,
        out_shape=jax.ShapeDtypeStruct((oris, parts * lanes), jnp.float32),
        grid=(steps,),
        in_specs=[
            pl.BlockSpec((images, oris), lambda i: (0, 0)),
            pl.BlockSpec((take, images, lanes), lambda i: (i, 0, 0)),
        ],
        out_specs=pl.BlockSpec((oris, take * lanes), lambda i: (0, i)),
        compiler_params=pltpu.CompilerParams(vmem_limit_bytes=32 * MIB),
        name="project",
    )(weights, columns)


def on_device(images, shifts, slices, class_of, log_prior, *, doms, parts):
    rows = images.shape[0]
    oris = slices.shape[0]
    own = shift_part(images, shifts, lax.axis_index("orient"), doms, parts)
    mine = lax.all_to_all(own, "dom", 0, 0).reshape(doms * rows, LANES)
    columns = lax.all_gather(mine, "orient")

    slice_float = slices.astype(jnp.float32)
    onehot = class_of[:, None] == jnp.arange(log_prior.shape[0], dtype=jnp.int32)[None, :]
    prior = jnp.sum(jnp.where(onehot, log_prior[None, :], 0.0), axis=1)
    bias = jnp.where(lax.axis_index("dom") == 0, prior, 0.0) - 0.5 * jnp.sum(slice_float * slice_float, axis=1)

    partial = partial_score(columns, slices, bias[None, :])
    pieces = lax.all_to_all(partial.reshape(doms, rows, oris), "dom", 0, 0)
    score, stats = total_score(pieces, parts)
    stats = lax.all_to_all(stats, "orient", 0, 0)
    copies, log_norm = weigh(score, stats, doms)
    weights = lax.all_to_all(copies, "dom", 0, 0).reshape(doms * rows, oris)
    return project(weights, columns), log_norm[0, :rows]


def solution(mesh):
    placed = (P("dom", None), P("dom", None), P("orient", "dom"), P("orient"), P())
    return jax.shard_map(
        functools.partial(on_device, doms=mesh.shape["dom"], parts=mesh.shape["orient"]),
        mesh=mesh,
        in_specs=placed,
        out_specs=(P("orient", "dom"), P("dom")),
        check_vma=False,
    )
```

time: 526 us -> 190 us (0.36)
  waiting for transfers between devices: 348 us -> 63.7 us
  other arithmetic: 33.9 us -> 1.01 us
  Pallas kernels: 0 us -> 13.8 us
  matrix products: 11.7 us -> 0 us
  blocking collectives: 93 us -> 83.8 us
  starting transfers between devices: 11.4 us -> 5.45 us
    reduce_scatter x1 -> x0, waiting for transfers between devices: 207 us -> none  [on_device(): lax.psum_scatter(product - 0.5 * norm_part[None, :], 'dom', scatter_dimen...]
    all_to_all x1, waiting for transfers between devices: 141 us -> 22.7 us  [on_device(): weights = lax.all_to_all(copies, 'dom', 0, 0).reshape(doms * rows, oris)]
    all_to_all x0 -> x3, blocking collectives: none -> 83.8 us  [the longest x1 49.2 us: on_device(): pieces = lax.all_to_all(partial.reshape(doms, rows, oris), 'dom', 0, 0)]
    all_gather x1 -> x0, blocking collectives: 42.5 us -> none  [on_device(): lax.all_gather(weights, 'dom', axis=0, tiled=True)]
    all_gather x0 -> x1, waiting for transfers between devices: none -> 41 us  [on_device(): columns = lax.all_gather(mine, 'orient')]
    another operation x1, other arithmetic: 28.8 us -> 0.63 us  [shift_part(): first = jnp.stack([index, jnp.int32(width // 2 // 256)]).astype(jnp.int32)]
    psum x1 -> x0, blocking collectives: 27.1 us -> none  [normalize(): lax.psum(jnp.sum(jnp.exp(score - peak[:, None]), axis=1), 'orient')]
    pmax x1 -> x0, blocking collectives: 23.3 us -> none  [normalize(): peak = lax.pmax(local_peak, 'orient')]
where the time goes in v1:
time: 190 us; the launch traced here: 189 us
  blocking collectives  83.8 us (44%)
  waiting for transfers between devices  63.7 us (34%)
  between operations  14.1 us (7%)
  Pallas kernels  13.8 us (7%)
  local copies, waits for them, and re-layouts  7.48 us (4%)
  starting transfers between devices  5.45 us (3%)
    all_to_all x1, blocking collectives, on_device(): pieces = lax.all_to_all(partial.reshape(doms, rows, oris), 'dom', 0, 0)  49.2 us
    all_gather x1, waiting for transfers between devices, on_device(): columns = lax.all_gather(mine, 'orient')  41 us
    all_to_all x1, blocking collectives, on_device(): mine = lax.all_to_all(own, 'dom', 0, 0).reshape(doms * rows, LANES)  25.4 us
    all_to_all x1, waiting for transfers between devices, on_device(): weights = lax.all_to_all(copies, 'dom', 0, 0).reshape(doms * rows, oris)  22.7 us
    all_to_all x1, blocking collectives, on_device(): stats = lax.all_to_all(stats, 'orient', 0, 0)  9.2 us
    unnamed x11, local copies, waits for them, and re-layouts  6.97 us
    pallas_call x1, Pallas kernels, shift_part(): pl.pallas_call(functools.partial(shift_kernel, parts), out_shape=jax.Shap...  6.13 us
    all_to_all x1, starting transfers between devices, on_device(): weights = lax.all_to_all(copies, 'dom', 0, 0).reshape(doms * rows, oris)  5.41 us
  transfers between devices with their start and end apart: 2, of which 2 were waited for; matrix products, arithmetic and copies ran while one was open for 0% of the time, Pallas kernels for 0%

profile of v1, /device:TPU:2, one launch (start us, length us, event | category | flops | bytes accessed | tf_op | source)
XLA Modules:
  0.0 189.4 jit_solution(2403918728832601057)
XLA Ops:
  7.2 0.0 all-gather.2.cloned.1.call-start
  7.2 1.4 copy.9.shifts
  8.6 0.6 pad_add_fusion.first
  9.2 0.0 copy-start.3
  9.2 0.0 copy-start.4
  9.2 0.0 copy-start.2
  9.2 6.1 %shift.1 = bf16[2,8,96,128]{3,2,1,0:T(8,128)(2,1)} custom-call(s32[2]{0:T(128)} %pad_add_fusion.first, s32[96,2]{1,0:T(8,128)} %copy.9.shifts, bf16[96,32768]{1,0:T(8,128)(2,1)} %imag.1, bf16[96,32768]{1,0:T(8,128)(2,1)} %imag.1), custom_call_target="tpu_custom_call" | custom-call | tf_op jit(solution)/shard_map/shift/pallas_call | solution.py:49
  15.4 25.4 %all_to_all.20 = bf16[16,96,128]{2,1,0:T(8,128)(2,1)} all-to-all(bf16[16,96,128]{2,1,0:T(8,128)(2,1)} %bitcast.11), channel_id=1, replica_groups=mesh['orient'=16,'dom'=16] {'dom'}, dimensions={0} | all-to-all | bytes 786432 | tf_op jit(solution)/shard_map/all_to_all | solution.py:183
  40.8 0.0 all-gather.2.cloned.1.call-update
  40.8 0.0 copy-done.3
  40.8 0.0 copy-done.4
  40.9 0.1 select_reduce_fusion
  40.9 0.0 copy-done.2
  40.9 0.3 multiply_reduce_fusion
  41.2 41.0 %all-gather.2.cloned.1.call-done.columns = bf16[16,1536,128]{2,1,0:T(8,128)(2,1)} async-done(((bf16[1,1536,128]{2,1,0:T(8,128)(2,1)}), bf16[16,1536,128]{2,1,0:T(8,128)(2,1)}) %all-gather.2.cloned.1.call-update) | async-done | bytes 6291472 | tf_op jit(solution)/shard_map/all_gather | solution.py:184
  82.3 0.0 copy-start
  82.3 2.8 %copy-done = bf16[16,1536,128]{2,1,0:T(8,128)(2,1)S(1)} copy-done((bf16[16,1536,128]{2,1,0:T(8,128)(2,1)S(1)}, bf16[16,1536,128]{2,1,0:T(8,128)(2,1)}, u32[]{:S(2)}) %copy-start) | copy-done | bytes 6291480
  85.0 2.9 %score.1 = f32[1536,256]{1,0:T(8,128)S(1)} custom-call(bf16[16,1536,128]{2,1,0:T(8,128)(2,1)S(1)} %copy-done, bf16[256,2048]{1,0:T(8,128)(2,1)S(1)} %copy-done.2, f32[1,256]{1,0:T(1,128)S(1)} %bitcast.10), custom_call_target="tpu_custom_call" | custom-call | tf_op jit(solution)/shard_map/score/pallas_call | solution.py:78
  87.9 49.2 %all_to_all.21.pieces = f32[16,96,256]{2,1,0:T(8,128)S(1)} all-to-all(f32[16,96,256]{2,1,0:T(8,128)S(1)} %bitcast.8), channel_id=1, replica_groups=mesh['orient'=16,'dom'=16] {'dom'}, dimensions={0} | all-to-all | bytes 3145728 | tf_op jit(solution)/shard_map/all_to_all | solution.py:192
  137.1 0.3 total.1
  137.4 9.2 %all_to_all.22.stats = f32[16,8,128]{2,1,0:T(8,128)S(1)} all-to-all(f32[16,8,128]{2,1,0:T(8,128)S(1)} %get-tuple-element.7), channel_id=1, replica_groups=mesh['orient'=16,'dom'=16] {'orient'}, dimensions={0} | all-to-all | bytes 131072 | tf_op jit(solution)/shard_map/all_to_all | solution.py:194
  146.6 1.1 weigh.1
  147.7 5.4 %all-to-all-start.3 = ((bf16[16,96,256]{2,1,0:T(8,128)(2,1)}), bf16[16,96,256]{2,1,0:T(8,128)(2,1)S(1)}, u32[]{:S(2)}, u32[]{:S(2)}) async-start(bf16[16,96,256]{2,1,0:T(8,128)(2,1)} %get-tuple-element.8), calls=%async_computation.3 | async-start | bytes 1572864 | tf_op jit(solution)/shard_map/all_to_all | solution.py:196
  153.1 0.5 slice_bitcast_fusion
  153.6 22.7 %all-to-all-done.3 = bf16[16,96,256]{2,1,0:T(8,128)(2,1)S(1)} async-done(((bf16[16,96,256]{2,1,0:T(8,128)(2,1)}), bf16[16,96,256]{2,1,0:T(8,128)(2,1)S(1)}, u32[]{:S(2)}, u32[]{:S(2)}) %all-to-all-start.3) | async-done | bytes 786464 | tf_op jit(solution)/shard_map/all_to_all | solution.py:196
  176.3 0.0 copy-start.1
  176.3 2.8 %copy-done.1 = bf16[16,1536,128]{2,1,0:T(8,128)(2,1)S(1)} copy-done((bf16[16,1536,128]{2,1,0:T(8,128)(2,1)S(1)}, bf16[16,1536,128]{2,1,0:T(8,128)(2,1)}, u32[]{:S(2)}) %copy-start.1) | copy-done | bytes 6291480
  179.1 3.4 %project.1 = f32[256,2048]{1,0:T(8,128)} custom-call(bf16[1536,256]{1,0:T(8,128)(2,1)S(1)} %bitcast.9, bf16[16,1536,128]{2,1,0:T(8,128)(2,1)S(1)} %copy-done.1), custom_call_target="tpu_custom_call" | custom-call | tf_op jit(solution)/shard_map/project/pallas_call | solution.py:165
  (1 shorter events, 0.0 us)
Async XLA Ops:
  7.2 75.1 %all-gather.2.cloned.1.call-start = ((), (), s32[]{:S(2)}) async-start(), calls=%async_computation.4 | async-start | bytes 6684672 | tf_op jit(solution)/shard_map/all_gather | solution.py:184
  9.2 31.6 %copy-start.3 = (s32[256]{0:T(256)S(1)}, s32[256]{0:T(256)}, u32[]{:S(2)}) copy-start(s32[256]{0:T(256)} %param.8) | copy-start | bytes 3076
  9.2 31.6 %copy-start.4 = (f32[8]{0:T(128)S(1)}, f32[8]{0:T(128)}, u32[]{:S(2)}) copy-start(f32[8]{0:T(128)} %param.9) | copy-start | bytes 100
  9.2 31.7 %copy-start.2 = (bf16[256,2048]{1,0:T(8,128)(2,1)S(1)}, bf16[256,2048]{1,0:T(8,128)(2,1)}, u32[]{:S(2)}) copy-start(bf16[256,2048]{1,0:T(8,128)(2,1)} %slices.1) | copy-start | bytes 3145732
  82.3 2.8 %copy-start = (bf16[16,1536,128]{2,1,0:T(8,128)(2,1)S(1)}, bf16[16,1536,128]{2,1,0:T(8,128)(2,1)}, u32[]{:S(2)}) copy-start(bf16[16,1536,128]{2,1,0:T(8,128)(2,1)} %all-gather.2.cloned.1.call-done.columns) | copy-start | bytes 18874372
  147.7 28.6 %all-to-all-start.3 = ((bf16[16,96,256]{2,1,0:T(8,128)(2,1)}), bf16[16,96,256]{2,1,0:T(8,128)(2,1)S(1)}, u32[]{:S(2)}, u32[]{:S(2)}) async-start(bf16[16,96,256]{2,1,0:T(8,128)(2,1)} %get-tuple-element.8), calls=%async_computation.3 | async-start | bytes 1572864 | tf_op jit(solution)/shard_map/all_to_all | solution.py:196
  176.3 2.8 %copy-start.1 = (bf16[16,1536,128]{2,1,0:T(8,128)(2,1)S(1)}, bf16[16,1536,128]{2,1,0:T(8,128)(2,1)}, u32[]{:S(2)}) copy-start(bf16[16,1536,128]{2,1,0:T(8,128)(2,1)} %all-gather.2.cloned.1.call-done.columns) | copy-start | bytes 18874372
Sparse Core Ops, SparseCore 0:
  40.9 41.2 all-gather.1

commit v2 on v1

v2 whole, which is shorter than its diff:
```python
import functools
import math

import jax
import jax.numpy as jnp
from jax import lax
from jax.experimental import pallas as pl
from jax.experimental.pallas import tpu as pltpu
from jax.sharding import PartitionSpec as P

BOX = 256
LANES = 128
WIDE = 256
MIB = 1 << 20

ORI = 16
DOM = 16
RING = 4
HALF = DOM // 2
Z_GROUPS = [list(range(HALF)), list(range(HALF, DOM))]
CORE = [(i, i ^ 1) for i in range(ORI)]
Y_LOW = [(i, i ^ 8) for i in range(ORI)]
Y_HIGH = [(i, i ^ 8) for i in range(DOM)]


def along_x(by):
    return [(i, i // 8 * 8 + (i // 2 + by) % RING * 2 + i % 2) for i in range(ORI)]


def shift_kernel(place, shifts, real, imag, out, cos_x, sin_x, cos_y, sin_y):
    step = pl.program_id(0)
    rows = real.shape[0]
    lane = lax.broadcasted_iota(jnp.int32, (rows, LANES), 1)

    @pl.when(step == 0)
    def _():
        total = shifts.shape[1]
        image = lax.broadcasted_iota(jnp.int32, (rows, total), 0) + place[1] * rows
        own = image == lax.broadcasted_iota(jnp.int32, (rows, total), 1)
        by_x = jnp.sum(jnp.where(own, shifts[0:1, :], 0), axis=1, keepdims=True)
        by_y = jnp.sum(jnp.where(own, shifts[1:2, :], 0), axis=1, keepdims=True)
        freq_y = (lane // 2) * 16 + lane % 2 + 2 * place[0] - place[2]
        angle_x = ((lane * by_x) & (BOX - 1)).astype(jnp.float32) * (2.0 * math.pi / BOX)
        angle_y = ((freq_y * by_y) & (BOX - 1)).astype(jnp.float32) * (2.0 * math.pi / BOX)
        cos_x[...] = jnp.cos(angle_x)
        sin_x[...] = jnp.sin(angle_x)
        cos_y[...] = jnp.cos(angle_y)
        sin_y[...] = jnp.sin(angle_y)

    cx = cos_x[...]
    sx = sin_x[...]
    for part in range(2):
        pick = lane == 2 * step + part
        cy = jnp.sum(jnp.where(pick, cos_y[...], 0.0), axis=1, keepdims=True)
        sy = jnp.sum(jnp.where(pick, sin_y[...], 0.0), axis=1, keepdims=True)
        cosine = cx * cy - sx * sy
        sine = sx * cy + cx * sy
        here = slice(part * LANES, (part + 1) * LANES)
        re = real[:, here].astype(jnp.float32)
        im = imag[:, here].astype(jnp.float32)
        out[0, 0, :, here] = (re * cosine + im * sine).astype(jnp.bfloat16)
        out[0, 1, :, here] = (im * cosine - re * sine).astype(jnp.bfloat16)


def shift_part(images, shifts, share, core):
    rows, width = images.shape
    rows = rows // 2
    shares = width // DOM // WIDE
    place = jnp.stack([share, core, jnp.int32(width // 2 // 256)]).astype(jnp.int32)
    return pl.pallas_call(
        shift_kernel,
        out_shape=jax.ShapeDtypeStruct((HALF, 2, rows, WIDE), jnp.bfloat16),
        grid_spec=pltpu.PrefetchScalarGridSpec(
            num_scalar_prefetch=1,
            grid=(HALF,),
            in_specs=[
                pl.BlockSpec(shifts.shape, lambda i, place: (0, 0)),
                pl.BlockSpec((rows, WIDE), lambda i, place: (place[1], i * shares + place[0])),
                pl.BlockSpec((rows, WIDE), lambda i, place: (place[1], (i + HALF) * shares + place[0])),
            ],
            out_specs=pl.BlockSpec((1, 2, rows, WIDE), lambda i, place: (i, 0, 0, 0)),
            scratch_shapes=[pltpu.VMEM((rows, LANES), jnp.float32)] * 4,
        ),
        name="shift",
    )(place, shifts, images, images)


def gather_shares(own):
    send = lambda block, perm: lax.ppermute(block, "orient", perm)
    low = send(own, along_x(1))
    high = send(own, along_x(-1))
    across = send(own, Y_LOW)
    across_high = send(high, Y_LOW)
    across_low = send(across, along_x(1))
    far = send(high, along_x(-1))
    cut = own.shape[0] // 2
    first = send(across_high[:cut], along_x(-1))
    second = send(across_low[cut:], along_x(1))
    return own, low, high, across, across_high, across_low, far, first, second


def score_kernel(place, own, low, high, across, across_high, across_low, far, first, second,
                 s_own, s_hi, s_core, s_both, bias, out, keep, give):
    step = pl.program_id(0)
    mine = place[0]
    rows = out.shape[0]
    wide = own.shape[-1]
    blocks = [own, low, high, across, across_high, across_low, far]
    for k, block in enumerate(blocks):
        share = place[1 + k]
        keep[share] = block[:, mine].reshape(rows, wide)
        give[share] = block[:, 1 - mine].reshape(rows, wide)
    share = place[1 + len(blocks)]

    @pl.when(step == 0)
    def _():
        keep[share] = first[:, mine].reshape(rows, wide)
        give[share] = first[:, 1 - mine].reshape(rows, wide)

    @pl.when(step == 1)
    def _():
        keep[share] = second[:, mine].reshape(rows, wide)
        give[share] = second[:, 1 - mine].reshape(rows, wide)

    shares = keep.shape[0]
    kept = jnp.concatenate([keep[s] for s in range(shares)], axis=1)
    given = jnp.concatenate([give[s] for s in range(shares)], axis=1)
    dims = (((1,), (1,)), ((), ()))
    oris = s_own.shape[0]
    for at, (near, other) in enumerate(((s_own, s_hi), (s_core, s_both))):
        product = lax.dot_general(kept, near[...], dims, preferred_element_type=jnp.float32)
        product += lax.dot_general(given, other[...], dims, preferred_element_type=jnp.float32)
        here = slice(at * oris, (at + 1) * oris)
        out[:, here] = product + bias[:, here]


def partial_score(place, blocks, slices, bias, steps=2):
    zs, _, rows, wide = blocks[0].shape
    images = zs * rows
    take = zs // steps
    oris, width = slices[0].shape
    shares = width // wide
    whole = lambda i, place: (i, 0, 0, 0)
    fixed = lambda i, place: (0, 0, 0, 0)
    flat = lambda i, place: (0, 0)
    return pl.pallas_call(
        score_kernel,
        out_shape=(
            jax.ShapeDtypeStruct((images, 2 * oris), jnp.float32),
            jax.ShapeDtypeStruct((shares, images, wide), jnp.bfloat16),
            jax.ShapeDtypeStruct((shares, images, wide), jnp.bfloat16),
        ),
        grid_spec=pltpu.PrefetchScalarGridSpec(
            num_scalar_prefetch=1,
            grid=(steps,),
            in_specs=[pl.BlockSpec((take, 2, rows, wide), whole)] * 7
            + [pl.BlockSpec((take, 2, rows, wide), fixed)] * 2
            + [pl.BlockSpec((oris, width), flat)] * 4
            + [pl.BlockSpec((1, 2 * oris), flat)],
            out_specs=[
                pl.BlockSpec((take * rows, 2 * oris), lambda i, place: (i, 0)),
                pl.BlockSpec((shares, take * rows, wide), lambda i, place: (0, i, 0)),
                pl.BlockSpec((shares, take * rows, wide), lambda i, place: (0, i, 0)),
            ],
        ),
        compiler_params=pltpu.CompilerParams(vmem_limit_bytes=56 * MIB),
        name="score",
    )(place, *blocks, *slices, bias)


def to_row(column):
    rows = column.shape[0]
    wide = jnp.broadcast_to(column, (rows, LANES))
    square = jnp.concatenate([wide, jnp.zeros((LANES - rows, LANES), jnp.float32)], axis=0)
    return jnp.transpose(square)[0:1]


def to_column(row, rows):
    return jnp.transpose(jnp.broadcast_to(row, (LANES, LANES)))[:rows, 0:1]


def total_kernel(pieces, near, other, stats):
    total = pieces[0]
    for d in range(1, pieces.shape[0]):
        total = total + pieces[d]
    oris = near.shape[1]
    near[...] = total[:, :oris]
    other[...] = total[:, oris:]
    peak = jnp.max(total, axis=1, keepdims=True)
    mass = jnp.sum(jnp.exp(total - peak), axis=1, keepdims=True)
    both = jnp.concatenate([to_row(peak), to_row(mass), jnp.zeros((6, LANES), jnp.float32)], axis=0)
    stats[...] = jnp.broadcast_to(both[None], stats.shape)


def total_score(pieces):
    _, rows, oris = pieces.shape
    return pl.pallas_call(
        total_kernel,
        out_shape=(
            jax.ShapeDtypeStruct((rows, oris // 2), jnp.float32),
            jax.ShapeDtypeStruct((rows, oris // 2), jnp.float32),
            jax.ShapeDtypeStruct((ORI, 8, LANES), jnp.float32),
        ),
        compiler_params=pltpu.CompilerParams(vmem_limit_bytes=32 * MIB),
        name="total",
    )(pieces)


def weight_kernel(place, near, came, stats, weights, log_norm):
    rows = near.shape[0]
    core = place[0]
    used = lax.broadcasted_iota(jnp.int32, (1, LANES), 1) < rows
    peak, total = [], []
    for c in range(2):
        peaks = jnp.concatenate([stats[p, 0:1, :] for p in range(c, ORI, 2)], axis=0)
        masses = jnp.concatenate([stats[p, 1:2, :] for p in range(c, ORI, 2)], axis=0)
        top = jnp.max(peaks, axis=0, keepdims=True)
        mass = jnp.sum(masses * jnp.exp(peaks - top), axis=0, keepdims=True)
        peak.append(top)
        total.append(jnp.where(used, mass, 1.0))
        log_norm[c : c + 1, :] = top + jnp.log(total[c])
    for at, part in ((core, near), (1 - core, came)):
        top = to_column(jnp.where(at == 0, peak[0], peak[1]), rows)
        mass = to_column(jnp.where(at == 0, total[0], total[1]), rows)
        chosen = (jnp.exp(part[...] - top) / mass).astype(jnp.bfloat16)
        here = pl.ds(pl.multiple_of(at * rows, 16), rows)
        weights[:, here, :] = jnp.broadcast_to(chosen[None], (weights.shape[0], *chosen.shape))


def weigh(place, near, came, stats):
    rows, oris = near.shape
    vmem = pl.BlockSpec(memory_space=pltpu.VMEM)
    return pl.pallas_call(
        weight_kernel,
        out_shape=(
            jax.ShapeDtypeStruct((DOM, 2 * rows, oris), jnp.bfloat16),
            jax.ShapeDtypeStruct((2, LANES), jnp.float32),
        ),
        in_specs=[pl.BlockSpec(memory_space=pltpu.SMEM), vmem, vmem, vmem],
        out_specs=(vmem, vmem),
        compiler_params=pltpu.CompilerParams(vmem_limit_bytes=32 * MIB),
        name="weigh",
    )(place, near, came, stats)


def project_kernel(place, weights, keep, from_core, from_hi, from_both, out, turned):
    rows = weights.shape[1] // 2
    images = keep.shape[1]

    @pl.when(pl.program_id(0) == 0)
    def _():
        for at in range(4):
            hi = place[0] if at < 2 else 1 - place[0]
            core = place[1] if at % 2 == 0 else 1 - place[1]
            part = weights[pl.ds(hi * HALF, HALF), pl.ds(pl.multiple_of(core * rows, 16), rows), :]
            turned[:, at * images : (at + 1) * images] = jnp.transpose(part.reshape(images, part.shape[-1]))

    block = jnp.concatenate([keep[0], from_core[0], from_hi[0], from_both[0]], axis=0)
    out[...] = jnp.dot(turned[...], block, preferred_element_type=jnp.float32)


def project(place, weights, columns):
    shares, images, wide = columns[0].shape
    oris = weights.shape[-1]
    return pl.pallas_call(
        project_kernel,
        out_shape=jax.ShapeDtypeStruct((oris, shares * wide), jnp.float32),
        grid_spec=pltpu.PrefetchScalarGridSpec(
            num_scalar_prefetch=1,
            grid=(shares,),
            in_specs=[pl.BlockSpec(weights.shape, lambda i, place: (0, 0, 0))]
            + [pl.BlockSpec((1, images, wide), lambda i, place: (i, 0, 0))] * 4,
            out_specs=pl.BlockSpec((oris, wide), lambda i, place: (0, i)),
            scratch_shapes=[pltpu.VMEM((oris, 4 * images), jnp.bfloat16)],
        ),
        compiler_params=pltpu.CompilerParams(vmem_limit_bytes=56 * MIB),
        name="project",
    )(place, weights, *columns)


def squares(block):
    block = block.astype(jnp.float32)
    return jnp.sum(block * block, axis=1)


def on_device(images, shifts, slices, class_of, log_prior):
    rows = images.shape[0] // 2
    oris = slices.shape[0]
    orient = lax.axis_index("orient")
    dom = lax.axis_index("dom")
    core, x, y_lo = orient % 2, orient // 2 % RING, orient // 8
    hi, z = dom // HALF, dom % HALF

    s_hi = lax.ppermute(slices, "dom", Y_HIGH)
    s_core = lax.ppermute(slices, "orient", CORE)
    s_both = lax.ppermute(s_hi, "orient", CORE)
    onehot = class_of[:, None] == jnp.arange(log_prior.shape[0], dtype=jnp.int32)[None, :]
    prior = jnp.sum(jnp.where(onehot, log_prior[None, :], 0.0), axis=1)
    prior = jnp.concatenate([prior, lax.ppermute(prior, "orient", CORE)])
    norms = jnp.concatenate([squares(slices) + squares(s_hi), squares(s_core) + squares(s_both)])
    bias = jnp.where(z == 0, prior, 0.0) - 0.5 * norms

    own = shift_part(images, shifts.T, y_lo * RING + x, core)
    mine = lax.all_to_all(own, "dom", 0, 0, axis_index_groups=Z_GROUPS)
    blocks = gather_shares(mine)
    here, there = y_lo * RING, (1 - y_lo) * RING
    step = lambda by: (x + by) % RING
    place = jnp.stack(
        [hi, here + x, here + step(3), here + step(1), there + x, there + step(1), there + step(3), here + step(2), there + step(2)]
    ).astype(jnp.int32)
    partial, keep, give = partial_score(place, blocks, (slices, s_hi, s_core, s_both), bias[None, :])

    from_hi = lax.ppermute(give, "dom", Y_HIGH)
    from_core = lax.ppermute(keep, "orient", CORE)
    from_both = lax.ppermute(from_hi, "orient", CORE)

    pieces = lax.all_to_all(partial.reshape(HALF, rows, 2 * oris), "dom", 0, 0, axis_index_groups=Z_GROUPS)
    near, other, stats = total_score(pieces)
    came = lax.ppermute(other, "orient", CORE)
    stats = lax.all_to_all(stats, "orient", 0, 0)
    copies, log_norm = weigh(core.astype(jnp.int32)[None], near, came, stats)
    weights = lax.all_to_all(copies, "dom", 0, 0)
    place = jnp.stack([hi, core]).astype(jnp.int32)
    projected = project(place, weights, (keep, from_core, from_hi, from_both))
    return projected, log_norm[:, :rows].reshape(2 * rows)


def solution(mesh):
    placed = (P("dom", None), P("dom", None), P("orient", "dom"), P("orient"), P())
    return jax.shard_map(
        on_device,
        mesh=mesh,
        in_specs=placed,
        out_specs=(P("orient", "dom"), P("dom")),
        check_vma=False,
    )
```

time: 190 us -> 168 us (0.88)
  blocking collectives: 83.8 us -> 0 us
  starting transfers between devices: 5.45 us -> 43.2 us
  waiting for transfers between devices: 63.7 us -> 88.2 us
  between operations: 14.1 us -> 0.79 us
  Pallas kernels: 13.8 us -> 25.5 us
  other arithmetic: 1.01 us -> 4.36 us
  local copies, waits for them, and re-layouts: 7.48 us -> 4.64 us
    all_to_all x3 -> x0, blocking collectives: 83.8 us -> none  [the longest x1 49.2 us: on_device(): pieces = lax.all_to_all(partial.reshape(doms, rows, oris), 'dom', 0, 0)]
    ppermute x0 -> x16, waiting for transfers between devices: none -> 56.7 us  [the longest x1 28.4 us: on_device(): from_hi = lax.ppermute(give, 'dom', Y_HIGH)]
    all_gather x1 -> x0, waiting for transfers between devices: 41 us -> none  [on_device(): columns = lax.all_gather(mine, 'orient')]
    all_to_all x1 -> x4, starting transfers between devices: 5.41 us -> 31.1 us  [the longest x1 8.47 us: on_device(): mine = lax.all_to_all(own, 'dom', 0, 0, axis_index_groups=Z_GROUPS)]
    ppermute x0 -> x16, starting transfers between devices: none -> 12.1 us  [the longest x8 7.71 us: gather_shares(): send = lambda block, perm: lax.ppermute(block, 'orient', perm)]
    pallas_call x5, Pallas kernels: 13.8 us -> 25.5 us  [the longest x1 9.21 us: project(): pl.pallas_call(project_kernel, out_shape=jax.ShapeDtypeStruct((oris, shar...]
    all_to_all x1 -> x4, waiting for transfers between devices: 22.7 us -> 31.5 us  [the longest x1 22 us: on_device(): weights = lax.all_to_all(copies, 'dom', 0, 0)]
    unnamed x11 -> x22, local copies, waits for them, and re-layouts: 6.97 us -> 1.6 us
  transfers between devices with their start and end apart: 2 -> 20, of which waited for: 2 -> 10; matrix products, arithmetic and copies ran while one was open for 0% -> 4% of each run, Pallas kernels for 0% -> 5%
where the time goes in v2:
time: 168 us; the launch traced here: 167 us
  waiting for transfers between devices  88.2 us (52%)
  starting transfers between devices  43.2 us (26%)
  Pallas kernels  25.5 us (15%)
  local copies, waits for them, and re-layouts  4.64 us (3%)
  other arithmetic  4.36 us (3%)
    ppermute x1, waiting for transfers between devices, on_device(): from_hi = lax.ppermute(give, 'dom', Y_HIGH)  28.4 us
    all_to_all x1, waiting for transfers between devices, on_device(): weights = lax.all_to_all(copies, 'dom', 0, 0)  22 us
    ppermute x8, waiting for transfers between devices, gather_shares(): send = lambda block, perm: lax.ppermute(block, 'orient', perm)  19 us
    pallas_call x1, Pallas kernels, project(): pl.pallas_call(project_kernel, out_shape=jax.ShapeDtypeStruct((oris, shar...  9.21 us
    all_to_all x1, starting transfers between devices, on_device(): mine = lax.all_to_all(own, 'dom', 0, 0, axis_index_groups=Z_GROUPS)  8.47 us
    all_to_all x1, starting transfers between devices, on_device(): lax.all_to_all(partial.reshape(HALF, rows, 2 * oris), 'dom', 0, 0, axis_i...  8.35 us
    pallas_call x1, Pallas kernels, partial_score(): pl.pallas_call(score_kernel, out_shape=(jax.ShapeDtypeStruct((images, 2 *...  8.34 us
    ppermute x1, waiting for transfers between devices, on_device(): s_hi = lax.ppermute(slices, 'dom', Y_HIGH)  8.3 us
  transfers between devices with their start and end apart: 20, of which 10 were waited for; matrix products, arithmetic and copies ran while one was open for 4% of the time, Pallas kernels for 5%

profile of v2, /device:TPU:2, one launch (start us, length us, event | category | flops | bytes accessed | tf_op | source)
XLA Modules:
  0.0 166.7 jit_solution(8802401310480991867)
XLA Ops:
  0.6 3.3 %collective-permute-start.8 = (bf16[256,2048]{1,0:T(8,128)(2,1)}, bf16[256,2048]{1,0:T(8,128)(2,1)S(1)}, u32[]{:S(2)}, u32[]{:S(2)}) collective-permute-start(bf16[256,2048]{1,0:T(8,128)(2,1)} %s_own.1), channel_id=1, source_target_pairs={{0,8},{1,9},{2,10},{3,11},{4,12},{5,13},{6,14},{7,15},{8,0},{9,1},... | collective-permute-start | bytes 3145736 | tf_op jit(solution)/shard_map/ppermute | solution.py:294
  3.9 0.7 pad_add_fusion.1.place
  4.6 5.9 %shift.1 = bf16[8,2,48,256]{3,2,1,0:T(8,128)(2,1)} custom-call(s32[3]{0:T(128)} %pad_add_fusion.1.place, s32[2,96]{1,0:T(2,128)} %bitcast.23, bf16[96,32768]{1,0:T(8,128)(2,1)} %imag.1, bf16[96,32768]{1,0:T(8,128)(2,1)} %imag.1), custom_call_target="tpu_custom_call" | custom-call | tf_op jit(solution)/shard_map/shift/pallas_call | solution.py:70
  10.5 8.5 %all-to-all-start = ((bf16[8,2,48,256]{3,2,1,0:T(8,128)(2,1)}), bf16[8,2,48,256]{3,2,1,0:T(8,128)(2,1)S(1)}, u32[]{:S(2)}, u32[]{:S(2)}) async-start(bf16[8,2,48,256]{3,2,1,0:T(8,128)(2,1)} %shift.1), calls=%async_computation | async-start | bytes 786432 | tf_op jit(solution)/shard_map/all_to_all | solution.py:304
  18.9 0.1 collective-permute-start.9
  19.0 8.3 %collective-permute-done.8.s_hi = bf16[256,2048]{1,0:T(8,128)(2,1)S(1)} collective-permute-done((bf16[256,2048]{1,0:T(8,128)(2,1)}, bf16[256,2048]{1,0:T(8,128)(2,1)S(1)}, u32[]{:S(2)}, u32[]{:S(2)}) %collective-permute-start.8) | collective-permute-done | bytes 1048608 | tf_op jit(solution)/shard_map/ppermute | solution.py:294
  27.3 6.0 %all-to-all-done.own = bf16[8,2,48,256]{3,2,1,0:T(8,128)(2,1)S(1)} async-done(((bf16[8,2,48,256]{3,2,1,0:T(8,128)(2,1)}), bf16[8,2,48,256]{3,2,1,0:T(8,128)(2,1)S(1)}, u32[]{:S(2)}, u32[]{:S(2)}) %all-to-all-start) | async-done | bytes 393248 | tf_op jit(solution)/shard_map/all_to_all | solution.py:304
  33.3 0.7 collective-permute-start.2
  34.0 0.5 collective-permute-start.1
  34.5 0.3 multiply_reduce_fusion.3
  34.8 7.9 %collective-permute-done.2.across = bf16[8,2,48,256]{3,2,1,0:T(8,128)(2,1)} collective-permute-done((bf16[8,2,48,256]{3,2,1,0:T(8,128)(2,1)S(1)}, bf16[8,2,48,256]{3,2,1,0:T(8,128)(2,1)}, u32[]{:S(2)}, u32[]{:S(2)}) %collective-permute-start.2) | collective-permute-done | bytes 393248 | tf_op jit(solution)/shard_map/ppermute | solution.py:89
  42.7 1.5 collective-permute-start.4
  44.2 0.7 collective-permute-start.3
  44.9 0.1 select_reduce_fusion
  45.0 0.6 stack.53.place
  45.6 1.2 collective-permute-start
  46.8 0.3 multiply_reduce_fusion.2
  47.1 0.9 collective-permute-start.5
  48.0 0.3 multiply_reduce_fusion.1
  48.3 6.8 %collective-permute-done.4.across_low = bf16[8,2,48,256]{3,2,1,0:T(8,128)(2,1)} collective-permute-done((bf16[8,2,48,256]{3,2,1,0:T(8,128)(2,1)}, bf16[8,2,48,256]{3,2,1,0:T(8,128)(2,1)}, u32[]{:S(2)}, u32[]{:S(2)}) %collective-permute-start.4) | collective-permute-done | bytes 393248 | tf_op jit(solution)/shard_map/ppermute | solution.py:89
  55.1 0.0 collective-permute-start.11
  55.1 0.9 slice.13
  56.0 0.0 collective-permute-done.3.across_high
  56.0 1.6 collective-permute-start.7
  57.6 0.9 slice.12
  58.5 0.0 collective-permute-done.10.s_both
  58.5 0.6 collective-permute-start.6
  59.2 1.5 multiply_reduce_fusion
  60.7 0.6 fusion.bias
  61.3 2.6 %collective-permute-done.7.second = bf16[4,2,48,256]{3,2,1,0:T(8,128)(2,1)S(1)} collective-permute-done((bf16[4,2,48,256]{3,2,1,0:T(8,128)(2,1)S(1)}, bf16[4,2,48,256]{3,2,1,0:T(8,128)(2,1)S(1)}, u32[]{:S(2)}, u32[]{:S(2)}) %collective-permute-start.7) | collective-permute-done | bytes 196640 | tf_op jit(solution)/shard_map/ppermute | solution.py:89
  63.9 1.8 %collective-permute-done.6.first = bf16[4,2,48,256]{3,2,1,0:T(8,128)(2,1)S(1)} collective-permute-done((bf16[4,2,48,256]{3,2,1,0:T(8,128)(2,1)S(1)}, bf16[4,2,48,256]{3,2,1,0:T(8,128)(2,1)S(1)}, u32[]{:S(2)}, u32[]{:S(2)}) %collective-permute-start.6) | collective-permute-done | bytes 196640 | tf_op jit(solution)/shard_map/ppermute | solution.py:89
  65.7 0.7 copy-done.8
  66.4 8.3 %score.1 = (f32[384,512]{1,0:T(8,128)}, bf16[8,384,256]{2,1,0:T(8,128)(2,1)}, bf16[8,384,256]{2,1,0:T(8,128)(2,1)}) custom-call(s32[9]{0:T(128)} %stack.53.place, bf16[8,2,48,256]{3,2,1,0:T(8,128)(2,1)} %copy-done.4, bf16[8,2,48,256]{3,2,1,0:T(8,128)(2,1)} %copy-done.5, bf16[8,2,48,256]{3,2,1,0:T(8,128)(2,1)} %collective-permute-done.1.high, ...), custom_call_target="tpu_custom_call" | custom-call | tf_op jit(solution)/shard_map/score/pallas_call | solution.py:146
  74.7 0.9 collective-permute-start.14
  75.6 8.4 %all-to-all-start.1 = ((f32[8,48,512]{2,1,0:T(8,128)}), f32[8,48,512]{2,1,0:T(8,128)S(1)}, u32[]{:S(2)}, u32[]{:S(2)}) async-start(f32[8,48,512]{2,1,0:T(8,128)} %bitcast.18), calls=%async_computation.1 | async-start | bytes 1572864 | tf_op jit(solution)/shard_map/all_to_all | solution.py:317
  84.0 28.4 %collective-permute-done.14.from_hi = bf16[8,384,256]{2,1,0:T(8,128)(2,1)} collective-permute-done((bf16[8,384,256]{2,1,0:T(8,128)(2,1)}, bf16[8,384,256]{2,1,0:T(8,128)(2,1)}, u32[]{:S(2)}, u32[]{:S(2)}) %collective-permute-start.14) | collective-permute-done | bytes 1572896 | tf_op jit(solution)/shard_map/ppermute | solution.py:313
  112.3 0.9 total.1
  113.2 6.2 %all-to-all-start.2 = ((f32[16,8,128]{2,1,0:T(8,128)}), f32[16,8,128]{2,1,0:T(8,128)S(1)}, u32[]{:S(2)}, u32[]{:S(2)}) async-start(f32[16,8,128]{2,1,0:T(8,128)} %get-tuple-element.13), calls=%async_computation.2 | async-start | bytes 131072 | tf_op jit(solution)/shard_map/all_to_all | solution.py:320
  119.4 0.1 collective-permute-start.12
  119.6 1.1 collective-permute-done.12.came
  120.7 3.5 %all-to-all-done.2.stats = f32[16,8,128]{2,1,0:T(8,128)S(1)} async-done(((f32[16,8,128]{2,1,0:T(8,128)}), f32[16,8,128]{2,1,0:T(8,128)S(1)}, u32[]{:S(2)}, u32[]{:S(2)}) %all-to-all-start.2) | async-done | bytes 65568 | tf_op jit(solution)/shard_map/all_to_all | solution.py:320
  124.2 1.1 weigh.1
  125.3 8.1 %all-to-all-start.3 = ((bf16[16,96,256]{2,1,0:T(8,128)(2,1)}), bf16[16,96,256]{2,1,0:T(8,128)(2,1)S(1)}, u32[]{:S(2)}, u32[]{:S(2)}) async-start(bf16[16,96,256]{2,1,0:T(8,128)(2,1)} %get-tuple-element.14), calls=%async_computation.3 | async-start | bytes 1572864 | tf_op jit(solution)/shard_map/all_to_all | solution.py:322
  133.4 0.7 pad_add_fusion.place
  134.1 0.6 reshape.74
  134.7 22.0 %all-to-all-done.3.weights = bf16[16,96,256]{2,1,0:T(8,128)(2,1)S(1)} async-done(((bf16[16,96,256]{2,1,0:T(8,128)(2,1)}), bf16[16,96,256]{2,1,0:T(8,128)(2,1)S(1)}, u32[]{:S(2)}, u32[]{:S(2)}) %all-to-all-start.3) | async-done | bytes 786464 | tf_op jit(solution)/shard_map/all_to_all | solution.py:322
  156.6 0.9 copy-done.3
  157.5 9.2 %project.1 = f32[256,2048]{1,0:T(8,128)} custom-call(s32[2]{0:T(128)} %pad_add_fusion.place, bf16[16,96,256]{2,1,0:T(8,128)(2,1)} %copy-done.3, bf16[8,384,256]{2,1,0:T(8,128)(2,1)} %get-tuple-element.15.keep, bf16[8,384,256]{2,1,0:T(8,128)(2,1)} %collective-permute-done.13.from_core, bf16[8,384,256]{2,1,0:T(8,128)(2,1)} %collective-permute-done.14.from_hi, ...), custom_call_target="tpu_custom_call" | custom-call | tf_op jit(solution)/shard_map/project/pallas_call | solution.py:265
  (33 shorter events, 0.1 us)
Async XLA Ops:
  0.6 26.7 %collective-permute-start.8 = (bf16[256,2048]{1,0:T(8,128)(2,1)}, bf16[256,2048]{1,0:T(8,128)(2,1)S(1)}, u32[]{:S(2)}, u32[]{:S(2)}) collective-permute-start(bf16[256,2048]{1,0:T(8,128)(2,1)} %s_own.1), channel_id=1, source_target_pairs={{0,8},{1,9},{2,10},{3,11},{4,12},{5,13},{6,14},{7,15},{8,0},{9,1},... | collective-permute-start | bytes 3145736 | tf_op jit(solution)/shard_map/ppermute | solution.py:294
  4.6 14.4 %copy-start = (bf16[256,2048]{1,0:T(8,128)(2,1)S(1)}, bf16[256,2048]{1,0:T(8,128)(2,1)}, u32[]{:S(2)}) copy-start(bf16[256,2048]{1,0:T(8,128)(2,1)} %s_own.1) | copy-start | bytes 3145732
  4.6 40.4 %copy-start.9 = (s32[256]{0:T(256)S(1)}, s32[256]{0:T(256)}, u32[]{:S(2)}) copy-start(s32[256]{0:T(256)} %param.8) | copy-start | bytes 3076
  4.6 40.4 %copy-start.10 = (f32[8]{0:T(128)S(1)}, f32[8]{0:T(128)}, u32[]{:S(2)}) copy-start(f32[8]{0:T(128)} %param.9) | copy-start | bytes 100
  10.5 22.9 %all-to-all-start = ((bf16[8,2,48,256]{3,2,1,0:T(8,128)(2,1)}), bf16[8,2,48,256]{3,2,1,0:T(8,128)(2,1)S(1)}, u32[]{:S(2)}, u32[]{:S(2)}) async-start(bf16[8,2,48,256]{3,2,1,0:T(8,128)(2,1)} %shift.1), calls=%async_computation | async-start | bytes 786432 | tf_op jit(solution)/shard_map/all_to_all | solution.py:304
  18.9 28.1 %collective-permute-start.9 = (bf16[256,2048]{1,0:T(8,128)(2,1)S(1)}, bf16[256,2048]{1,0:T(8,128)(2,1)S(1)}, u32[]{:S(2)}, u32[]{:S(2)}) collective-permute-start(bf16[256,2048]{1,0:T(8,128)(2,1)S(1)} %copy-done), channel_id=1, source_target_pairs={{0,16},{16,0},{32,48},{48,32},{64,80},{80,64},{96,112},{112,96},{1... | collective-permute-start | bytes 3145736 | tf_op jit(solution)/shard_map/ppermute | solution.py:295
  27.3 33.3 %copy-start.1 = (bf16[256,2048]{1,0:T(8,128)(2,1)}, bf16[256,2048]{1,0:T(8,128)(2,1)S(1)}, u32[]{:S(2)}) copy-start(bf16[256,2048]{1,0:T(8,128)(2,1)S(1)} %collective-permute-done.8.s_hi) | copy-start | bytes 3145732
  27.3 31.2 %collective-permute-start.10 = (bf16[256,2048]{1,0:T(8,128)(2,1)S(1)}, bf16[256,2048]{1,0:T(8,128)(2,1)}, u32[]{:S(2)}, u32[]{:S(2)}) collective-permute-start(bf16[256,2048]{1,0:T(8,128)(2,1)S(1)} %collective-permute-done.8.s_hi), channel_id=1, source_target_pairs={{0,16},{16,0},{32,48},{48,32},{64,80},{80,64},{96,112},{112,96},{1... | collective-permute-start | bytes 3145736 | tf_op jit(solution)/shard_map/ppermute | solution.py:296
  33.3 27.4 %copy-start.4 = (bf16[8,2,48,256]{3,2,1,0:T(8,128)(2,1)}, bf16[8,2,48,256]{3,2,1,0:T(8,128)(2,1)S(1)}, u32[]{:S(2)}) copy-start(bf16[8,2,48,256]{3,2,1,0:T(8,128)(2,1)S(1)} %all-to-all-done.own) | copy-start | bytes 1179652
  33.3 9.4 %collective-permute-start.2 = (bf16[8,2,48,256]{3,2,1,0:T(8,128)(2,1)S(1)}, bf16[8,2,48,256]{3,2,1,0:T(8,128)(2,1)}, u32[]{:S(2)}, u32[]{:S(2)}) collective-permute-start(bf16[8,2,48,256]{3,2,1,0:T(8,128)(2,1)S(1)} %all-to-all-done.own), channel_id=1, source_target_pairs={{0,128},{16,144},{32,160},{48,176},{64,192},{80,208},{96,224},{112... | collective-permute-start | bytes 1179656 | tf_op jit(solution)/shard_map/ppermute | solution.py:89
  34.0 10.2 %collective-permute-start.1 = (bf16[8,2,48,256]{3,2,1,0:T(8,128)(2,1)S(1)}, bf16[8,2,48,256]{3,2,1,0:T(8,128)(2,1)}, u32[]{:S(2)}, u32[]{:S(2)}) collective-permute-start(bf16[8,2,48,256]{3,2,1,0:T(8,128)(2,1)S(1)} %all-to-all-done.own), channel_id=1, source_target_pairs={{0,96},{16,112},{32,0},{48,16},{64,32},{80,48},{96,64},{112,80},{1... | collective-permute-start | bytes 1179656 | tf_op jit(solution)/shard_map/ppermute | solution.py:89
  42.7 12.4 %collective-permute-start.4 = (bf16[8,2,48,256]{3,2,1,0:T(8,128)(2,1)}, bf16[8,2,48,256]{3,2,1,0:T(8,128)(2,1)}, u32[]{:S(2)}, u32[]{:S(2)}) collective-permute-start(bf16[8,2,48,256]{3,2,1,0:T(8,128)(2,1)} %collective-permute-done.2.across), channel_id=1, source_target_pairs={{0,32},{16,48},{32,64},{48,80},{64,96},{80,112},{96,0},{112,16},{1... | collective-permute-start | bytes 1179656 | tf_op jit(solution)/shard_map/ppermute | solution.py:89
  44.2 11.8 %collective-permute-start.3 = (bf16[8,2,48,256]{3,2,1,0:T(8,128)(2,1)}, bf16[8,2,48,256]{3,2,1,0:T(8,128)(2,1)}, u32[]{:S(2)}, u32[]{:S(2)}) collective-permute-start(bf16[8,2,48,256]{3,2,1,0:T(8,128)(2,1)} %collective-permute-done.1.high), channel_id=1, source_target_pairs={{0,128},{16,144},{32,160},{48,176},{64,192},{80,208},{96,224},{112... | collective-permute-start | bytes 1179656 | tf_op jit(solution)/shard_map/ppermute | solution.py:89
  45.6 15.7 %collective-permute-start = (bf16[8,2,48,256]{3,2,1,0:T(8,128)(2,1)S(1)}, bf16[8,2,48,256]{3,2,1,0:T(8,128)(2,1)S(1)}, u32[]{:S(2)}, u32[]{:S(2)}) collective-permute-start(bf16[8,2,48,256]{3,2,1,0:T(8,128)(2,1)S(1)} %all-to-all-done.own), channel_id=1, source_target_pairs={{0,32},{16,48},{32,64},{48,80},{64,96},{80,112},{96,0},{112,16},{1... | collective-permute-start | bytes 1179656 | tf_op jit(solution)/shard_map/ppermute | solution.py:89
  47.1 18.6 %copy-start.2 = (bf16[256,2048]{1,0:T(8,128)(2,1)}, bf16[256,2048]{1,0:T(8,128)(2,1)S(1)}, u32[]{:S(2)}) copy-start(bf16[256,2048]{1,0:T(8,128)(2,1)S(1)} %collective-permute-done.9.s_core) | copy-start | bytes 3145732
  47.1 14.2 %collective-permute-start.5 = (bf16[8,2,48,256]{3,2,1,0:T(8,128)(2,1)}, bf16[8,2,48,256]{3,2,1,0:T(8,128)(2,1)S(1)}, u32[]{:S(2)}, u32[]{:S(2)}) collective-permute-start(bf16[8,2,48,256]{3,2,1,0:T(8,128)(2,1)} %collective-permute-done.1.high), channel_id=1, source_target_pairs={{0,96},{16,112},{32,0},{48,16},{64,32},{80,48},{96,64},{112,80},{1... | collective-permute-start | bytes 1179656 | tf_op jit(solution)/shard_map/ppermute | solution.py:89
  55.1 5.6 %collective-permute-start.11 = (f32[256]{0:T(256)S(1)}, f32[256]{0:T(256)S(1)}, u32[]{:S(2)}, u32[]{:S(2)}) collective-permute-start(f32[256]{0:T(256)S(1)} %select_reduce_fusion), channel_id=1, source_target_pairs={{0,16},{16,0},{32,48},{48,32},{64,80},{80,64},{96,112},{112,96},{1... | collective-permute-start | bytes 3080 | tf_op jit(solution)/shard_map/ppermute | solution.py:299
  56.0 7.9 %collective-permute-start.7 = (bf16[4,2,48,256]{3,2,1,0:T(8,128)(2,1)S(1)}, bf16[4,2,48,256]{3,2,1,0:T(8,128)(2,1)S(1)}, u32[]{:S(2)}, u32[]{:S(2)}) collective-permute-start(bf16[4,2,48,256]{3,2,1,0:T(8,128)(2,1)S(1)} %slice.13), channel_id=1, source_target_pairs={{0,32},{16,48},{32,64},{48,80},{64,96},{80,112},{96,0},{112,16},{1... | collective-permute-start | bytes 589832 | tf_op jit(solution)/shard_map/ppermute | solution.py:89
  58.5 7.1 %collective-permute-start.6 = (bf16[4,2,48,256]{3,2,1,0:T(8,128)(2,1)S(1)}, bf16[4,2,48,256]{3,2,1,0:T(8,128)(2,1)S(1)}, u32[]{:S(2)}, u32[]{:S(2)}) collective-permute-start(bf16[4,2,48,256]{3,2,1,0:T(8,128)(2,1)S(1)} %slice.12), channel_id=1, source_target_pairs={{0,96},{16,112},{32,0},{48,16},{64,32},{80,48},{96,64},{112,80},{1... | collective-permute-start | bytes 589832 | tf_op jit(solution)/shard_map/ppermute | solution.py:89
  61.3 4.4 %copy-start.5 = (bf16[8,2,48,256]{3,2,1,0:T(8,128)(2,1)}, bf16[8,2,48,256]{3,2,1,0:T(8,128)(2,1)S(1)}, u32[]{:S(2)}) copy-start(bf16[8,2,48,256]{3,2,1,0:T(8,128)(2,1)S(1)} %collective-permute-done.low) | copy-start | bytes 1179652
  61.3 4.3 %copy-start.6 = (bf16[8,2,48,256]{3,2,1,0:T(8,128)(2,1)}, bf16[8,2,48,256]{3,2,1,0:T(8,128)(2,1)S(1)}, u32[]{:S(2)}) copy-start(bf16[8,2,48,256]{3,2,1,0:T(8,128)(2,1)S(1)} %collective-permute-done.5.far) | copy-start | bytes 1179652
  63.9 1.8 %copy-start.7 = (bf16[4,2,48,256]{3,2,1,0:T(8,128)(2,1)}, bf16[4,2,48,256]{3,2,1,0:T(8,128)(2,1)S(1)}, u32[]{:S(2)}) copy-start(bf16[4,2,48,256]{3,2,1,0:T(8,128)(2,1)S(1)} %collective-permute-done.7.second) | copy-start | bytes 589828
  65.7 0.7 copy-start.8
  74.7 37.6 %collective-permute-start.14 = (bf16[8,384,256]{2,1,0:T(8,128)(2,1)}, bf16[8,384,256]{2,1,0:T(8,128)(2,1)}, u32[]{:S(2)}, u32[]{:S(2)}) collective-permute-start(bf16[8,384,256]{2,1,0:T(8,128)(2,1)} %get-tuple-element.16), channel_id=1, source_target_pairs={{0,8},{1,9},{2,10},{3,11},{4,12},{5,13},{6,14},{7,15},{8,0},{9,1},... | collective-permute-start | bytes 4718600 | tf_op jit(solution)/shard_map/ppermute | solution.py:313
  75.6 36.7 %all-to-all-start.1 = ((f32[8,48,512]{2,1,0:T(8,128)}), f32[8,48,512]{2,1,0:T(8,128)S(1)}, u32[]{:S(2)}, u32[]{:S(2)}) async-start(f32[8,48,512]{2,1,0:T(8,128)} %bitcast.18), calls=%async_computation.1 | async-start | bytes 1572864 | tf_op jit(solution)/shard_map/all_to_all | solution.py:317
  84.0 50.7 %collective-permute-start.13 = (bf16[8,384,256]{2,1,0:T(8,128)(2,1)}, bf16[8,384,256]{2,1,0:T(8,128)(2,1)}, u32[]{:S(2)}, u32[]{:S(2)}) collective-permute-start(bf16[8,384,256]{2,1,0:T(8,128)(2,1)} %get-tuple-element.15.keep), channel_id=1, source_target_pairs={{0,16},{16,0},{32,48},{48,32},{64,80},{80,64},{96,112},{112,96},{1... | collective-permute-start | bytes 4718600 | tf_op jit(solution)/shard_map/ppermute | solution.py:314
  112.3 44.3 %collective-permute-start.15 = (bf16[8,384,256]{2,1,0:T(8,128)(2,1)}, bf16[8,384,256]{2,1,0:T(8,128)(2,1)}, u32[]{:S(2)}, u32[]{:S(2)}) collective-permute-start(bf16[8,384,256]{2,1,0:T(8,128)(2,1)} %collective-permute-done.14.from_hi), channel_id=1, source_target_pairs={{0,16},{16,0},{32,48},{48,32},{64,80},{80,64},{96,112},{112,96},{1... | collective-permute-start | bytes 4718600 | tf_op jit(solution)/shard_map/ppermute | solution.py:315
  113.2 11.0 %all-to-all-start.2 = ((f32[16,8,128]{2,1,0:T(8,128)}), f32[16,8,128]{2,1,0:T(8,128)S(1)}, u32[]{:S(2)}, u32[]{:S(2)}) async-start(f32[16,8,128]{2,1,0:T(8,128)} %get-tuple-element.13), calls=%async_computation.2 | async-start | bytes 131072 | tf_op jit(solution)/shard_map/all_to_all | solution.py:320
  119.4 1.2 collective-permute-start.12
  125.3 31.3 %all-to-all-start.3 = ((bf16[16,96,256]{2,1,0:T(8,128)(2,1)}), bf16[16,96,256]{2,1,0:T(8,128)(2,1)S(1)}, u32[]{:S(2)}, u32[]{:S(2)}) async-start(bf16[16,96,256]{2,1,0:T(8,128)(2,1)} %get-tuple-element.14), calls=%async_computation.3 | async-start | bytes 1572864 | tf_op jit(solution)/shard_map/all_to_all | solution.py:322
  156.6 0.9 copy-start.3

commit v3 on v0

v3 whole, which is shorter than its diff:
```python
import functools
import math

import jax
import jax.numpy as jnp
from jax import lax
from jax.experimental import pallas as pl
from jax.experimental.pallas import tpu as pltpu
from jax.sharding import PartitionSpec as P

BOX = 256
LANES = 128
WIDE = 256
MIB = 1 << 20

ORI = 16
DOM = 16
RING = 4
HALF = DOM // 2
Z_GROUPS = [list(range(HALF)), list(range(HALF, DOM))]
CORE = [(i, i ^ 1) for i in range(ORI)]
Y_LOW = [(i, i ^ 8) for i in range(ORI)]
Y_HIGH = [(i, i ^ 8) for i in range(DOM)]


def along_x(by):
    return [(i, i // 8 * 8 + (i // 2 + by * (1 - i % 2 * 2)) % RING * 2 + i % 2) for i in range(ORI)]


AHEAD = along_x(1)
BACK = along_x(-1)


def turn_wave(turn):
    quarter = (turn + BOX // 8) >> 6
    angle = (turn - (quarter << 6)).astype(jnp.float32) * (2.0 * math.pi / BOX)
    sq = angle * angle
    sine = angle * (1.0 + sq * (-1.0 / 6 + sq * (1.0 / 120 + sq * (-1.0 / 5040 + sq * (1.0 / 362880)))))
    cosine = 1.0 + sq * (-0.5 + sq * (1.0 / 24 + sq * (-1.0 / 720 + sq * (1.0 / 40320))))
    odd = (quarter & 1) == 1
    first = jnp.where(odd, sine, cosine)
    second = jnp.where(odd, cosine, sine)
    first = jnp.where(((quarter + 1) & 2) == 2, -first, first)
    second = jnp.where((quarter & 2) == 2, -second, second)
    return first, second


def shift_kernel(place, shifts, images, out, held, sems):
    share, core, hi = place[0], place[1], place[3]
    zs, _, rows, wide = out.shape
    shares = images.shape[1] // (2 * zs * wide)
    row = pl.ds(pl.multiple_of(core * rows, 16), rows)
    copies = []
    for at in range(2 * zs):
        column = pl.ds(pl.multiple_of((at * shares + share) * wide, wide), wide)
        copies.append(pltpu.make_async_copy(images.at[row, column], held.at[at], sems.at[at]))
        copies[at].start()

    total = shifts.shape[1]
    lane = lax.broadcasted_iota(jnp.int32, (rows, LANES), 1)
    image = lax.broadcasted_iota(jnp.int32, (rows, total), 0) + core * rows
    own = image == lax.broadcasted_iota(jnp.int32, (rows, total), 1)
    by_x = jnp.sum(jnp.where(own, shifts[0:1, :], 0), axis=1, keepdims=True)
    by_y = jnp.sum(jnp.where(own, shifts[1:2, :], 0), axis=1, keepdims=True)
    freq_y = (lane // 2) * (2 * shares) + lane % 2 + 2 * share - place[2]
    cx, sx = turn_wave((lane * by_x) & (BOX - 1))
    cos_y, sin_y = turn_wave((freq_y * by_y) & (BOX - 1))
    for z in range(zs):
        copies[z].wait()
        copies[z + zs].wait()
        for part in range(2):
            pick = 2 * z + part
            cy = cos_y[:, pick : pick + 1]
            sy = sin_y[:, pick : pick + 1]
            cosine = cx * cy - sx * sy
            sine = sx * cy + cx * sy
            here = slice(part * LANES, (part + 1) * LANES)
            re = held[z, :, here].astype(jnp.float32)
            im = held[z + zs, :, here].astype(jnp.float32)
            out[z, hi, :, here] = (re * cosine + im * sine).astype(jnp.bfloat16)
            out[z, 1 - hi, :, here] = (im * cosine - re * sine).astype(jnp.bfloat16)


def shift_part(images, shifts, share, core, hi):
    rows, width = images.shape
    rows = rows // 2
    place = jnp.stack([share, core, jnp.int32(width // 2 // 256), hi]).astype(jnp.int32)
    vmem = pl.BlockSpec(memory_space=pltpu.VMEM)
    return pl.pallas_call(
        shift_kernel,
        out_shape=jax.ShapeDtypeStruct((HALF, 2, rows, WIDE), jnp.bfloat16),
        in_specs=[pl.BlockSpec(memory_space=pltpu.SMEM), vmem, pl.BlockSpec(memory_space=pl.ANY)],
        out_specs=vmem,
        scratch_shapes=[pltpu.VMEM((DOM, rows, WIDE), jnp.bfloat16), pltpu.SemaphoreType.DMA((DOM,))],
        compiler_params=pltpu.CompilerParams(vmem_limit_bytes=16 * MIB),
        name="shift",
    )(place, shifts, images)


def score_kernel(count, place, *refs):
    blocks, refs = refs[:count], refs[count:]
    slices, refs = refs[: 4 * count], refs[4 * count :]
    before, out, keep, give, sems = refs[0], *refs[-4:]
    images, oris = out.shape
    wide = blocks[0].shape[-1]
    copies = []
    for k, block in enumerate(blocks):
        for side, filed in enumerate((keep, give)):
            copies.append(pltpu.make_async_copy(block.at[:, side], filed.at[place[k]], sems.at[2 * k + side]))
    for copy in copies:
        copy.start()
    dims = (((1,), (1,)), ((), ()))
    left = jnp.concatenate([block[:, side].reshape(images, wide) for side in range(2) for block in blocks], axis=1)
    for at in range(2):
        right = jnp.concatenate([slices[(2 * at + side) * count + k][...] for side in range(2) for k in range(count)], axis=1)
        here = slice(at * oris // 2, (at + 1) * oris // 2)
        out[:, here] = lax.dot_general(left, right, dims, preferred_element_type=jnp.float32) + before[:, here]
    for copy in copies:
        copy.wait()


def add_score(place, blocks, slices, before, filed):
    count = len(blocks)
    zs, _, rows, wide = blocks[0].shape
    oris, width = slices[0].shape
    shares = width // wide
    images = zs * rows
    every = lambda shape: pl.BlockSpec(shape, lambda i, place: (0,) * len(shape))
    chunk = lambda k: pl.BlockSpec((oris, wide), lambda i, place: (0, place[k]))
    anywhere = pl.BlockSpec(memory_space=pl.ANY)
    whole = jax.ShapeDtypeStruct((shares, zs, rows, wide), jnp.bfloat16)
    inputs = [*blocks, *(part for part in slices for _ in range(count)), before, *filed]
    return pl.pallas_call(
        functools.partial(score_kernel, count),
        out_shape=(jax.ShapeDtypeStruct((images, 2 * oris), jnp.float32), whole, whole),
        grid_spec=pltpu.PrefetchScalarGridSpec(
            num_scalar_prefetch=1,
            grid=(1,),
            in_specs=[every(block.shape) for block in blocks]
            + [chunk(k) for _ in slices for k in range(count)]
            + [every(before.shape)]
            + [anywhere] * len(filed),
            out_specs=[every((images, 2 * oris)), anywhere, anywhere],
            scratch_shapes=[pltpu.SemaphoreType.DMA((2 * count,))],
        ),
        input_output_aliases={len(inputs) - 1: 1, len(inputs): 2} if filed else {},
        compiler_params=pltpu.CompilerParams(vmem_limit_bytes=24 * MIB),
        name="score",
    )(place, *inputs)


def to_row(column):
    rows = column.shape[0]
    wide = jnp.broadcast_to(column, (rows, LANES))
    square = jnp.concatenate([wide, jnp.zeros((LANES - rows, LANES), jnp.float32)], axis=0)
    return jnp.transpose(square)[0:1]


def to_column(row, rows):
    return jnp.transpose(jnp.broadcast_to(row, (LANES, LANES)))[:rows, 0:1]


def total_kernel(pieces, near, other, stats):
    total = pieces[0]
    for d in range(1, pieces.shape[0]):
        total = total + pieces[d]
    oris = near.shape[1]
    near[...] = total[:, :oris]
    other[...] = total[:, oris:]
    peak = jnp.max(total, axis=1, keepdims=True)
    mass = jnp.sum(jnp.exp(total - peak), axis=1, keepdims=True)
    both = jnp.concatenate([to_row(peak), to_row(mass), jnp.zeros((6, LANES), jnp.float32)], axis=0)
    stats[...] = jnp.broadcast_to(both[None], stats.shape)


def total_score(pieces):
    _, rows, oris = pieces.shape
    return pl.pallas_call(
        total_kernel,
        out_shape=(
            jax.ShapeDtypeStruct((rows, oris // 2), jnp.float32),
            jax.ShapeDtypeStruct((rows, oris // 2), jnp.float32),
            jax.ShapeDtypeStruct((ORI, 8, LANES), jnp.float32),
        ),
        compiler_params=pltpu.CompilerParams(vmem_limit_bytes=32 * MIB),
        name="total",
    )(pieces)


def weight_kernel(place, near, came, stats, weights, log_norm):
    rows = near.shape[0]
    core = place[0]
    used = lax.broadcasted_iota(jnp.int32, (1, LANES), 1) < rows
    peak, total = [], []
    for c in range(2):
        peaks = jnp.concatenate([stats[p, 0:1, :] for p in range(c, ORI, 2)], axis=0)
        masses = jnp.concatenate([stats[p, 1:2, :] for p in range(c, ORI, 2)], axis=0)
        top = jnp.max(peaks, axis=0, keepdims=True)
        mass = jnp.sum(masses * jnp.exp(peaks - top), axis=0, keepdims=True)
        peak.append(top)
        total.append(jnp.where(used, mass, 1.0))
        log_norm[c : c + 1, :] = top + jnp.log(total[c])
    for at, (c, part) in enumerate(((core, near), (1 - core, came))):
        top = to_column(jnp.where(c == 0, peak[0], peak[1]), rows)
        mass = to_column(jnp.where(c == 0, total[0], total[1]), rows)
        weights[at] = (jnp.exp(part[...] - top) / mass).astype(jnp.bfloat16)


def weigh(place, near, came, stats):
    rows, oris = near.shape
    vmem = pl.BlockSpec(memory_space=pltpu.VMEM)
    return pl.pallas_call(
        weight_kernel,
        out_shape=(
            jax.ShapeDtypeStruct((2, rows, oris), jnp.bfloat16),
            jax.ShapeDtypeStruct((2, LANES), jnp.float32),
        ),
        in_specs=[pl.BlockSpec(memory_space=pltpu.SMEM), vmem, vmem, vmem],
        out_specs=(vmem, vmem),
        compiler_params=pltpu.CompilerParams(vmem_limit_bytes=16 * MIB),
        name="weigh",
    )(place, near, came, stats)


def spread_kernel(near, other, out):
    zs = out.shape[0]
    out[:, 0:2] = jnp.broadcast_to(near[...][None], (zs, *near.shape))
    out[:, 2:4] = jnp.broadcast_to(other[...][None], (zs, *other.shape))


def spread(near, other):
    _, rows, oris = near.shape
    return pl.pallas_call(
        spread_kernel,
        out_shape=jax.ShapeDtypeStruct((HALF, 4, rows, oris), jnp.bfloat16),
        compiler_params=pltpu.CompilerParams(vmem_limit_bytes=16 * MIB),
        name="spread",
    )(near, other)


def project_kernel(weights, *refs):
    columns, out = refs[:-1], refs[-1]
    zs, groups, rows, oris = weights.shape
    images = zs * rows
    left = jnp.concatenate([weights[:, g].reshape(images, oris) for g in range(groups)], axis=0)
    right = []
    for column in columns:
        take, _, _, wide = column.shape
        right.append(jnp.concatenate([column[s].reshape(images, wide) for s in range(take)], axis=1))
    right = jnp.concatenate(right, axis=0)
    out[...] = lax.dot_general(left, right, (((0,), (0,)), ((), ())), preferred_element_type=jnp.float32)


def project(weights, columns, steps=4):
    shares, zs, rows, wide = columns[0].shape
    take = shares // steps
    oris = weights.shape[-1]
    return pl.pallas_call(
        project_kernel,
        out_shape=jax.ShapeDtypeStruct((oris, shares * wide), jnp.float32),
        grid=(steps,),
        in_specs=[pl.BlockSpec(weights.shape, lambda i: (0, 0, 0, 0))]
        + [pl.BlockSpec((take, zs, rows, wide), lambda i: (i, 0, 0, 0))] * 4,
        out_specs=pl.BlockSpec((oris, take * wide), lambda i: (0, i)),
        compiler_params=pltpu.CompilerParams(vmem_limit_bytes=24 * MIB),
        name="project",
    )(weights, *columns)


def squares(block):
    block = block.astype(jnp.float32)
    return jnp.sum(block * block, axis=1)


def on_device(images, shifts, slices, class_of, log_prior):
    rows = images.shape[0] // 2
    oris = slices.shape[0]
    orient = lax.axis_index("orient")
    dom = lax.axis_index("dom")
    core, x, y_lo = orient % 2, orient // 2 % RING, orient // 8
    hi, z = dom // HALF, dom % HALF

    s_hi = lax.ppermute(slices, "dom", Y_HIGH)
    s_core = lax.ppermute(slices, "orient", CORE)
    s_both = lax.ppermute(s_hi, "orient", CORE)
    onehot = class_of[:, None] == jnp.arange(log_prior.shape[0], dtype=jnp.int32)[None, :]
    prior = jnp.sum(jnp.where(onehot, log_prior[None, :], 0.0), axis=1)
    prior = jnp.concatenate([prior, lax.ppermute(prior, "orient", CORE)])
    norms = jnp.concatenate([squares(slices) + squares(s_hi), squares(s_core) + squares(s_both)])
    bias = jnp.where(z == 0, prior, 0.0) - 0.5 * norms

    share = y_lo * RING + x
    own = shift_part(images, shifts.T, share, core, hi)
    own = lax.all_to_all(own, "dom", 0, 0, axis_index_groups=Z_GROUPS)

    send = lambda block, perm: lax.ppermute(block, "orient", perm)
    behind = send(own, AHEAD)
    front = send(own, BACK)
    across = send(own, Y_LOW)
    far = send(front, BACK)
    across_front = send(front, Y_LOW)
    across_behind = send(across, AHEAD)
    across_far = send(across_front, BACK)
    ahead = 1 - 2 * core
    here, there = y_lo * RING, (1 - y_lo) * RING
    step = lambda by: (x + by * ahead) % RING
    place = lambda *shares: jnp.stack(shares).astype(jnp.int32)
    parts = (slices, s_hi, s_core, s_both)
    partial, keep, give = add_score(
        place(share, here + step(-1), here + step(1), there + x), (own, behind, front, across), parts, bias[None, :], ()
    )
    partial, keep, give = add_score(
        place(here + step(2), there + step(1), there + step(-1)), (far, across_front, across_behind), parts, partial, (keep, give)
    )
    partial, keep, give = add_score(place(there + step(2)), (across_far,), parts, partial, (keep, give))

    from_hi = lax.ppermute(give, "dom", Y_HIGH)
    from_core = lax.ppermute(keep, "orient", CORE)
    pieces = lax.all_to_all(partial.reshape(HALF, rows, 2 * oris), "dom", 0, 0, axis_index_groups=Z_GROUPS)
    near, other, stats = total_score(pieces)
    came = lax.ppermute(other, "orient", CORE)
    stats = lax.all_to_all(stats, "orient", 0, 0)
    weights, log_norm = weigh(core.astype(jnp.int32)[None], near, came, stats)
    copies = spread(weights, lax.ppermute(weights, "dom", Y_HIGH))
    from_hi, _ = lax.optimization_barrier((from_hi, copies))
    from_both = lax.ppermute(from_hi, "orient", CORE)
    weights = lax.all_to_all(copies, "dom", 0, 0, axis_index_groups=Z_GROUPS)
    projected = project(weights, (keep, from_core, from_hi, from_both))
    return projected, log_norm[:, :rows].reshape(2 * rows)


def solution(mesh):
    placed = (P("dom", None), P("dom", None), P("orient", "dom"), P("orient"), P())
    return jax.shard_map(
        on_device,
        mesh=mesh,
        in_specs=placed,
        out_specs=(P("orient", "dom"), P("dom")),
        check_vma=False,
    )
```

time: 526 us -> 149 us (0.28)
  waiting for transfers between devices: 348 us -> 61.4 us
  blocking collectives: 93 us -> 27.5 us
  other arithmetic: 33.9 us -> 2.7 us
  starting transfers between devices: 11.4 us -> 30.8 us
  Pallas kernels: 0 us -> 17.6 us
  between operations: 14.1 us -> 0.79 us
  matrix products: 11.7 us -> 0 us
  local copies, waits for them, and re-layouts: 10.8 us -> 5.19 us
    reduce_scatter x1 -> x0, waiting for transfers between devices: 207 us -> none  [on_device(): lax.psum_scatter(product - 0.5 * norm_part[None, :], 'dom', scatter_dimen...]
    all_to_all x1 -> x3, waiting for transfers between devices: 141 us -> 32.6 us  [the longest x1 23.4 us: on_device(): weights = lax.all_to_all(copies, 'dom', 0, 0, axis_index_groups=Z_GROUPS)]
    all_gather x1 -> x0, blocking collectives: 42.5 us -> none  [on_device(): lax.all_gather(weights, 'dom', axis=0, tiled=True)]
    ppermute x0 -> x16, waiting for transfers between devices: none -> 28.8 us  [the longest x7 14.4 us: on_device(): send = lambda block, perm: lax.ppermute(block, 'orient', perm)]
    another operation x1 -> x3, other arithmetic: 28.8 us -> 0.23 us  [the longest x2 0.15 us: on_device(): place = lambda *shares: jnp.stack(shares).astype(jnp.int32)]
    all_to_all x0 -> x1, blocking collectives: none -> 27.5 us  [on_device(): lax.all_to_all(partial.reshape(HALF, rows, 2 * oris), 'dom', 0, 0, axis_i...]
    psum x1 -> x0, blocking collectives: 27.1 us -> none  [normalize(): lax.psum(jnp.sum(jnp.exp(score - peak[:, None]), axis=1), 'orient')]
    pmax x1 -> x0, blocking collectives: 23.3 us -> none  [normalize(): peak = lax.pmax(local_peak, 'orient')]
  transfers between devices with their start and end apart: 2 -> 19, of which waited for: 2 -> 10; matrix products, arithmetic and copies ran while one was open for 0% -> 2% of each run, Pallas kernels for 0% -> 7%
where the time goes in v3:
time: 149 us; the launch traced here: 146 us
  waiting for transfers between devices  61.4 us (41%)
  starting transfers between devices  30.8 us (21%)
  blocking collectives  27.5 us (18%)
  Pallas kernels  17.6 us (12%)
  local copies, waits for them, and re-layouts  5.19 us (3%)
  other arithmetic  2.7 us (2%)
    all_to_all x1, blocking collectives, on_device(): lax.all_to_all(partial.reshape(HALF, rows, 2 * oris), 'dom', 0, 0, axis_i...  27.5 us
    all_to_all x1, waiting for transfers between devices, on_device(): weights = lax.all_to_all(copies, 'dom', 0, 0, axis_index_groups=Z_GROUPS)  23.4 us
    ppermute x7, waiting for transfers between devices, on_device(): send = lambda block, perm: lax.ppermute(block, 'orient', perm)  14.4 us
    ppermute x1, waiting for transfers between devices, on_device(): s_hi = lax.ppermute(slices, 'dom', Y_HIGH)  8.73 us
    all_to_all x1, starting transfers between devices, on_device(): own = lax.all_to_all(own, 'dom', 0, 0, axis_index_groups=Z_GROUPS)  8.48 us
    pallas_call x3, Pallas kernels, add_score(): pl.pallas_call(functools.partial(score_kernel, count), out_shape=(jax.Sha...  7.67 us
    ppermute x7, starting transfers between devices, on_device(): send = lambda block, perm: lax.ppermute(block, 'orient', perm)  5.99 us
    all_to_all x1, waiting for transfers between devices, on_device(): own = lax.all_to_all(own, 'dom', 0, 0, axis_index_groups=Z_GROUPS)  5.57 us
  transfers between devices with their start and end apart: 19, of which 10 were waited for; matrix products, arithmetic and copies ran while one was open for 2% of the time, Pallas kernels for 7%

profile of v3, /device:TPU:2, one launch (start us, length us, event | category | flops | bytes accessed | tf_op | source)
XLA Modules:
  0.0 146.0 jit_solution(5142526986374730059)
XLA Ops:
  0.6 3.3 %collective-permute-start.3 = (bf16[256,2048]{1,0:T(8,128)(2,1)}, bf16[256,2048]{1,0:T(8,128)(2,1)S(1)}, u32[]{:S(2)}, u32[]{:S(2)}) collective-permute-start(bf16[256,2048]{1,0:T(8,128)(2,1)} %refs_1_.1), channel_id=1, source_target_pairs={{0,8},{1,9},{2,10},{3,11},{4,12},{5,13},{6,14},{7,15},{8,0},{9,1},... | collective-permute-start | bytes 3145736 | tf_op jit(solution)/shard_map/ppermute | solution.py:283
  3.9 0.1 pad_add_fusion.place
  4.0 2.8 %copy-done.3 = bf16[96,32768]{1,0:T(8,128)(2,1)S(1)} copy-done((bf16[96,32768]{1,0:T(8,128)(2,1)S(1)}, bf16[96,32768]{1,0:T(8,128)(2,1)}, u32[]{:S(2)}) %copy-start.3) | copy-done | bytes 6291480
  6.8 0.7 copy-done.4
  7.5 2.6 %shift.1 = bf16[8,2,48,256]{3,2,1,0:T(8,128)(2,1)} custom-call(s32[4]{0:T(128)S(1)} %pad_add_fusion.place, s32[2,96]{1,0:T(2,128)S(1)} %bitcast.18, bf16[96,32768]{1,0:T(8,128)(2,1)S(1)} %copy-done.3), custom_call_target="tpu_custom_call" | custom-call | tf_op jit(solution)/shard_map/shift/pallas_call | solution.py:89
  10.0 8.5 %all-to-all-start = ((bf16[8,2,48,256]{3,2,1,0:T(8,128)(2,1)}), bf16[8,2,48,256]{3,2,1,0:T(8,128)(2,1)S(1)}, u32[]{:S(2)}, u32[]{:S(2)}) async-start(bf16[8,2,48,256]{3,2,1,0:T(8,128)(2,1)} %shift.1), calls=%async_computation | async-start | bytes 786432 | tf_op jit(solution)/shard_map/all_to_all | solution.py:294
  18.5 0.1 collective-permute-start.4
  18.6 8.7 %collective-permute-done.3.refs_8_.refs_9_.refs_10_.refs_11_.refs_6_.refs_7_.refs_2_ = bf16[256,2048]{1,0:T(8,128)(2,1)S(1)} collective-permute-done((bf16[256,2048]{1,0:T(8,128)(2,1)}, bf16[256,2048]{1,0:T(8,128)(2,1)S(1)}, u32[]{:S(2)}, u32[]{:S(2)}) %collective-permute-start.3) | collective-permute-done | bytes 1048608 | tf_op jit(solution)/shard_map/ppermute | solution.py:283
  27.3 5.6 %all-to-all-done.refs_0_ = bf16[8,2,48,256]{3,2,1,0:T(8,128)(2,1)S(1)} async-done(((bf16[8,2,48,256]{3,2,1,0:T(8,128)(2,1)}), bf16[8,2,48,256]{3,2,1,0:T(8,128)(2,1)S(1)}, u32[]{:S(2)}, u32[]{:S(2)}) %all-to-all-start) | async-done | bytes 393248 | tf_op jit(solution)/shard_map/all_to_all | solution.py:294
  32.9 0.5 collective-permute-start
  33.4 0.1 pad_add_fusion.2.place
  33.5 0.1 select_reduce_fusion
  33.6 0.7 collective-permute-start.7
  34.3 6.5 %collective-permute-done.refs_2_ = bf16[8,2,48,256]{3,2,1,0:T(8,128)(2,1)} collective-permute-done((bf16[8,2,48,256]{3,2,1,0:T(8,128)(2,1)S(1)}, bf16[8,2,48,256]{3,2,1,0:T(8,128)(2,1)}, u32[]{:S(2)}, u32[]{:S(2)}) %collective-permute-start) | collective-permute-done | bytes 393248 | tf_op jit(solution)/shard_map/ppermute | solution.py:296
  40.8 0.7 collective-permute-start.1
  41.5 0.1 pad_add_fusion.1.place
  41.5 0.3 multiply_reduce_fusion.3
  41.8 1.6 %collective-permute-start.9 = (bf16[8,2,48,256]{3,2,1,0:T(8,128)(2,1)S(1)}, bf16[8,2,48,256]{3,2,1,0:T(8,128)(2,1)S(1)}, u32[]{:S(2)}, u32[]{:S(2)}) collective-permute-start(bf16[8,2,48,256]{3,2,1,0:T(8,128)(2,1)S(1)} %all-to-all-done.refs_0_), channel_id=1, source_target_pairs={{0,32},{16,112},{32,64},{48,16},{64,96},{80,48},{96,0},{112,80},{1... | collective-permute-start | bytes 1179656 | tf_op jit(solution)/shard_map/ppermute | solution.py:296
  43.4 0.3 multiply_reduce_fusion.2
  43.7 0.0 collective-permute-done.4.refs_12_.refs_13_.refs_14_.refs_15_.refs_9_.refs_10_.refs_11_.refs_3_
  43.7 0.6 collective-permute-start.6
  44.3 1.5 %collective-permute-done.7.refs_3_ = bf16[8,2,48,256]{3,2,1,0:T(8,128)(2,1)} collective-permute-done((bf16[8,2,48,256]{3,2,1,0:T(8,128)(2,1)S(1)}, bf16[8,2,48,256]{3,2,1,0:T(8,128)(2,1)}, u32[]{:S(2)}, u32[]{:S(2)}) %collective-permute-start.7) | collective-permute-done | bytes 393248 | tf_op jit(solution)/shard_map/ppermute | solution.py:296
  45.8 1.3 collective-permute-start.8
  47.1 5.0 %collective-permute-done.1.refs_1_ = bf16[8,2,48,256]{3,2,1,0:T(8,128)(2,1)} collective-permute-done((bf16[8,2,48,256]{3,2,1,0:T(8,128)(2,1)}, bf16[8,2,48,256]{3,2,1,0:T(8,128)(2,1)}, u32[]{:S(2)}, u32[]{:S(2)}) %collective-permute-start.1) | collective-permute-done | bytes 393248 | tf_op jit(solution)/shard_map/ppermute | solution.py:296
  52.1 0.6 collective-permute-start.2
  52.7 0.3 multiply_reduce_fusion.1
  53.0 0.1 collective-permute-start.10
  53.1 1.5 %multiply_reduce_fusion = f32[256]{0:T(256)S(1)} fusion(bf16[256,2048]{1,0:T(8,128)(2,1)} %collective-permute-done.5.refs_16_.refs_17_.refs_18_.refs_19_.refs_12_.refs_13_.refs_14_.refs_4_), kind=kLoop, calls=%fused_computation | loop fusion | flops 1572608 | bytes 1049600 | tf_op jit(solution)/shard_map/reduce_sum | solution.py:272
  54.6 3.1 %score.3 = (f32[384,512]{1,0:T(8,128)S(1)}, bf16[8,8,48,256]{3,2,1,0:T(8,128)(2,1)S(1)}, bf16[8,8,48,256]{3,2,1,0:T(8,128)(2,1)}) custom-call(s32[4]{0:T(128)S(1)} %pad_add_fusion.2.place, bf16[8,2,48,256]{3,2,1,0:T(8,128)(2,1)S(1)} %all-to-all-done.refs_0_, bf16[8,2,48,256]{3,2,1,0:T(8,128)(2,1)S(1)} %collective-permute-done.9.refs_1_, ...), custom_call_target="tpu_custom_call" | custom-call | tf_op jit(solution)/shard_map/score/pallas_call | solution.py:133
  57.8 1.5 collective-permute-done.8.refs_2_
  59.3 2.7 %score.4 = (f32[384,512]{1,0:T(8,128)S(1)}, bf16[8,8,48,256]{3,2,1,0:T(8,128)(2,1)S(1)}, bf16[8,8,48,256]{3,2,1,0:T(8,128)(2,1)}) custom-call(s32[3]{0:T(128)S(1)} %pad_add_fusion.1.place, bf16[8,2,48,256]{3,2,1,0:T(8,128)(2,1)S(1)} %collective-permute-done.6.refs_0_, ...), custom_call_target="tpu_custom_call", output_to_operand_aliasing={{1}: (17, {}), {2}: (18, {})} | custom-call | tf_op jit(solution)/shard_map/score/pallas_call | solution.py:133
  62.0 1.8 %score.5 = (f32[384,512]{1,0:T(8,128)S(1)}, bf16[8,8,48,256]{3,2,1,0:T(8,128)(2,1)S(1)}, bf16[8,8,48,256]{3,2,1,0:T(8,128)(2,1)}) custom-call(s32[1]{0:T(128)} %bitcast.1.place, bf16[8,2,48,256]{3,2,1,0:T(8,128)(2,1)S(1)} %collective-permute-done.2.refs_0_, bf16[256,2048]{1,0:T(8,128)(2,1)S(1)} %copy-done, ...), custom_call_target="tpu_custom_call", output_to_operand_aliasing={{1}: (7, {}), {2}: (8, {})} | custom-call | tf_op jit(solution)/shard_map/score/pallas_call | solution.py:133
  63.8 1.1 copy-done.1
  64.9 2.6 %collective-permute-start.14 = (bf16[8,8,48,256]{3,2,1,0:T(8,128)(2,1)}, bf16[8,8,48,256]{3,2,1,0:T(8,128)(2,1)}, u32[]{:S(2)}, u32[]{:S(2)}) collective-permute-start(bf16[8,8,48,256]{3,2,1,0:T(8,128)(2,1)} %get-tuple-element.29), channel_id=1, source_target_pairs={{0,8},{1,9},{2,10},{3,11},{4,12},{5,13},{6,14},{7,15},{8,0},{9,1},... | collective-permute-start | bytes 4718600 | tf_op jit(solution)/shard_map/ppermute | solution.py:317
  67.6 27.5 %all_to_all.20.pieces = f32[8,48,512]{2,1,0:T(8,128)S(1)} all-to-all(f32[8,48,512]{2,1,0:T(8,128)S(1)} %bitcast.17), channel_id=1, replica_groups={{0,1,2,3,4,5,6,7},{8,9,10,11,12,13,14,15},{16,17,18,19,20,21,22,23},{24..., dimensions={0} | all-to-all | bytes 1572864 | tf_op jit(solution)/shard_map/all_to_all | solution.py:319
  95.1 0.9 total.1
  96.0 5.4 %all-to-all-start.2 = ((f32[16,8,128]{2,1,0:T(8,128)}), f32[16,8,128]{2,1,0:T(8,128)S(1)}, u32[]{:S(2)}, u32[]{:S(2)}) async-start(f32[16,8,128]{2,1,0:T(8,128)} %get-tuple-element.26), calls=%async_computation.2 | async-start | bytes 131072 | tf_op jit(solution)/shard_map/all_to_all | solution.py:322
  101.4 0.1 collective-permute-start.11
  101.5 1.1 collective-permute-done.11.came
  102.6 3.6 %all-to-all-done.2.stats = f32[16,8,128]{2,1,0:T(8,128)S(1)} async-done(((f32[16,8,128]{2,1,0:T(8,128)}), f32[16,8,128]{2,1,0:T(8,128)S(1)}, u32[]{:S(2)}, u32[]{:S(2)}) %all-to-all-start.2) | async-done | bytes 65568 | tf_op jit(solution)/shard_map/all_to_all | solution.py:322
  106.2 0.2 weigh.1
  106.4 1.1 collective-permute-start.12
  107.6 4.5 %collective-permute-done.12.other = bf16[2,48,256]{2,1,0:T(8,128)(2,1)S(1)} collective-permute-done((bf16[2,48,256]{2,1,0:T(8,128)(2,1)S(1)}, bf16[2,48,256]{2,1,0:T(8,128)(2,1)S(1)}, u32[]{:S(2)}, u32[]{:S(2)}) %collective-permute-start.12) | collective-permute-done | bytes 49184 | tf_op jit(solution)/shard_map/ppermute | solution.py:324
  112.1 1.0 spread.1
  113.1 3.5 %all-to-all-start.3 = ((bf16[8,4,48,256]{3,2,1,0:T(8,128)(2,1)}), bf16[8,4,48,256]{3,2,1,0:T(8,128)(2,1)S(1)}, u32[]{:S(2)}, u32[]{:S(2)}) async-start(bf16[8,4,48,256]{3,2,1,0:T(8,128)(2,1)} %spread.1), calls=%async_computation.3 | async-start | bytes 1572864 | tf_op jit(solution)/shard_map/all_to_all | solution.py:327
  116.6 0.6 reshape.74
  117.2 23.4 %all-to-all-done.3.weights = bf16[8,4,48,256]{3,2,1,0:T(8,128)(2,1)S(1)} async-done(((bf16[8,4,48,256]{3,2,1,0:T(8,128)(2,1)}), bf16[8,4,48,256]{3,2,1,0:T(8,128)(2,1)S(1)}, u32[]{:S(2)}, u32[]{:S(2)}) %all-to-all-start.3) | async-done | bytes 786464 | tf_op jit(solution)/shard_map/all_to_all | solution.py:327
  140.7 5.4 %project.1 = f32[256,2048]{1,0:T(8,128)} custom-call(bf16[8,4,48,256]{3,2,1,0:T(8,128)(2,1)S(1)} %all-to-all-done.3.weights, bf16[8,8,48,256]{3,2,1,0:T(8,128)(2,1)S(1)} %copy-done.2, bf16[8,8,48,256]{3,2,1,0:T(8,128)(2,1)} %collective-permute-done.13.refs_1_, bf16[8,8,48,256]{3,2,1,0:T(8,128)(2,1)} %collective-permute-done.14.refs_2_, ...), custom_call_target="tpu_custom_call" | custom-call | tf_op jit(solution)/shard_map/project/pallas_call | solution.py:258
  (25 shorter events, 0.1 us)
Async XLA Ops:
  0.6 26.7 %collective-permute-start.3 = (bf16[256,2048]{1,0:T(8,128)(2,1)}, bf16[256,2048]{1,0:T(8,128)(2,1)S(1)}, u32[]{:S(2)}, u32[]{:S(2)}) collective-permute-start(bf16[256,2048]{1,0:T(8,128)(2,1)} %refs_1_.1), channel_id=1, source_target_pairs={{0,8},{1,9},{2,10},{3,11},{4,12},{5,13},{6,14},{7,15},{8,0},{9,1},... | collective-permute-start | bytes 3145736 | tf_op jit(solution)/shard_map/ppermute | solution.py:283
  4.0 2.8 %copy-start.3 = (bf16[96,32768]{1,0:T(8,128)(2,1)S(1)}, bf16[96,32768]{1,0:T(8,128)(2,1)}, u32[]{:S(2)}) copy-start(bf16[96,32768]{1,0:T(8,128)(2,1)} %images.1) | copy-start | bytes 18874372
  6.8 0.7 copy-start.4
  7.5 11.0 %copy-start = (bf16[256,2048]{1,0:T(8,128)(2,1)S(1)}, bf16[256,2048]{1,0:T(8,128)(2,1)}, u32[]{:S(2)}) copy-start(bf16[256,2048]{1,0:T(8,128)(2,1)} %refs_1_.1) | copy-start | bytes 3145732
  7.5 26.1 %copy-start.5 = (s32[256]{0:T(256)S(1)}, s32[256]{0:T(256)}, u32[]{:S(2)}) copy-start(s32[256]{0:T(256)} %param.8) | copy-start | bytes 3076
  7.5 26.1 %copy-start.6 = (f32[8]{0:T(128)S(1)}, f32[8]{0:T(128)}, u32[]{:S(2)}) copy-start(f32[8]{0:T(128)} %param.9) | copy-start | bytes 100
  10.0 22.9 %all-to-all-start = ((bf16[8,2,48,256]{3,2,1,0:T(8,128)(2,1)}), bf16[8,2,48,256]{3,2,1,0:T(8,128)(2,1)S(1)}, u32[]{:S(2)}, u32[]{:S(2)}) async-start(bf16[8,2,48,256]{3,2,1,0:T(8,128)(2,1)} %shift.1), calls=%async_computation | async-start | bytes 786432 | tf_op jit(solution)/shard_map/all_to_all | solution.py:294
  18.5 25.2 %collective-permute-start.4 = (bf16[256,2048]{1,0:T(8,128)(2,1)S(1)}, bf16[256,2048]{1,0:T(8,128)(2,1)S(1)}, u32[]{:S(2)}, u32[]{:S(2)}) collective-permute-start(bf16[256,2048]{1,0:T(8,128)(2,1)S(1)} %copy-done), channel_id=1, source_target_pairs={{0,16},{16,0},{32,48},{48,32},{64,80},{80,64},{96,112},{112,96},{1... | collective-permute-start | bytes 3145736 | tf_op jit(solution)/shard_map/ppermute | solution.py:284
  27.3 25.6 %collective-permute-start.5 = (bf16[256,2048]{1,0:T(8,128)(2,1)S(1)}, bf16[256,2048]{1,0:T(8,128)(2,1)}, u32[]{:S(2)}, u32[]{:S(2)}) collective-permute-start(bf16[256,2048]{1,0:T(8,128)(2,1)S(1)} %collective-permute-done.3.refs_8_.refs_9_.refs_10_.refs_11_.refs_6_.refs_7_.refs_2_), channel_id=1, source_target_pairs={{0,16},{16,0},{32,48},{48,32},{64,80},{80,64},{96,112},{112,96},{1... | collective-permute-start | bytes 3145736 | tf_op jit(solution)/shard_map/ppermute | solution.py:285
  32.9 7.9 %collective-permute-start = (bf16[8,2,48,256]{3,2,1,0:T(8,128)(2,1)S(1)}, bf16[8,2,48,256]{3,2,1,0:T(8,128)(2,1)}, u32[]{:S(2)}, u32[]{:S(2)}) collective-permute-start(bf16[8,2,48,256]{3,2,1,0:T(8,128)(2,1)S(1)} %all-to-all-done.refs_0_), channel_id=1, source_target_pairs={{0,96},{16,48},{32,0},{48,80},{64,32},{80,112},{96,64},{112,16},{1... | collective-permute-start | bytes 1179656 | tf_op jit(solution)/shard_map/ppermute | solution.py:296
  33.6 12.2 %collective-permute-start.7 = (bf16[8,2,48,256]{3,2,1,0:T(8,128)(2,1)S(1)}, bf16[8,2,48,256]{3,2,1,0:T(8,128)(2,1)}, u32[]{:S(2)}, u32[]{:S(2)}) collective-permute-start(bf16[8,2,48,256]{3,2,1,0:T(8,128)(2,1)S(1)} %all-to-all-done.refs_0_), channel_id=1, source_target_pairs={{0,128},{16,144},{32,160},{48,176},{64,192},{80,208},{96,224},{112... | collective-permute-start | bytes 1179656 | tf_op jit(solution)/shard_map/ppermute | solution.py:296
  40.8 11.3 %collective-permute-start.1 = (bf16[8,2,48,256]{3,2,1,0:T(8,128)(2,1)}, bf16[8,2,48,256]{3,2,1,0:T(8,128)(2,1)}, u32[]{:S(2)}, u32[]{:S(2)}) collective-permute-start(bf16[8,2,48,256]{3,2,1,0:T(8,128)(2,1)} %collective-permute-done.refs_2_), channel_id=1, source_target_pairs={{0,128},{16,144},{32,160},{48,176},{64,192},{80,208},{96,224},{112... | collective-permute-start | bytes 1179656 | tf_op jit(solution)/shard_map/ppermute | solution.py:296
  41.8 12.8 %collective-permute-start.9 = (bf16[8,2,48,256]{3,2,1,0:T(8,128)(2,1)S(1)}, bf16[8,2,48,256]{3,2,1,0:T(8,128)(2,1)S(1)}, u32[]{:S(2)}, u32[]{:S(2)}) collective-permute-start(bf16[8,2,48,256]{3,2,1,0:T(8,128)(2,1)S(1)} %all-to-all-done.refs_0_), channel_id=1, source_target_pairs={{0,32},{16,112},{32,64},{48,16},{64,96},{80,48},{96,0},{112,80},{1... | collective-permute-start | bytes 1179656 | tf_op jit(solution)/shard_map/ppermute | solution.py:296
  43.7 14.1 %collective-permute-start.6 = (bf16[8,2,48,256]{3,2,1,0:T(8,128)(2,1)}, bf16[8,2,48,256]{3,2,1,0:T(8,128)(2,1)S(1)}, u32[]{:S(2)}, u32[]{:S(2)}) collective-permute-start(bf16[8,2,48,256]{3,2,1,0:T(8,128)(2,1)} %collective-permute-done.refs_2_), channel_id=1, source_target_pairs={{0,96},{16,48},{32,0},{48,80},{64,32},{80,112},{96,64},{112,16},{1... | collective-permute-start | bytes 1179656 | tf_op jit(solution)/shard_map/ppermute | solution.py:296
  45.8 13.5 %collective-permute-start.8 = (bf16[8,2,48,256]{3,2,1,0:T(8,128)(2,1)}, bf16[8,2,48,256]{3,2,1,0:T(8,128)(2,1)S(1)}, u32[]{:S(2)}, u32[]{:S(2)}) collective-permute-start(bf16[8,2,48,256]{3,2,1,0:T(8,128)(2,1)} %collective-permute-done.7.refs_3_), channel_id=1, source_target_pairs={{0,32},{16,112},{32,64},{48,16},{64,96},{80,48},{96,0},{112,80},{1... | collective-permute-start | bytes 1179656 | tf_op jit(solution)/shard_map/ppermute | solution.py:296
  52.1 9.9 %collective-permute-start.2 = (bf16[8,2,48,256]{3,2,1,0:T(8,128)(2,1)}, bf16[8,2,48,256]{3,2,1,0:T(8,128)(2,1)S(1)}, u32[]{:S(2)}, u32[]{:S(2)}) collective-permute-start(bf16[8,2,48,256]{3,2,1,0:T(8,128)(2,1)} %collective-permute-done.1.refs_1_), channel_id=1, source_target_pairs={{0,96},{16,48},{32,0},{48,80},{64,32},{80,112},{96,64},{112,16},{1... | collective-permute-start | bytes 1179656 | tf_op jit(solution)/shard_map/ppermute | solution.py:296
  53.0 1.6 %collective-permute-start.10 = (f32[256]{0:T(256)S(1)}, f32[256]{0:T(256)S(1)}, u32[]{:S(2)}, u32[]{:S(2)}) collective-permute-start(f32[256]{0:T(256)S(1)} %select_reduce_fusion), channel_id=1, source_target_pairs={{0,16},{16,0},{32,48},{48,32},{64,80},{80,64},{96,112},{112,96},{1... | collective-permute-start | bytes 3080 | tf_op jit(solution)/shard_map/ppermute | solution.py:288
  63.8 1.1 copy-start.1
  64.9 42.6 %copy-start.2 = (bf16[8,8,48,256]{3,2,1,0:T(8,128)(2,1)S(1)}, bf16[8,8,48,256]{3,2,1,0:T(8,128)(2,1)}, u32[]{:S(2)}) copy-start(bf16[8,8,48,256]{3,2,1,0:T(8,128)(2,1)} %copy-done.1) | copy-start | bytes 4718596
  64.9 48.1 %collective-permute-start.14 = (bf16[8,8,48,256]{3,2,1,0:T(8,128)(2,1)}, bf16[8,8,48,256]{3,2,1,0:T(8,128)(2,1)}, u32[]{:S(2)}, u32[]{:S(2)}) collective-permute-start(bf16[8,8,48,256]{3,2,1,0:T(8,128)(2,1)} %get-tuple-element.29), channel_id=1, source_target_pairs={{0,8},{1,9},{2,10},{3,11},{4,12},{5,13},{6,14},{7,15},{8,0},{9,1},... | collective-permute-start | bytes 4718600 | tf_op jit(solution)/shard_map/ppermute | solution.py:317
  96.0 10.2 %all-to-all-start.2 = ((f32[16,8,128]{2,1,0:T(8,128)}), f32[16,8,128]{2,1,0:T(8,128)S(1)}, u32[]{:S(2)}, u32[]{:S(2)}) async-start(f32[16,8,128]{2,1,0:T(8,128)} %get-tuple-element.26), calls=%async_computation.2 | async-start | bytes 131072 | tf_op jit(solution)/shard_map/all_to_all | solution.py:322
  101.4 1.2 collective-permute-start.11
  106.4 5.7 %collective-permute-start.12 = (bf16[2,48,256]{2,1,0:T(8,128)(2,1)S(1)}, bf16[2,48,256]{2,1,0:T(8,128)(2,1)S(1)}, u32[]{:S(2)}, u32[]{:S(2)}) collective-permute-start(bf16[2,48,256]{2,1,0:T(8,128)(2,1)S(1)} %get-tuple-element.27.near), channel_id=1, source_target_pairs={{0,8},{1,9},{2,10},{3,11},{4,12},{5,13},{6,14},{7,15},{8,0},{9,1},... | collective-permute-start | bytes 147464 | tf_op jit(solution)/shard_map/ppermute | solution.py:324
  107.6 9.7 %collective-permute-start.13 = (bf16[8,8,48,256]{3,2,1,0:T(8,128)(2,1)S(1)}, bf16[8,8,48,256]{3,2,1,0:T(8,128)(2,1)}, u32[]{:S(2)}, u32[]{:S(2)}) collective-permute-start(bf16[8,8,48,256]{3,2,1,0:T(8,128)(2,1)S(1)} %copy-done.2), channel_id=1, source_target_pairs={{0,16},{16,0},{32,48},{48,32},{64,80},{80,64},{96,112},{112,96},{1... | collective-permute-start | bytes 4718600 | tf_op jit(solution)/shard_map/ppermute | solution.py:318
  113.1 27.6 %collective-permute-start.15 = (bf16[8,8,48,256]{3,2,1,0:T(8,128)(2,1)}, bf16[8,8,48,256]{3,2,1,0:T(8,128)(2,1)}, u32[]{:S(2)}, u32[]{:S(2)}) collective-permute-start(bf16[8,8,48,256]{3,2,1,0:T(8,128)(2,1)} %collective-permute-done.14.refs_2_), channel_id=1, source_target_pairs={{0,16},{16,0},{32,48},{48,32},{64,80},{80,64},{96,112},{112,96},{1... | collective-permute-start | bytes 4718600 | tf_op jit(solution)/shard_map/ppermute | solution.py:326
  113.1 27.6 %all-to-all-start.3 = ((bf16[8,4,48,256]{3,2,1,0:T(8,128)(2,1)}), bf16[8,4,48,256]{3,2,1,0:T(8,128)(2,1)S(1)}, u32[]{:S(2)}, u32[]{:S(2)}) async-start(bf16[8,4,48,256]{3,2,1,0:T(8,128)(2,1)} %spread.1), calls=%async_computation.3 | async-start | bytes 1572864 | tf_op jit(solution)/shard_map/all_to_all | solution.py:327

commit v4 on v3

--- a/solution.py
+++ b/solution.py
@@ -25,6 +25,15 @@
 
 def along_x(by):
     return [(i, i // 8 * 8 + (i // 2 + by * (1 - i % 2 * 2)) % RING * 2 + i % 2) for i in range(ORI)]
+
+
+def along_z(by):
+    pairs = []
+    for o in range(ORI):
+        for d in range(DOM):
+            z = (d % HALF + by * (1 - o % 2 * 2)) % HALF
+            pairs.append((o * DOM + d, o * DOM + d // HALF * HALF + z))
+    return pairs
 
 
 AHEAD = along_x(1)
@@ -92,7 +101,7 @@
         in_specs=[pl.BlockSpec(memory_space=pltpu.SMEM), vmem, pl.BlockSpec(memory_space=pl.ANY)],
         out_specs=vmem,
         scratch_shapes=[pltpu.VMEM((DOM, rows, WIDE), jnp.bfloat16), pltpu.SemaphoreType.DMA((DOM,))],
-        compiler_params=pltpu.CompilerParams(vmem_limit_bytes=16 * MIB),
+        compiler_params=pltpu.CompilerParams(vmem_limit_bytes=60 * MIB),
         name="shift",
     )(place, shifts, images)
 
@@ -128,11 +137,12 @@
     every = lambda shape: pl.BlockSpec(shape, lambda i, place: (0,) * len(shape))
     chunk = lambda k: pl.BlockSpec((oris, wide), lambda i, place: (0, place[k]))
     anywhere = pl.BlockSpec(memory_space=pl.ANY)
-    whole = jax.ShapeDtypeStruct((shares, zs, rows, wide), jnp.bfloat16)
+    whole = pltpu.HBM((shares, zs, rows, wide), jnp.bfloat16)
+    total = (pltpu.HBM if count == 1 else jax.ShapeDtypeStruct)((images, 2 * oris), jnp.float32)
     inputs = [*blocks, *(part for part in slices for _ in range(count)), before, *filed]
     return pl.pallas_call(
         functools.partial(score_kernel, count),
-        out_shape=(jax.ShapeDtypeStruct((images, 2 * oris), jnp.float32), whole, whole),
+        out_shape=(total, whole, whole),
         grid_spec=pltpu.PrefetchScalarGridSpec(
             num_scalar_prefetch=1,
             grid=(1,),
@@ -222,49 +232,45 @@
     )(place, near, came, stats)
 
 
-def spread_kernel(near, other, out):
-    zs = out.shape[0]
-    out[:, 0:2] = jnp.broadcast_to(near[...][None], (zs, *near.shape))
-    out[:, 2:4] = jnp.broadcast_to(other[...][None], (zs, *other.shape))
-
-
-def spread(near, other):
-    _, rows, oris = near.shape
-    return pl.pallas_call(
-        spread_kernel,
-        out_shape=jax.ShapeDtypeStruct((HALF, 4, rows, oris), jnp.bfloat16),
-        compiler_params=pltpu.CompilerParams(vmem_limit_bytes=16 * MIB),
-        name="spread",
-    )(near, other)
-
-
-def project_kernel(weights, *refs):
-    columns, out = refs[:-1], refs[-1]
-    zs, groups, rows, oris = weights.shape
+def project_kernel(place, *refs):
+    zs = HALF
+    weights, columns, (out, left) = refs[:zs], refs[zs:-2], refs[-2:]
+    groups, rows, oris = weights[0].shape
     images = zs * rows
-    left = jnp.concatenate([weights[:, g].reshape(images, oris) for g in range(groups)], axis=0)
+
+    @pl.when(pl.program_id(0) == 0)
+    def _():
+        for k, block in enumerate(weights):
+            z = lax.rem(place[0] + zs - k * place[1], zs)
+            for g in range(groups):
+                left[pl.ds(pl.multiple_of(g * images + z * rows, 16), rows), :] = block[g]
+
     right = []
     for column in columns:
         take, _, _, wide = column.shape
         right.append(jnp.concatenate([column[s].reshape(images, wide) for s in range(take)], axis=1))
     right = jnp.concatenate(right, axis=0)
-    out[...] = lax.dot_general(left, right, (((0,), (0,)), ((), ())), preferred_element_type=jnp.float32)
-
-
-def project(weights, columns, steps=4):
+    out[...] = lax.dot_general(left[...], right, (((0,), (0,)), ((), ())), preferred_element_type=jnp.float32)
+
+
+def project(place, weights, columns, steps=4):
     shares, zs, rows, wide = columns[0].shape
     take = shares // steps
-    oris = weights.shape[-1]
+    groups, _, oris = weights[0].shape
     return pl.pallas_call(
         project_kernel,
         out_shape=jax.ShapeDtypeStruct((oris, shares * wide), jnp.float32),
-        grid=(steps,),
-        in_specs=[pl.BlockSpec(weights.shape, lambda i: (0, 0, 0, 0))]
-        + [pl.BlockSpec((take, zs, rows, wide), lambda i: (i, 0, 0, 0))] * 4,
-        out_specs=pl.BlockSpec((oris, take * wide), lambda i: (0, i)),
-        compiler_params=pltpu.CompilerParams(vmem_limit_bytes=24 * MIB),
+        grid_spec=pltpu.PrefetchScalarGridSpec(
+            num_scalar_prefetch=1,
+            grid=(steps,),
+            in_specs=[pl.BlockSpec((groups, rows, oris), lambda i, place: (0, 0, 0))] * zs
+            + [pl.BlockSpec((take, zs, rows, wide), lambda i, place: (i, 0, 0, 0))] * 4,
+            out_specs=pl.BlockSpec((oris, take * wide), lambda i, place: (0, i)),
+            scratch_shapes=[pltpu.VMEM((groups * zs * rows, oris), jnp.bfloat16)],
+        ),
+        compiler_params=pltpu.CompilerParams(vmem_limit_bytes=60 * MIB),
         name="project",
-    )(weights, *columns)
+    )(place, *weights, *columns)
 
 
 def squares(block):
@@ -321,11 +327,17 @@
     came = lax.ppermute(other, "orient", CORE)
     stats = lax.all_to_all(stats, "orient", 0, 0)
     weights, log_norm = weigh(core.astype(jnp.int32)[None], near, came, stats)
-    copies = spread(weights, lax.ppermute(weights, "dom", Y_HIGH))
-    from_hi, _ = lax.optimization_barrier((from_hi, copies))
+    weights = jnp.concatenate([weights, lax.ppermute(weights, "dom", Y_HIGH)])
+    from_hi, _ = lax.optimization_barrier((from_hi, weights))
     from_both = lax.ppermute(from_hi, "orient", CORE)
-    weights = lax.all_to_all(copies, "dom", 0, 0, axis_index_groups=Z_GROUPS)
-    projected = project(weights, (keep, from_core, from_hi, from_both))
+
+    around = lambda by, block: lax.ppermute(block, ("orient", "dom"), along_z(by))
+    one, back_one = around(1, weights), around(-1, weights)
+    two, back_two = around(2, weights), around(-2, weights)
+    three, back_three = around(2, one), around(-2, back_one)
+    four = around(2, two)
+    weights = (weights, one, two, three, four, back_three, back_two, back_one)
+    projected = project(place(z, ahead), weights, (keep, from_core, from_hi, from_both))
     return projected, log_norm[:, :rows].reshape(2 * rows)
 
 

time: 149 us -> 144 us (0.966)
  blocking collectives: 27.5 us -> 0 us
  starting transfers between devices: 30.8 us -> 49.6 us
  waiting for transfers between devices: 61.4 us -> 66.3 us
  local copies, waits for them, and re-layouts: 5.19 us -> 1.21 us
  Pallas kernels: 17.6 us -> 20.3 us
    all_to_all x1 -> x0, blocking collectives: 27.5 us -> none  [on_device(): lax.all_to_all(partial.reshape(HALF, rows, 2 * oris), 'dom', 0, 0, axis_i...]
    ppermute x1 -> x8, starting transfers between devices: 1.14 us -> 15.6 us  [the longest x7 13.6 us: on_device(): lax.ppermute(block, ('orient', 'dom'), along_z(by))]
    ppermute x1 -> x8, waiting for transfers between devices: 4.54 us -> 9.37 us  [the longest x7 5.62 us: on_device(): lax.ppermute(block, ('orient', 'dom'), along_z(by))]
    all_to_all x1, waiting for transfers between devices: 3.6 us -> 7.7 us  [on_device(): stats = lax.all_to_all(stats, 'orient', 0, 0)]
    unnamed x14 -> x25, local copies, waits for them, and re-layouts: 4.6 us -> 0.61 us
    all_to_all x1, waiting for transfers between devices: 23.4 us -> 20.2 us  [on_device(): lax.all_to_all(partial.reshape(HALF, rows, 2 * oris), 'dom', 0, 0, axis_i...]
    all_to_all x1, starting transfers between devices: 3.55 us -> 6.8 us  [on_device(): lax.all_to_all(partial.reshape(HALF, rows, 2 * oris), 'dom', 0, 0, axis_i...]
    ppermute x1, waiting for transfers between devices: 8.73 us -> 10.8 us  [on_device(): s_hi = lax.ppermute(slices, 'dom', Y_HIGH)]
  transfers between devices with their start and end apart: 19 -> 26, of which waited for: 10 -> 14; matrix products, arithmetic and copies ran while one was open for 2% -> 3% of each run, Pallas kernels for 7% -> 8%
where the time goes in v4:
time: 144 us; the launch traced here: 142 us
  waiting for transfers between devices  66.3 us (46%)
  starting transfers between devices  49.6 us (34%)
  Pallas kernels  20.3 us (14%)
  other arithmetic  3.94 us (3%)
    all_to_all x1, waiting for transfers between devices, on_device(): lax.all_to_all(partial.reshape(HALF, rows, 2 * oris), 'dom', 0, 0, axis_i...  20.2 us
    ppermute x7, waiting for transfers between devices, on_device(): send = lambda block, perm: lax.ppermute(block, 'orient', perm)  14 us
    ppermute x7, starting transfers between devices, on_device(): lax.ppermute(block, ('orient', 'dom'), along_z(by))  13.6 us
    ppermute x1, waiting for transfers between devices, on_device(): s_hi = lax.ppermute(slices, 'dom', Y_HIGH)  10.8 us
    pallas_call x3, Pallas kernels, add_score(): pl.pallas_call(functools.partial(score_kernel, count), out_shape=(total,...  9.07 us
    all_to_all x1, starting transfers between devices, on_device(): own = lax.all_to_all(own, 'dom', 0, 0, axis_index_groups=Z_GROUPS)  8.48 us
    all_to_all x1, waiting for transfers between devices, on_device(): stats = lax.all_to_all(stats, 'orient', 0, 0)  7.7 us
    all_to_all x1, starting transfers between devices, on_device(): lax.all_to_all(partial.reshape(HALF, rows, 2 * oris), 'dom', 0, 0, axis_i...  6.8 us
  transfers between devices with their start and end apart: 26, of which 14 were waited for; matrix products, arithmetic and copies ran while one was open for 3% of the time, Pallas kernels for 8%

profile of v4, /device:TPU:2, one launch (start us, length us, event | category | flops | bytes accessed | tf_op | source)
XLA Modules:
  0.0 142.2 jit_solution(11533572345183261016)
XLA Ops:
  0.6 3.3 %collective-permute-start.3 = (bf16[256,2048]{1,0:T(8,128)(2,1)}, bf16[256,2048]{1,0:T(8,128)(2,1)S(1)}, u32[]{:S(2)}, u32[]{:S(2)}) collective-permute-start(bf16[256,2048]{1,0:T(8,128)(2,1)} %refs_1_.1), channel_id=1, source_target_pairs={{0,8},{1,9},{2,10},{3,11},{4,12},{5,13},{6,14},{7,15},{8,0},{9,1},... | collective-permute-start | bytes 3145736 | tf_op jit(solution)/shard_map/ppermute | solution.py:289
  3.9 0.7 pad_add_fusion.1.place
  4.6 3.4 %shift.1 = bf16[8,2,48,256]{3,2,1,0:T(8,128)(2,1)} custom-call(s32[4]{0:T(128)} %pad_add_fusion.1.place, s32[2,96]{1,0:T(2,128)} %bitcast.24, bf16[96,32768]{1,0:T(8,128)(2,1)} %images.1), custom_call_target="tpu_custom_call" | custom-call | tf_op jit(solution)/shard_map/shift/pallas_call | solution.py:98
  8.0 8.5 %all-to-all-start = ((bf16[8,2,48,256]{3,2,1,0:T(8,128)(2,1)}), bf16[8,2,48,256]{3,2,1,0:T(8,128)(2,1)S(1)}, u32[]{:S(2)}, u32[]{:S(2)}) async-start(bf16[8,2,48,256]{3,2,1,0:T(8,128)(2,1)} %shift.1), calls=%async_computation | async-start | bytes 786432 | tf_op jit(solution)/shard_map/all_to_all | solution.py:300
  16.6 10.8 %collective-permute-done.3.refs_8_.refs_9_.refs_10_.refs_11_.refs_6_.refs_7_.refs_2_ = bf16[256,2048]{1,0:T(8,128)(2,1)S(1)} collective-permute-done((bf16[256,2048]{1,0:T(8,128)(2,1)}, bf16[256,2048]{1,0:T(8,128)(2,1)S(1)}, u32[]{:S(2)}, u32[]{:S(2)}) %collective-permute-start.3) | collective-permute-done | bytes 1048608 | tf_op jit(solution)/shard_map/ppermute | solution.py:289
  27.3 3.5 %all-to-all-done.refs_0_ = bf16[8,2,48,256]{3,2,1,0:T(8,128)(2,1)S(1)} async-done(((bf16[8,2,48,256]{3,2,1,0:T(8,128)(2,1)}), bf16[8,2,48,256]{3,2,1,0:T(8,128)(2,1)S(1)}, u32[]{:S(2)}, u32[]{:S(2)}) %all-to-all-start) | async-done | bytes 393248 | tf_op jit(solution)/shard_map/all_to_all | solution.py:300
  30.9 0.5 collective-permute-start
  31.6 0.7 collective-permute-start.7
  32.3 6.5 %collective-permute-done.refs_2_ = bf16[8,2,48,256]{3,2,1,0:T(8,128)(2,1)} collective-permute-done((bf16[8,2,48,256]{3,2,1,0:T(8,128)(2,1)S(1)}, bf16[8,2,48,256]{3,2,1,0:T(8,128)(2,1)}, u32[]{:S(2)}, u32[]{:S(2)}) %collective-permute-start) | collective-permute-done | bytes 393248 | tf_op jit(solution)/shard_map/ppermute | solution.py:302
  38.8 0.7 collective-permute-start.1
  39.5 0.3 multiply_reduce_fusion.3
  39.8 1.6 %collective-permute-start.9 = (bf16[8,2,48,256]{3,2,1,0:T(8,128)(2,1)S(1)}, bf16[8,2,48,256]{3,2,1,0:T(8,128)(2,1)S(1)}, u32[]{:S(2)}, u32[]{:S(2)}) collective-permute-start(bf16[8,2,48,256]{3,2,1,0:T(8,128)(2,1)S(1)} %all-to-all-done.refs_0_), channel_id=1, source_target_pairs={{0,32},{16,112},{32,64},{48,16},{64,96},{80,48},{96,0},{112,80},{1... | collective-permute-start | bytes 1179656 | tf_op jit(solution)/shard_map/ppermute | solution.py:302
  41.4 0.3 multiply_reduce_fusion.2
  41.7 0.6 collective-permute-start.6
  42.3 1.5 %collective-permute-done.7.refs_3_ = bf16[8,2,48,256]{3,2,1,0:T(8,128)(2,1)} collective-permute-done((bf16[8,2,48,256]{3,2,1,0:T(8,128)(2,1)S(1)}, bf16[8,2,48,256]{3,2,1,0:T(8,128)(2,1)}, u32[]{:S(2)}, u32[]{:S(2)}) %collective-permute-start.7) | collective-permute-done | bytes 393248 | tf_op jit(solution)/shard_map/ppermute | solution.py:302
  43.8 1.3 collective-permute-start.8
  45.1 5.0 %collective-permute-done.1.refs_1_ = bf16[8,2,48,256]{3,2,1,0:T(8,128)(2,1)} collective-permute-done((bf16[8,2,48,256]{3,2,1,0:T(8,128)(2,1)}, bf16[8,2,48,256]{3,2,1,0:T(8,128)(2,1)}, u32[]{:S(2)}, u32[]{:S(2)}) %collective-permute-start.1) | collective-permute-done | bytes 393248 | tf_op jit(solution)/shard_map/ppermute | solution.py:302
  50.1 0.6 collective-permute-start.2
  50.7 0.3 multiply_reduce_fusion.1
  51.1 1.5 %multiply_reduce_fusion = f32[256]{0:T(256)S(1)} fusion(bf16[256,2048]{1,0:T(8,128)(2,1)} %collective-permute-done.5.refs_16_.refs_17_.refs_18_.refs_19_.refs_12_.refs_13_.refs_14_.refs_4_), kind=kLoop, calls=%fused_computation | loop fusion | flops 1572608 | bytes 1049600 | tf_op jit(solution)/shard_map/reduce_sum | solution.py:278
  52.6 3.6 %score.3 = (f32[384,512]{1,0:T(8,128)S(1)}, bf16[8,8,48,256]{3,2,1,0:T(8,128)(2,1)}, bf16[8,8,48,256]{3,2,1,0:T(8,128)(2,1)}) custom-call(s32[4]{0:T(128)S(1)} %pad_add_fusion.3.place, bf16[8,2,48,256]{3,2,1,0:T(8,128)(2,1)S(1)} %all-to-all-done.refs_0_, bf16[8,2,48,256]{3,2,1,0:T(8,128)(2,1)S(1)} %collective-permute-done.9.refs_1_, ...), custom_call_target="tpu_custom_call" | custom-call | tf_op jit(solution)/shard_map/score/pallas_call | solution.py:143
  56.2 1.0 collective-permute-done.8.refs_2_
  57.2 2.9 %score.4 = (f32[384,512]{1,0:T(8,128)S(1)}, bf16[8,8,48,256]{3,2,1,0:T(8,128)(2,1)}, bf16[8,8,48,256]{3,2,1,0:T(8,128)(2,1)}) custom-call(s32[3]{0:T(128)S(1)} %pad_add_fusion.2.place, bf16[8,2,48,256]{3,2,1,0:T(8,128)(2,1)S(1)} %collective-permute-done.6.refs_0_, ...), custom_call_target="tpu_custom_call", output_to_operand_aliasing={{1}: (17, {}), {2}: (18, {})} | custom-call | tf_op jit(solution)/shard_map/score/pallas_call | solution.py:143
  60.1 2.6 %score.5 = (f32[384,512]{1,0:T(8,128)}, bf16[8,8,48,256]{3,2,1,0:T(8,128)(2,1)}, bf16[8,8,48,256]{3,2,1,0:T(8,128)(2,1)}) custom-call(s32[1]{0:T(128)} %bitcast.3.place, bf16[8,2,48,256]{3,2,1,0:T(8,128)(2,1)S(1)} %collective-permute-done.2.refs_0_, bf16[256,2048]{1,0:T(8,128)(2,1)S(1)} %copy-done, ...), custom_call_target="tpu_custom_call", output_to_operand_aliasing={{1}: (7, {}), {2}: (8, {})} | custom-call | tf_op jit(solution)/shard_map/score/pallas_call | solution.py:143
  62.8 6.8 %all-to-all-start.1 = ((f32[8,48,512]{2,1,0:T(8,128)}), f32[8,48,512]{2,1,0:T(8,128)S(1)}, u32[]{:S(2)}, u32[]{:S(2)}) async-start(f32[8,48,512]{2,1,0:T(8,128)} %bitcast.20), calls=%async_computation.1 | async-start | bytes 1572864 | tf_op jit(solution)/shard_map/all_to_all | solution.py:325
  69.6 3.1 %collective-permute-start.21 = (bf16[8,8,48,256]{3,2,1,0:T(8,128)(2,1)}, bf16[8,8,48,256]{3,2,1,0:T(8,128)(2,1)}, u32[]{:S(2)}, u32[]{:S(2)}) collective-permute-start(bf16[8,8,48,256]{3,2,1,0:T(8,128)(2,1)} %get-tuple-element.29), channel_id=1, source_target_pairs={{0,8},{1,9},{2,10},{3,11},{4,12},{5,13},{6,14},{7,15},{8,0},{9,1},... | collective-permute-start | bytes 4718600 | tf_op jit(solution)/shard_map/ppermute | solution.py:323
  72.6 20.2 %all-to-all-done.1.pieces = f32[8,48,512]{2,1,0:T(8,128)S(1)} async-done(((f32[8,48,512]{2,1,0:T(8,128)}), f32[8,48,512]{2,1,0:T(8,128)S(1)}, u32[]{:S(2)}, u32[]{:S(2)}) %all-to-all-start.1) | async-done | bytes 786464 | tf_op jit(solution)/shard_map/all_to_all | solution.py:325
  92.8 0.9 total.1
  93.7 5.6 %all-to-all-start.2 = ((f32[16,8,128]{2,1,0:T(8,128)}), f32[16,8,128]{2,1,0:T(8,128)S(1)}, u32[]{:S(2)}, u32[]{:S(2)}) async-start(f32[16,8,128]{2,1,0:T(8,128)} %get-tuple-element.26), calls=%async_computation.2 | async-start | bytes 131072 | tf_op jit(solution)/shard_map/all_to_all | solution.py:328
  99.5 0.4 collective-permute-start.20
  99.8 0.7 collective-permute-done.11.came
  100.6 7.7 %all-to-all-done.2.stats = f32[16,8,128]{2,1,0:T(8,128)S(1)} async-done(((f32[16,8,128]{2,1,0:T(8,128)}), f32[16,8,128]{2,1,0:T(8,128)S(1)}, u32[]{:S(2)}, u32[]{:S(2)}) %all-to-all-start.2) | async-done | bytes 65568 | tf_op jit(solution)/shard_map/all_to_all | solution.py:328
  108.5 1.9 %collective-permute-start.12 = (bf16[2,48,256]{2,1,0:T(8,128)(2,1)S(1)}, bf16[2,48,256]{2,1,0:T(8,128)(2,1)S(1)}, u32[]{:S(2)}, u32[]{:S(2)}) collective-permute-start(bf16[2,48,256]{2,1,0:T(8,128)(2,1)S(1)} %get-tuple-element.27), channel_id=1, source_target_pairs={{0,8},{1,9},{2,10},{3,11},{4,12},{5,13},{6,14},{7,15},{8,0},{9,1},... | collective-permute-start | bytes 147464 | tf_op jit(solution)/shard_map/ppermute | solution.py:330
  110.4 3.7 %collective-permute-done.12 = bf16[2,48,256]{2,1,0:T(8,128)(2,1)S(1)} collective-permute-done((bf16[2,48,256]{2,1,0:T(8,128)(2,1)S(1)}, bf16[2,48,256]{2,1,0:T(8,128)(2,1)S(1)}, u32[]{:S(2)}, u32[]{:S(2)}) %collective-permute-start.12) | collective-permute-done | bytes 49184 | tf_op jit(solution)/shard_map/ppermute | solution.py:330
  114.3 1.8 %collective-permute-start.13 = (bf16[4,48,256]{2,1,0:T(8,128)(2,1)S(1)}, bf16[4,48,256]{2,1,0:T(8,128)(2,1)S(1)}, u32[]{:S(2)}, u32[]{:S(2)}) collective-permute-start(bf16[4,48,256]{2,1,0:T(8,128)(2,1)S(1)} %constant_dynamic-update-slice_fusion.refs_0_), channel_id=1, source_target_pairs={{0,1},{1,2},{2,3},{3,4},{4,5},{5,6},{6,7},{7,0},{8,9},{9,10},{10,1... | collective-permute-start | bytes 294920 | tf_op jit(solution)/shard_map/ppermute | solution.py:334
  116.1 2.4 %collective-permute-start.14 = (bf16[4,48,256]{2,1,0:T(8,128)(2,1)S(1)}, bf16[4,48,256]{2,1,0:T(8,128)(2,1)S(1)}, u32[]{:S(2)}, u32[]{:S(2)}) collective-permute-start(bf16[4,48,256]{2,1,0:T(8,128)(2,1)S(1)} %constant_dynamic-update-slice_fusion.refs_0_), channel_id=1, source_target_pairs={{0,2},{1,3},{2,4},{3,5},{4,6},{5,7},{6,0},{7,1},{8,10},{9,11},{10,... | collective-permute-start | bytes 294920 | tf_op jit(solution)/shard_map/ppermute | solution.py:334
  118.5 1.8 %collective-permute-start.17 = (bf16[4,48,256]{2,1,0:T(8,128)(2,1)S(1)}, bf16[4,48,256]{2,1,0:T(8,128)(2,1)S(1)}, u32[]{:S(2)}, u32[]{:S(2)}) collective-permute-start(bf16[4,48,256]{2,1,0:T(8,128)(2,1)S(1)} %constant_dynamic-update-slice_fusion.refs_0_), channel_id=1, source_target_pairs={{0,7},{1,0},{2,1},{3,2},{4,3},{5,4},{6,5},{7,6},{8,15},{9,8},{10,9... | collective-permute-start | bytes 294920 | tf_op jit(solution)/shard_map/ppermute | solution.py:334
  120.2 0.3 collective-permute-start.19
  120.5 2.6 %collective-permute-start.15 = (bf16[4,48,256]{2,1,0:T(8,128)(2,1)S(1)}, bf16[4,48,256]{2,1,0:T(8,128)(2,1)S(1)}, u32[]{:S(2)}, u32[]{:S(2)}) collective-permute-start(bf16[4,48,256]{2,1,0:T(8,128)(2,1)S(1)} %collective-permute-done.13.refs_1_), channel_id=1, source_target_pairs={{0,2},{1,3},{2,4},{3,5},{4,6},{5,7},{6,0},{7,1},{8,10},{9,11},{10,... | collective-permute-start | bytes 294920 | tf_op jit(solution)/shard_map/ppermute | solution.py:334
  123.2 1.1 collective-permute-done.14.refs_2_
  124.3 4.8 %collective-permute-start.16 = (bf16[4,48,256]{2,1,0:T(8,128)(2,1)S(1)}, bf16[4,48,256]{2,1,0:T(8,128)(2,1)S(1)}, u32[]{:S(2)}, u32[]{:S(2)}) collective-permute-start(bf16[4,48,256]{2,1,0:T(8,128)(2,1)S(1)} %collective-permute-done.14.refs_2_), channel_id=1, source_target_pairs={{0,2},{1,3},{2,4},{3,5},{4,6},{5,7},{6,0},{7,1},{8,10},{9,11},{10,... | collective-permute-start | bytes 294920 | tf_op jit(solution)/shard_map/ppermute | solution.py:334
  129.1 0.7 pad_add_fusion.place
  129.7 0.6 reshape.74
  130.3 0.5 collective-permute-done.19.refs_6_
  130.8 2.0 %collective-permute-done.16.refs_4_ = bf16[4,48,256]{2,1,0:T(8,128)(2,1)S(1)} collective-permute-done((bf16[4,48,256]{2,1,0:T(8,128)(2,1)S(1)}, bf16[4,48,256]{2,1,0:T(8,128)(2,1)S(1)}, u32[]{:S(2)}, u32[]{:S(2)}) %collective-permute-start.16) | collective-permute-done | bytes 98336 | tf_op jit(solution)/shard_map/ppermute | solution.py:334
  132.8 2.1 %collective-permute-done.18.refs_5_ = bf16[4,48,256]{2,1,0:T(8,128)(2,1)S(1)} collective-permute-done((bf16[4,48,256]{2,1,0:T(8,128)(2,1)S(1)}, bf16[4,48,256]{2,1,0:T(8,128)(2,1)S(1)}, u32[]{:S(2)}, u32[]{:S(2)}) %collective-permute-start.18) | collective-permute-done | bytes 98336 | tf_op jit(solution)/shard_map/ppermute | solution.py:334
  134.9 0.6 copy-done.9
  135.5 6.8 %project.1 = f32[256,2048]{1,0:T(8,128)} custom-call(s32[2]{0:T(128)} %pad_add_fusion.place, bf16[4,48,256]{2,1,0:T(8,128)(2,1)} %copy-done.2, bf16[4,48,256]{2,1,0:T(8,128)(2,1)} %copy-done.3, bf16[4,48,256]{2,1,0:T(8,128)(2,1)} %copy-done.4, bf16[4,48,256]{2,1,0:T(8,128)(2,1)} %copy-done.7, bf16[4,48,256]{2,1,0:T(8,128)(2,1)} %copy-done.8, ...), custom_call_target="tpu_custom_call" | custom-call | tf_op jit(solution)/shard_map/project/pallas_call | solution.py:260
  (50 shorter events, 1.0 us)
Async XLA Ops:
  0.6 26.7 %collective-permute-start.3 = (bf16[256,2048]{1,0:T(8,128)(2,1)}, bf16[256,2048]{1,0:T(8,128)(2,1)S(1)}, u32[]{:S(2)}, u32[]{:S(2)}) collective-permute-start(bf16[256,2048]{1,0:T(8,128)(2,1)} %refs_1_.1), channel_id=1, source_target_pairs={{0,8},{1,9},{2,10},{3,11},{4,12},{5,13},{6,14},{7,15},{8,0},{9,1},... | collective-permute-start | bytes 3145736 | tf_op jit(solution)/shard_map/ppermute | solution.py:289
  4.6 11.9 %copy-start = (bf16[256,2048]{1,0:T(8,128)(2,1)S(1)}, bf16[256,2048]{1,0:T(8,128)(2,1)}, u32[]{:S(2)}) copy-start(bf16[256,2048]{1,0:T(8,128)(2,1)} %refs_1_.1) | copy-start | bytes 3145732
  4.6 26.9 %copy-start.10 = (s32[256]{0:T(256)S(1)}, s32[256]{0:T(256)}, u32[]{:S(2)}) copy-start(s32[256]{0:T(256)} %param.8) | copy-start | bytes 3076
  4.6 26.9 %copy-start.11 = (f32[8]{0:T(128)S(1)}, f32[8]{0:T(128)}, u32[]{:S(2)}) copy-start(f32[8]{0:T(128)} %param.9) | copy-start | bytes 100
  8.0 22.9 %all-to-all-start = ((bf16[8,2,48,256]{3,2,1,0:T(8,128)(2,1)}), bf16[8,2,48,256]{3,2,1,0:T(8,128)(2,1)S(1)}, u32[]{:S(2)}, u32[]{:S(2)}) async-start(bf16[8,2,48,256]{3,2,1,0:T(8,128)(2,1)} %shift.1), calls=%async_computation | async-start | bytes 786432 | tf_op jit(solution)/shard_map/all_to_all | solution.py:300
  16.5 25.2 %collective-permute-start.4 = (bf16[256,2048]{1,0:T(8,128)(2,1)S(1)}, bf16[256,2048]{1,0:T(8,128)(2,1)S(1)}, u32[]{:S(2)}, u32[]{:S(2)}) collective-permute-start(bf16[256,2048]{1,0:T(8,128)(2,1)S(1)} %copy-done), channel_id=1, source_target_pairs={{0,16},{16,0},{32,48},{48,32},{64,80},{80,64},{96,112},{112,96},{1... | collective-permute-start | bytes 3145736 | tf_op jit(solution)/shard_map/ppermute | solution.py:290
  27.3 23.6 %collective-permute-start.5 = (bf16[256,2048]{1,0:T(8,128)(2,1)S(1)}, bf16[256,2048]{1,0:T(8,128)(2,1)}, u32[]{:S(2)}, u32[]{:S(2)}) collective-permute-start(bf16[256,2048]{1,0:T(8,128)(2,1)S(1)} %collective-permute-done.3.refs_8_.refs_9_.refs_10_.refs_11_.refs_6_.refs_7_.refs_2_), channel_id=1, source_target_pairs={{0,16},{16,0},{32,48},{48,32},{64,80},{80,64},{96,112},{112,96},{1... | collective-permute-start | bytes 3145736 | tf_op jit(solution)/shard_map/ppermute | solution.py:291
  30.9 7.9 %collective-permute-start = (bf16[8,2,48,256]{3,2,1,0:T(8,128)(2,1)S(1)}, bf16[8,2,48,256]{3,2,1,0:T(8,128)(2,1)}, u32[]{:S(2)}, u32[]{:S(2)}) collective-permute-start(bf16[8,2,48,256]{3,2,1,0:T(8,128)(2,1)S(1)} %all-to-all-done.refs_0_), channel_id=1, source_target_pairs={{0,96},{16,48},{32,0},{48,80},{64,32},{80,112},{96,64},{112,16},{1... | collective-permute-start | bytes 1179656 | tf_op jit(solution)/shard_map/ppermute | solution.py:302
  31.6 12.2 %collective-permute-start.7 = (bf16[8,2,48,256]{3,2,1,0:T(8,128)(2,1)S(1)}, bf16[8,2,48,256]{3,2,1,0:T(8,128)(2,1)}, u32[]{:S(2)}, u32[]{:S(2)}) collective-permute-start(bf16[8,2,48,256]{3,2,1,0:T(8,128)(2,1)S(1)} %all-to-all-done.refs_0_), channel_id=1, source_target_pairs={{0,128},{16,144},{32,160},{48,176},{64,192},{80,208},{96,224},{112... | collective-permute-start | bytes 1179656 | tf_op jit(solution)/shard_map/ppermute | solution.py:302
  38.8 11.3 %collective-permute-start.1 = (bf16[8,2,48,256]{3,2,1,0:T(8,128)(2,1)}, bf16[8,2,48,256]{3,2,1,0:T(8,128)(2,1)}, u32[]{:S(2)}, u32[]{:S(2)}) collective-permute-start(bf16[8,2,48,256]{3,2,1,0:T(8,128)(2,1)} %collective-permute-done.refs_2_), channel_id=1, source_target_pairs={{0,128},{16,144},{32,160},{48,176},{64,192},{80,208},{96,224},{112... | collective-permute-start | bytes 1179656 | tf_op jit(solution)/shard_map/ppermute | solution.py:302
  39.8 12.8 %collective-permute-start.9 = (bf16[8,2,48,256]{3,2,1,0:T(8,128)(2,1)S(1)}, bf16[8,2,48,256]{3,2,1,0:T(8,128)(2,1)S(1)}, u32[]{:S(2)}, u32[]{:S(2)}) collective-permute-start(bf16[8,2,48,256]{3,2,1,0:T(8,128)(2,1)S(1)} %all-to-all-done.refs_0_), channel_id=1, source_target_pairs={{0,32},{16,112},{32,64},{48,16},{64,96},{80,48},{96,0},{112,80},{1... | collective-permute-start | bytes 1179656 | tf_op jit(solution)/shard_map/ppermute | solution.py:302
  41.7 14.5 %collective-permute-start.6 = (bf16[8,2,48,256]{3,2,1,0:T(8,128)(2,1)}, bf16[8,2,48,256]{3,2,1,0:T(8,128)(2,1)S(1)}, u32[]{:S(2)}, u32[]{:S(2)}) collective-permute-start(bf16[8,2,48,256]{3,2,1,0:T(8,128)(2,1)} %collective-permute-done.refs_2_), channel_id=1, source_target_pairs={{0,96},{16,48},{32,0},{48,80},{64,32},{80,112},{96,64},{112,16},{1... | collective-permute-start | bytes 1179656 | tf_op jit(solution)/shard_map/ppermute | solution.py:302
  43.8 13.5 %collective-permute-start.8 = (bf16[8,2,48,256]{3,2,1,0:T(8,128)(2,1)}, bf16[8,2,48,256]{3,2,1,0:T(8,128)(2,1)S(1)}, u32[]{:S(2)}, u32[]{:S(2)}) collective-permute-start(bf16[8,2,48,256]{3,2,1,0:T(8,128)(2,1)} %collective-permute-done.7.refs_3_), channel_id=1, source_target_pairs={{0,32},{16,112},{32,64},{48,16},{64,96},{80,48},{96,0},{112,80},{1... | collective-permute-start | bytes 1179656 | tf_op jit(solution)/shard_map/ppermute | solution.py:302
  50.1 10.1 %collective-permute-start.2 = (bf16[8,2,48,256]{3,2,1,0:T(8,128)(2,1)}, bf16[8,2,48,256]{3,2,1,0:T(8,128)(2,1)S(1)}, u32[]{:S(2)}, u32[]{:S(2)}) collective-permute-start(bf16[8,2,48,256]{3,2,1,0:T(8,128)(2,1)} %collective-permute-done.1.refs_1_), channel_id=1, source_target_pairs={{0,96},{16,48},{32,0},{48,80},{64,32},{80,112},{96,64},{112,16},{1... | collective-permute-start | bytes 1179656 | tf_op jit(solution)/shard_map/ppermute | solution.py:302
  51.0 1.6 %collective-permute-start.10 = (f32[256]{0:T(256)S(1)}, f32[256]{0:T(256)S(1)}, u32[]{:S(2)}, u32[]{:S(2)}) collective-permute-start(f32[256]{0:T(256)S(1)} %select_reduce_fusion), channel_id=1, source_target_pairs={{0,16},{16,0},{32,48},{48,32},{64,80},{80,64},{96,112},{112,96},{1... | collective-permute-start | bytes 3080 | tf_op jit(solution)/shard_map/ppermute | solution.py:294
  62.8 36.7 %copy-start.1 = (bf16[8,8,48,256]{3,2,1,0:T(8,128)(2,1)S(1)}, bf16[8,8,48,256]{3,2,1,0:T(8,128)(2,1)}, u32[]{:S(2)}) copy-start(bf16[8,8,48,256]{3,2,1,0:T(8,128)(2,1)} %get-tuple-element.28.refs_8_) | copy-start | bytes 4718596
  62.8 30.0 %all-to-all-start.1 = ((f32[8,48,512]{2,1,0:T(8,128)}), f32[8,48,512]{2,1,0:T(8,128)S(1)}, u32[]{:S(2)}, u32[]{:S(2)}) async-start(f32[8,48,512]{2,1,0:T(8,128)} %bitcast.20), calls=%async_computation.1 | async-start | bytes 1572864 | tf_op jit(solution)/shard_map/all_to_all | solution.py:325
  69.6 44.6 %collective-permute-start.21 = (bf16[8,8,48,256]{3,2,1,0:T(8,128)(2,1)}, bf16[8,8,48,256]{3,2,1,0:T(8,128)(2,1)}, u32[]{:S(2)}, u32[]{:S(2)}) collective-permute-start(bf16[8,8,48,256]{3,2,1,0:T(8,128)(2,1)} %get-tuple-element.29), channel_id=1, source_target_pairs={{0,8},{1,9},{2,10},{3,11},{4,12},{5,13},{6,14},{7,15},{8,0},{9,1},... | collective-permute-start | bytes 4718600 | tf_op jit(solution)/shard_map/ppermute | solution.py:323
  93.7 14.6 %all-to-all-start.2 = ((f32[16,8,128]{2,1,0:T(8,128)}), f32[16,8,128]{2,1,0:T(8,128)S(1)}, u32[]{:S(2)}, u32[]{:S(2)}) async-start(f32[16,8,128]{2,1,0:T(8,128)} %get-tuple-element.26), calls=%async_computation.2 | async-start | bytes 131072 | tf_op jit(solution)/shard_map/all_to_all | solution.py:328
  99.3 1.2 collective-permute-start.11
  99.5 20.8 %collective-permute-start.20 = (bf16[8,8,48,256]{3,2,1,0:T(8,128)(2,1)S(1)}, bf16[8,8,48,256]{3,2,1,0:T(8,128)(2,1)}, u32[]{:S(2)}, u32[]{:S(2)}) collective-permute-start(bf16[8,8,48,256]{3,2,1,0:T(8,128)(2,1)S(1)} %copy-done.1), channel_id=1, source_target_pairs={{0,16},{16,0},{32,48},{48,32},{64,80},{80,64},{96,112},{112,96},{1... | collective-permute-start | bytes 4718600 | tf_op jit(solution)/shard_map/ppermute | solution.py:324
  108.5 5.7 %collective-permute-start.12 = (bf16[2,48,256]{2,1,0:T(8,128)(2,1)S(1)}, bf16[2,48,256]{2,1,0:T(8,128)(2,1)S(1)}, u32[]{:S(2)}, u32[]{:S(2)}) collective-permute-start(bf16[2,48,256]{2,1,0:T(8,128)(2,1)S(1)} %get-tuple-element.27), channel_id=1, source_target_pairs={{0,8},{1,9},{2,10},{3,11},{4,12},{5,13},{6,14},{7,15},{8,0},{9,1},... | collective-permute-start | bytes 147464 | tf_op jit(solution)/shard_map/ppermute | solution.py:330
  114.2 20.6 %copy-start.2 = (bf16[4,48,256]{2,1,0:T(8,128)(2,1)}, bf16[4,48,256]{2,1,0:T(8,128)(2,1)S(1)}, u32[]{:S(2)}) copy-start(bf16[4,48,256]{2,1,0:T(8,128)(2,1)S(1)} %constant_dynamic-update-slice_fusion.refs_0_) | copy-start | bytes 294916
  114.2 20.6 %collective-permute-start.22 = (bf16[8,8,48,256]{3,2,1,0:T(8,128)(2,1)}, bf16[8,8,48,256]{3,2,1,0:T(8,128)(2,1)}, u32[]{:S(2)}, u32[]{:S(2)}) collective-permute-start(bf16[8,8,48,256]{3,2,1,0:T(8,128)(2,1)} %collective-permute-done.21.refs_10_), channel_id=1, source_target_pairs={{0,16},{16,0},{32,48},{48,32},{64,80},{80,64},{96,112},{112,96},{1... | collective-permute-start | bytes 4718600 | tf_op jit(solution)/shard_map/ppermute | solution.py:332
  114.3 6.2 %collective-permute-start.13 = (bf16[4,48,256]{2,1,0:T(8,128)(2,1)S(1)}, bf16[4,48,256]{2,1,0:T(8,128)(2,1)S(1)}, u32[]{:S(2)}, u32[]{:S(2)}) collective-permute-start(bf16[4,48,256]{2,1,0:T(8,128)(2,1)S(1)} %constant_dynamic-update-slice_fusion.refs_0_), channel_id=1, source_target_pairs={{0,1},{1,2},{2,3},{3,4},{4,5},{5,6},{6,7},{7,0},{8,9},{9,10},{10,1... | collective-permute-start | bytes 294920 | tf_op jit(solution)/shard_map/ppermute | solution.py:334
  116.1 8.2 %collective-permute-start.14 = (bf16[4,48,256]{2,1,0:T(8,128)(2,1)S(1)}, bf16[4,48,256]{2,1,0:T(8,128)(2,1)S(1)}, u32[]{:S(2)}, u32[]{:S(2)}) collective-permute-start(bf16[4,48,256]{2,1,0:T(8,128)(2,1)S(1)} %constant_dynamic-update-slice_fusion.refs_0_), channel_id=1, source_target_pairs={{0,2},{1,3},{2,4},{3,5},{4,6},{5,7},{6,0},{7,1},{8,10},{9,11},{10,... | collective-permute-start | bytes 294920 | tf_op jit(solution)/shard_map/ppermute | solution.py:334
  118.5 10.6 %collective-permute-start.17 = (bf16[4,48,256]{2,1,0:T(8,128)(2,1)S(1)}, bf16[4,48,256]{2,1,0:T(8,128)(2,1)S(1)}, u32[]{:S(2)}, u32[]{:S(2)}) collective-permute-start(bf16[4,48,256]{2,1,0:T(8,128)(2,1)S(1)} %constant_dynamic-update-slice_fusion.refs_0_), channel_id=1, source_target_pairs={{0,7},{1,0},{2,1},{3,2},{4,3},{5,4},{6,5},{7,6},{8,15},{9,8},{10,9... | collective-permute-start | bytes 294920 | tf_op jit(solution)/shard_map/ppermute | solution.py:334
  120.2 10.5 %collective-permute-start.19 = (bf16[4,48,256]{2,1,0:T(8,128)(2,1)S(1)}, bf16[4,48,256]{2,1,0:T(8,128)(2,1)S(1)}, u32[]{:S(2)}, u32[]{:S(2)}) collective-permute-start(bf16[4,48,256]{2,1,0:T(8,128)(2,1)S(1)} %constant_dynamic-update-slice_fusion.refs_0_), channel_id=1, source_target_pairs={{0,6},{1,7},{2,0},{3,1},{4,2},{5,3},{6,4},{7,5},{8,14},{9,15},{10,... | collective-permute-start | bytes 294920 | tf_op jit(solution)/shard_map/ppermute | solution.py:334
  120.5 14.3 %copy-start.3 = (bf16[4,48,256]{2,1,0:T(8,128)(2,1)}, bf16[4,48,256]{2,1,0:T(8,128)(2,1)S(1)}, u32[]{:S(2)}) copy-start(bf16[4,48,256]{2,1,0:T(8,128)(2,1)S(1)} %collective-permute-done.13.refs_1_) | copy-start | bytes 294916
  120.5 10.3 %collective-permute-start.15 = (bf16[4,48,256]{2,1,0:T(8,128)(2,1)S(1)}, bf16[4,48,256]{2,1,0:T(8,128)(2,1)S(1)}, u32[]{:S(2)}, u32[]{:S(2)}) collective-permute-start(bf16[4,48,256]{2,1,0:T(8,128)(2,1)S(1)} %collective-permute-done.13.refs_1_), channel_id=1, source_target_pairs={{0,2},{1,3},{2,4},{3,5},{4,6},{5,7},{6,0},{7,1},{8,10},{9,11},{10,... | collective-permute-start | bytes 294920 | tf_op jit(solution)/shard_map/ppermute | solution.py:334
  124.3 10.5 %copy-start.4 = (bf16[4,48,256]{2,1,0:T(8,128)(2,1)}, bf16[4,48,256]{2,1,0:T(8,128)(2,1)S(1)}, u32[]{:S(2)}) copy-start(bf16[4,48,256]{2,1,0:T(8,128)(2,1)S(1)} %collective-permute-done.14.refs_2_) | copy-start | bytes 294916
  124.3 8.4 %collective-permute-start.16 = (bf16[4,48,256]{2,1,0:T(8,128)(2,1)S(1)}, bf16[4,48,256]{2,1,0:T(8,128)(2,1)S(1)}, u32[]{:S(2)}, u32[]{:S(2)}) collective-permute-start(bf16[4,48,256]{2,1,0:T(8,128)(2,1)S(1)} %collective-permute-done.14.refs_2_), channel_id=1, source_target_pairs={{0,2},{1,3},{2,4},{3,5},{4,6},{5,7},{6,0},{7,1},{8,10},{9,11},{10,... | collective-permute-start | bytes 294920 | tf_op jit(solution)/shard_map/ppermute | solution.py:334
  129.1 5.8 %copy-start.5 = (bf16[4,48,256]{2,1,0:T(8,128)(2,1)}, bf16[4,48,256]{2,1,0:T(8,128)(2,1)S(1)}, u32[]{:S(2)}) copy-start(bf16[4,48,256]{2,1,0:T(8,128)(2,1)S(1)} %collective-permute-done.17.refs_7_) | copy-start | bytes 294916
  129.1 5.7 %collective-permute-start.18 = (bf16[4,48,256]{2,1,0:T(8,128)(2,1)S(1)}, bf16[4,48,256]{2,1,0:T(8,128)(2,1)S(1)}, u32[]{:S(2)}, u32[]{:S(2)}) collective-permute-start(bf16[4,48,256]{2,1,0:T(8,128)(2,1)S(1)} %collective-permute-done.17.refs_7_), channel_id=1, source_target_pairs={{0,6},{1,7},{2,0},{3,1},{4,2},{5,3},{6,4},{7,5},{8,14},{9,15},{10,... | collective-permute-start | bytes 294920 | tf_op jit(solution)/shard_map/ppermute | solution.py:334
  130.8 4.1 %copy-start.6 = (bf16[4,48,256]{2,1,0:T(8,128)(2,1)}, bf16[4,48,256]{2,1,0:T(8,128)(2,1)S(1)}, u32[]{:S(2)}) copy-start(bf16[4,48,256]{2,1,0:T(8,128)(2,1)S(1)} %collective-permute-done.19.refs_6_) | copy-start | bytes 294916
  130.8 4.1 %copy-start.7 = (bf16[4,48,256]{2,1,0:T(8,128)(2,1)}, bf16[4,48,256]{2,1,0:T(8,128)(2,1)S(1)}, u32[]{:S(2)}) copy-start(bf16[4,48,256]{2,1,0:T(8,128)(2,1)S(1)} %collective-permute-done.15.refs_3_) | copy-start | bytes 294916
  132.8 2.1 %copy-start.8 = (bf16[4,48,256]{2,1,0:T(8,128)(2,1)}, bf16[4,48,256]{2,1,0:T(8,128)(2,1)S(1)}, u32[]{:S(2)}) copy-start(bf16[4,48,256]{2,1,0:T(8,128)(2,1)S(1)} %collective-permute-done.16.refs_4_) | copy-start | bytes 294916
  134.8 0.6 copy-start.9

commit v5 on v4

--- a/solution.py
+++ b/solution.py
@@ -21,6 +21,7 @@
 CORE = [(i, i ^ 1) for i in range(ORI)]
 Y_LOW = [(i, i ^ 8) for i in range(ORI)]
 Y_HIGH = [(i, i ^ 8) for i in range(DOM)]
+CORE_HIGH = [(i, i ^ (DOM + 8)) for i in range(ORI * DOM)]
 
 
 def along_x(by):
@@ -197,80 +198,108 @@
     )(pieces)
 
 
-def weight_kernel(place, near, came, stats, weights, log_norm):
+def weight_kernel(place, near, came, near_hi, came_hi, stats, stats_hi, weights, log_norm):
     rows = near.shape[0]
     core = place[0]
     used = lax.broadcasted_iota(jnp.int32, (1, LANES), 1) < rows
     peak, total = [], []
-    for c in range(2):
-        peaks = jnp.concatenate([stats[p, 0:1, :] for p in range(c, ORI, 2)], axis=0)
-        masses = jnp.concatenate([stats[p, 1:2, :] for p in range(c, ORI, 2)], axis=0)
-        top = jnp.max(peaks, axis=0, keepdims=True)
-        mass = jnp.sum(masses * jnp.exp(peaks - top), axis=0, keepdims=True)
-        peak.append(top)
-        total.append(jnp.where(used, mass, 1.0))
-        log_norm[c : c + 1, :] = top + jnp.log(total[c])
-    for at, (c, part) in enumerate(((core, near), (1 - core, came))):
-        top = to_column(jnp.where(c == 0, peak[0], peak[1]), rows)
-        mass = to_column(jnp.where(c == 0, total[0], total[1]), rows)
+    for hi, given in enumerate((stats, stats_hi)):
+        for c in range(2):
+            peaks = jnp.concatenate([given[p, 0:1, :] for p in range(c, ORI, 2)], axis=0)
+            masses = jnp.concatenate([given[p, 1:2, :] for p in range(c, ORI, 2)], axis=0)
+            top = jnp.max(peaks, axis=0, keepdims=True)
+            mass = jnp.sum(masses * jnp.exp(peaks - top), axis=0, keepdims=True)
+            peak.append(top)
+            total.append(jnp.where(used, mass, 1.0))
+            if hi == 0:
+                log_norm[c : c + 1, :] = top + jnp.log(total[c])
+    for at, part in enumerate((near, came, near_hi, came_hi)):
+        first = (core if at % 2 == 0 else 1 - core) == 0
+        hi = 2 * (at // 2)
+        top = to_column(jnp.where(first, peak[hi], peak[hi + 1]), rows)
+        mass = to_column(jnp.where(first, total[hi], total[hi + 1]), rows)
         weights[at] = (jnp.exp(part[...] - top) / mass).astype(jnp.bfloat16)
 
 
-def weigh(place, near, came, stats):
-    rows, oris = near.shape
+def weigh(place, scores, stats, stats_hi):
+    rows, oris = scores[0].shape
     vmem = pl.BlockSpec(memory_space=pltpu.VMEM)
     return pl.pallas_call(
         weight_kernel,
         out_shape=(
-            jax.ShapeDtypeStruct((2, rows, oris), jnp.bfloat16),
+            jax.ShapeDtypeStruct((4, rows, oris), jnp.bfloat16),
             jax.ShapeDtypeStruct((2, LANES), jnp.float32),
         ),
-        in_specs=[pl.BlockSpec(memory_space=pltpu.SMEM), vmem, vmem, vmem],
+        in_specs=[pl.BlockSpec(memory_space=pltpu.SMEM)] + [vmem] * 6,
         out_specs=(vmem, vmem),
         compiler_params=pltpu.CompilerParams(vmem_limit_bytes=16 * MIB),
         name="weigh",
-    )(place, near, came, stats)
+    )(place, *scores, stats, stats_hi)
+
+
+def stage_kernel(*refs):
+    columns, out, sems = refs[:-2], refs[-2], refs[-1]
+    copies = [pltpu.make_async_copy(column, out.at[g], sems.at[g]) for g, column in enumerate(columns)]
+    for copy in copies:
+        copy.start()
+    for copy in copies:
+        copy.wait()
+
+
+def stage(*columns):
+    anywhere = pl.BlockSpec(memory_space=pl.ANY)
+    return pl.pallas_call(
+        stage_kernel,
+        out_shape=pltpu.VMEM((len(columns), *columns[0].shape), jnp.bfloat16),
+        in_specs=[anywhere] * len(columns),
+        out_specs=anywhere,
+        scratch_shapes=[pltpu.SemaphoreType.DMA((len(columns),))],
+        compiler_params=pltpu.CompilerParams(vmem_limit_bytes=16 * MIB),
+        cost_estimate=pl.CostEstimate(flops=0, transcendentals=0, bytes_accessed=12 * MIB),
+        name="stage",
+    )(*columns)
 
 
 def project_kernel(place, *refs):
     zs = HALF
-    weights, columns, (out, left) = refs[:zs], refs[zs:-2], refs[-2:]
+    weights, columns, (out, left, done, sems) = refs[:zs], refs[zs], refs[zs + 1 :]
     groups, rows, oris = weights[0].shape
     images = zs * rows
-
-    @pl.when(pl.program_id(0) == 0)
-    def _():
-        for k, block in enumerate(weights):
-            z = lax.rem(place[0] + zs - k * place[1], zs)
-            for g in range(groups):
-                left[pl.ds(pl.multiple_of(g * images + z * rows, 16), rows), :] = block[g]
-
-    right = []
-    for column in columns:
-        take, _, _, wide = column.shape
-        right.append(jnp.concatenate([column[s].reshape(images, wide) for s in range(take)], axis=1))
-    right = jnp.concatenate(right, axis=0)
-    out[...] = lax.dot_general(left[...], right, (((0,), (0,)), ((), ())), preferred_element_type=jnp.float32)
-
-
-def project(place, weights, columns, steps=4):
-    shares, zs, rows, wide = columns[0].shape
-    take = shares // steps
+    _, shares, _, _, wide = columns.shape
+    for k, block in enumerate(weights):
+        z = lax.rem(place[0] + zs - k * place[1], zs)
+        for g in range(groups):
+            left[pl.ds(pl.multiple_of(g * images + z * rows, 16), rows), :] = block[g]
+    copies = []
+    for at in range(0, shares, 2):
+        right = jnp.concatenate(
+            [columns[:, s].reshape(groups * images, wide) for s in (at, at + 1)], axis=1
+        )
+        done[at // 2] = lax.dot_general(left[...], right, (((0,), (0,)), ((), ())), preferred_element_type=jnp.float32)
+        here = pl.ds(at * wide, 2 * wide)
+        copies.append(pltpu.make_async_copy(done.at[at // 2], out.at[:, here], sems.at[at // 2]))
+        copies[-1].start()
+    for copy in copies:
+        copy.wait()
+
+
+def project(place, weights, columns):
+    _, shares, zs, rows, wide = columns.shape
     groups, _, oris = weights[0].shape
+    vmem = pl.BlockSpec(memory_space=pltpu.VMEM)
     return pl.pallas_call(
         project_kernel,
         out_shape=jax.ShapeDtypeStruct((oris, shares * wide), jnp.float32),
-        grid_spec=pltpu.PrefetchScalarGridSpec(
-            num_scalar_prefetch=1,
-            grid=(steps,),
-            in_specs=[pl.BlockSpec((groups, rows, oris), lambda i, place: (0, 0, 0))] * zs
-            + [pl.BlockSpec((take, zs, rows, wide), lambda i, place: (i, 0, 0, 0))] * 4,
-            out_specs=pl.BlockSpec((oris, take * wide), lambda i, place: (0, i)),
-            scratch_shapes=[pltpu.VMEM((groups * zs * rows, oris), jnp.bfloat16)],
-        ),
-        compiler_params=pltpu.CompilerParams(vmem_limit_bytes=60 * MIB),
+        in_specs=[pl.BlockSpec(memory_space=pltpu.SMEM)] + [vmem] * (len(weights) + 1),
+        out_specs=pl.BlockSpec(memory_space=pl.ANY),
+        scratch_shapes=[
+            pltpu.VMEM((groups * zs * rows, oris), jnp.bfloat16),
+            pltpu.VMEM((shares // 2, oris, 2 * wide), jnp.float32),
+            pltpu.SemaphoreType.DMA((shares // 2,)),
+        ],
+        compiler_params=pltpu.CompilerParams(vmem_limit_bytes=32 * MIB),
         name="project",
-    )(place, *weights, *columns)
+    )(place, *weights, columns)
 
 
 def squares(block):
@@ -303,7 +332,8 @@
     behind = send(own, AHEAD)
     front = send(own, BACK)
     across = send(own, Y_LOW)
-    far = send(front, BACK)
+    after, _ = lax.optimization_barrier((front, behind))
+    far = send(after, BACK)
     across_front = send(front, Y_LOW)
     across_behind = send(across, AHEAD)
     across_far = send(across_front, BACK)
@@ -324,20 +354,26 @@
     from_core = lax.ppermute(keep, "orient", CORE)
     pieces = lax.all_to_all(partial.reshape(HALF, rows, 2 * oris), "dom", 0, 0, axis_index_groups=Z_GROUPS)
     near, other, stats = total_score(pieces)
-    came = lax.ppermute(other, "orient", CORE)
+    both_axes = ("orient", "dom")
     stats = lax.all_to_all(stats, "orient", 0, 0)
-    weights, log_norm = weigh(core.astype(jnp.int32)[None], near, came, stats)
-    weights = jnp.concatenate([weights, lax.ppermute(weights, "dom", Y_HIGH)])
+    scores = (
+        near,
+        lax.ppermute(other, "orient", CORE),
+        lax.ppermute(near, "dom", Y_HIGH),
+        lax.ppermute(other, both_axes, CORE_HIGH),
+    )
+    stats, *scores = lax.optimization_barrier((stats, *scores))
+    weights, log_norm = weigh(core.astype(jnp.int32)[None], scores, stats, lax.ppermute(stats, "dom", Y_HIGH))
     from_hi, _ = lax.optimization_barrier((from_hi, weights))
     from_both = lax.ppermute(from_hi, "orient", CORE)
 
-    around = lambda by, block: lax.ppermute(block, ("orient", "dom"), along_z(by))
+    around = lambda by, block: lax.ppermute(block, both_axes, along_z(by))
     one, back_one = around(1, weights), around(-1, weights)
     two, back_two = around(2, weights), around(-2, weights)
     three, back_three = around(2, one), around(-2, back_one)
     four = around(2, two)
     weights = (weights, one, two, three, four, back_three, back_two, back_one)
-    projected = project(place(z, ahead), weights, (keep, from_core, from_hi, from_both))
+    projected = project(place(z, ahead), weights, stage(keep, from_core, from_hi, from_both))
     return projected, log_norm[:, :rows].reshape(2 * rows)
 
 

time: 144 us -> 138 us (0.958)
  blocking collectives: 0 us -> 29.2 us
  waiting for transfers between devices: 66.3 us -> 39.2 us
  starting transfers between devices: 49.6 us -> 43.4 us
    all_to_all x0 -> x1, blocking collectives: none -> 29.2 us  [on_device(): lax.all_to_all(partial.reshape(HALF, rows, 2 * oris), 'dom', 0, 0, axis_i...]
    all_to_all x1 -> x0, waiting for transfers between devices: 20.2 us -> none  [on_device(): lax.all_to_all(partial.reshape(HALF, rows, 2 * oris), 'dom', 0, 0, axis_i...]
    all_to_all x1, waiting for transfers between devices: 7.7 us -> 0.01 us  [on_device(): stats = lax.all_to_all(stats, 'orient', 0, 0)]
    all_to_all x1 -> x0, starting transfers between devices: 6.8 us -> none  [on_device(): lax.all_to_all(partial.reshape(HALF, rows, 2 * oris), 'dom', 0, 0, axis_i...]
    pallas_call x1, Pallas kernels: 6.78 us -> 3.81 us  [project(): pl.pallas_call(project_kernel, out_shape=jax.ShapeDtypeStruct((oris, shar...]
    pallas_call x1 -> x2, Pallas kernels: 0.22 us -> 2.35 us  [the longest x1 2.05 us: stage(): pl.pallas_call(stage_kernel, out_shape=pltpu.VMEM((len(columns), *columns...]
    ppermute x9 -> x11, waiting for transfers between devices: 10.1 us -> 11.1 us  [the longest x7 5 us: on_device(): around = lambda by, block: lax.ppermute(block, both_axes, along_z(by))]
    ppermute x9 -> x11, starting transfers between devices: 15.7 us -> 16.2 us  [the longest x7 10.4 us: on_device(): around = lambda by, block: lax.ppermute(block, both_axes, along_z(by))]
  transfers between devices with their start and end apart: 26 -> 27, of which waited for: 14 -> 12; matrix products, arithmetic and copies ran while one was open for 3% -> 3% of each run, Pallas kernels for 8% -> 10%
where the time goes in v5:
time: 138 us; the launch traced here: 136 us
  starting transfers between devices  43.4 us (31%)
  waiting for transfers between devices  39.2 us (28%)
  blocking collectives  29.2 us (21%)
  Pallas kernels  19.7 us (14%)
  other arithmetic  3.35 us (2%)
    all_to_all x1, blocking collectives, on_device(): lax.all_to_all(partial.reshape(HALF, rows, 2 * oris), 'dom', 0, 0, axis_i...  29.2 us
    ppermute x7, waiting for transfers between devices, on_device(): send = lambda block, perm: lax.ppermute(block, 'orient', perm)  13.7 us
    ppermute x1, waiting for transfers between devices, on_device(): s_hi = lax.ppermute(slices, 'dom', Y_HIGH)  10.8 us
    ppermute x7, starting transfers between devices, on_device(): around = lambda by, block: lax.ppermute(block, both_axes, along_z(by))  10.4 us
    pallas_call x3, Pallas kernels, add_score(): pl.pallas_call(functools.partial(score_kernel, count), out_shape=(total,...  9.25 us
    all_to_all x1, starting transfers between devices, on_device(): own = lax.all_to_all(own, 'dom', 0, 0, axis_index_groups=Z_GROUPS)  8.48 us
    ppermute x7, starting transfers between devices, on_device(): send = lambda block, perm: lax.ppermute(block, 'orient', perm)  6.52 us
    all_to_all x1, starting transfers between devices, on_device(): stats = lax.all_to_all(stats, 'orient', 0, 0)  6.16 us
  transfers between devices with their start and end apart: 27, of which 12 were waited for; matrix products, arithmetic and copies ran while one was open for 3% of the time, Pallas kernels for 10%

profile of v5, /device:TPU:2, one launch (start us, length us, event | category | flops | bytes accessed | tf_op | source)
XLA Modules:
  0.0 136.4 jit_solution(13586602598333731223)
XLA Ops:
  0.6 3.3 %collective-permute-start.3 = (bf16[256,2048]{1,0:T(8,128)(2,1)}, bf16[256,2048]{1,0:T(8,128)(2,1)S(1)}, u32[]{:S(2)}, u32[]{:S(2)}) collective-permute-start(bf16[256,2048]{1,0:T(8,128)(2,1)} %refs_1_.1), channel_id=1, source_target_pairs={{0,8},{1,9},{2,10},{3,11},{4,12},{5,13},{6,14},{7,15},{8,0},{9,1},... | collective-permute-start | bytes 3145736 | tf_op jit(solution)/shard_map/ppermute | solution.py:318
  3.9 0.7 pad_add_fusion.1.place
  4.6 3.4 %shift.1 = bf16[8,2,48,256]{3,2,1,0:T(8,128)(2,1)} custom-call(s32[4]{0:T(128)} %pad_add_fusion.1.place, s32[2,96]{1,0:T(2,128)} %bitcast.24, bf16[96,32768]{1,0:T(8,128)(2,1)} %images.1), custom_call_target="tpu_custom_call" | custom-call | tf_op jit(solution)/shard_map/shift/pallas_call | solution.py:99
  8.0 8.5 %all-to-all-start = ((bf16[8,2,48,256]{3,2,1,0:T(8,128)(2,1)}), bf16[8,2,48,256]{3,2,1,0:T(8,128)(2,1)S(1)}, u32[]{:S(2)}, u32[]{:S(2)}) async-start(bf16[8,2,48,256]{3,2,1,0:T(8,128)(2,1)} %shift.1), calls=%async_computation | async-start | bytes 786432 | tf_op jit(solution)/shard_map/all_to_all | solution.py:329
  16.6 10.8 %collective-permute-done.3.refs_8_.refs_9_.refs_10_.refs_11_.refs_6_.refs_7_.refs_2_ = bf16[256,2048]{1,0:T(8,128)(2,1)S(1)} collective-permute-done((bf16[256,2048]{1,0:T(8,128)(2,1)}, bf16[256,2048]{1,0:T(8,128)(2,1)S(1)}, u32[]{:S(2)}, u32[]{:S(2)}) %collective-permute-start.3) | collective-permute-done | bytes 1048608 | tf_op jit(solution)/shard_map/ppermute | solution.py:318
  27.3 3.5 %all-to-all-done.refs_0_ = bf16[8,2,48,256]{3,2,1,0:T(8,128)(2,1)S(1)} async-done(((bf16[8,2,48,256]{3,2,1,0:T(8,128)(2,1)}), bf16[8,2,48,256]{3,2,1,0:T(8,128)(2,1)S(1)}, u32[]{:S(2)}, u32[]{:S(2)}) %all-to-all-start) | async-done | bytes 393248 | tf_op jit(solution)/shard_map/all_to_all | solution.py:329
  30.9 0.5 collective-permute-start
  31.6 1.5 %collective-permute-start.6 = (bf16[8,2,48,256]{3,2,1,0:T(8,128)(2,1)S(1)}, bf16[8,2,48,256]{3,2,1,0:T(8,128)(2,1)}, u32[]{:S(2)}, u32[]{:S(2)}) collective-permute-start(bf16[8,2,48,256]{3,2,1,0:T(8,128)(2,1)S(1)} %all-to-all-done.refs_0_), channel_id=1, source_target_pairs={{0,32},{16,112},{32,64},{48,16},{64,96},{80,48},{96,0},{112,80},{1... | collective-permute-start | bytes 1179656 | tf_op jit(solution)/shard_map/ppermute | solution.py:331
  33.1 0.7 collective-permute-start.8
  33.7 7.9 %collective-permute-done.refs_2_ = bf16[8,2,48,256]{3,2,1,0:T(8,128)(2,1)} collective-permute-done((bf16[8,2,48,256]{3,2,1,0:T(8,128)(2,1)S(1)}, bf16[8,2,48,256]{3,2,1,0:T(8,128)(2,1)}, u32[]{:S(2)}, u32[]{:S(2)}) %collective-permute-start) | collective-permute-done | bytes 393248 | tf_op jit(solution)/shard_map/ppermute | solution.py:331
  41.6 0.7 collective-permute-start.1
  42.4 0.3 multiply_reduce_fusion.3
  42.7 0.3 multiply_reduce_fusion.2
  43.1 0.6 collective-permute-start.7
  43.7 0.9 collective-permute-done.8.refs_3_
  44.6 0.8 collective-permute-start.9
  45.4 4.9 %collective-permute-done.1.refs_1_ = bf16[8,2,48,256]{3,2,1,0:T(8,128)(2,1)} collective-permute-done((bf16[8,2,48,256]{3,2,1,0:T(8,128)(2,1)}, bf16[8,2,48,256]{3,2,1,0:T(8,128)(2,1)}, u32[]{:S(2)}, u32[]{:S(2)}) %collective-permute-start.1) | collective-permute-done | bytes 393248 | tf_op jit(solution)/shard_map/ppermute | solution.py:331
  50.3 1.7 %collective-permute-start.2 = (bf16[8,2,48,256]{3,2,1,0:T(8,128)(2,1)}, bf16[8,2,48,256]{3,2,1,0:T(8,128)(2,1)S(1)}, u32[]{:S(2)}, u32[]{:S(2)}) collective-permute-start(bf16[8,2,48,256]{3,2,1,0:T(8,128)(2,1)} %collective-permute-done.1.refs_1_), channel_id=1, source_target_pairs={{0,96},{16,48},{32,0},{48,80},{64,32},{80,112},{96,64},{112,16},{1... | collective-permute-start | bytes 1179656 | tf_op jit(solution)/shard_map/ppermute | solution.py:331
  52.0 0.3 multiply_reduce_fusion.1
  52.3 1.5 %multiply_reduce_fusion = f32[256]{0:T(256)S(1)} fusion(bf16[256,2048]{1,0:T(8,128)(2,1)} %collective-permute-done.5.refs_16_.refs_17_.refs_18_.refs_19_.refs_12_.refs_13_.refs_14_.refs_4_), kind=kLoop, calls=%fused_computation | loop fusion | flops 1572608 | bytes 1049600 | tf_op jit(solution)/shard_map/reduce_sum | solution.py:307
  53.9 3.8 %score.3 = (f32[384,512]{1,0:T(8,128)S(1)}, bf16[8,8,48,256]{3,2,1,0:T(8,128)(2,1)}, bf16[8,8,48,256]{3,2,1,0:T(8,128)(2,1)}) custom-call(s32[4]{0:T(128)S(1)} %pad_add_fusion.3.place, bf16[8,2,48,256]{3,2,1,0:T(8,128)(2,1)S(1)} %all-to-all-done.refs_0_, bf16[8,2,48,256]{3,2,1,0:T(8,128)(2,1)} %collective-permute-done.6.refs_1_, ...), custom_call_target="tpu_custom_call" | custom-call | tf_op jit(solution)/shard_map/score/pallas_call | solution.py:144
  57.7 2.9 %score.4 = (f32[384,512]{1,0:T(8,128)S(1)}, bf16[8,8,48,256]{3,2,1,0:T(8,128)(2,1)}, bf16[8,8,48,256]{3,2,1,0:T(8,128)(2,1)}) custom-call(s32[3]{0:T(128)S(1)} %pad_add_fusion.2.place, bf16[8,2,48,256]{3,2,1,0:T(8,128)(2,1)S(1)} %collective-permute-done.7.refs_0_, ...), custom_call_target="tpu_custom_call", output_to_operand_aliasing={{1}: (17, {}), {2}: (18, {})} | custom-call | tf_op jit(solution)/shard_map/score/pallas_call | solution.py:144
  60.6 2.6 %score.5 = (f32[384,512]{1,0:T(8,128)}, bf16[8,8,48,256]{3,2,1,0:T(8,128)(2,1)}, bf16[8,8,48,256]{3,2,1,0:T(8,128)(2,1)}) custom-call(s32[1]{0:T(128)} %bitcast.3.place, bf16[8,2,48,256]{3,2,1,0:T(8,128)(2,1)S(1)} %collective-permute-done.2.refs_0_, bf16[256,2048]{1,0:T(8,128)(2,1)S(1)} %copy-done, ...), custom_call_target="tpu_custom_call", output_to_operand_aliasing={{1}: (7, {}), {2}: (8, {})} | custom-call | tf_op jit(solution)/shard_map/score/pallas_call | solution.py:144
  63.2 2.0 %collective-permute-start.23 = (bf16[8,8,48,256]{3,2,1,0:T(8,128)(2,1)}, bf16[8,8,48,256]{3,2,1,0:T(8,128)(2,1)S(1)}, u32[]{:S(2)}, u32[]{:S(2)}) collective-permute-start(bf16[8,8,48,256]{3,2,1,0:T(8,128)(2,1)} %get-tuple-element.41), channel_id=1, source_target_pairs={{0,8},{1,9},{2,10},{3,11},{4,12},{5,13},{6,14},{7,15},{8,0},{9,1},... | collective-permute-start | bytes 4718600 | tf_op jit(solution)/shard_map/ppermute | solution.py:353
  65.2 29.2 %all_to_all.15.pieces = f32[8,48,512]{2,1,0:T(8,128)S(1)} all-to-all(f32[8,48,512]{2,1,0:T(8,128)} %bitcast.20), channel_id=1, replica_groups={{0,1,2,3,4,5,6,7},{8,9,10,11,12,13,14,15},{16,17,18,19,20,21,22,23},{24..., dimensions={0} | all-to-all | bytes 1572864 | tf_op jit(solution)/shard_map/all_to_all | solution.py:355
  94.5 0.9 total.1
  95.3 6.2 %all-to-all-start.2 = ((f32[16,8,128]{2,1,0:T(8,128)}), f32[16,8,128]{2,1,0:T(8,128)S(1)}, u32[]{:S(2)}, u32[]{:S(2)}) async-start(f32[16,8,128]{2,1,0:T(8,128)} %get-tuple-element.31), calls=%async_computation.2 | async-start | bytes 131072 | tf_op jit(solution)/shard_map/all_to_all | solution.py:358
  101.5 0.1 collective-permute-start.11
  101.6 1.1 collective-permute-start.12
  102.8 2.1 %collective-permute-start.13 = (f32[48,256]{1,0:T(8,128)S(1)}, f32[48,256]{1,0:T(8,128)S(1)}, u32[]{:S(2)}, u32[]{:S(2)}) collective-permute-start(f32[48,256]{1,0:T(8,128)S(1)} %get-tuple-element.33), channel_id=1, source_target_pairs={{0,24},{1,25},{2,26},{3,27},{4,28},{5,29},{6,30},{7,31},{8,16},{9,... | collective-permute-start | bytes 147464 | tf_op jit(solution)/shard_map/ppermute | solution.py:363
  104.9 0.4 collective-permute-start.22
  105.3 1.9 %collective-permute-done.12.near_hi = f32[48,256]{1,0:T(8,128)S(1)} collective-permute-done((f32[48,256]{1,0:T(8,128)S(1)}, f32[48,256]{1,0:T(8,128)S(1)}, u32[]{:S(2)}, u32[]{:S(2)}) %collective-permute-start.12) | collective-permute-done | bytes 49184 | tf_op jit(solution)/shard_map/ppermute | solution.py:362
  107.3 0.8 collective-permute-done.13.came_hi
  108.1 2.4 %collective-permute-start.14 = (f32[16,8,128]{2,1,0:T(8,128)S(1)}, f32[16,8,128]{2,1,0:T(8,128)S(1)}, u32[]{:S(2)}, u32[]{:S(2)}) collective-permute-start(f32[16,8,128]{2,1,0:T(8,128)S(1)} %all-to-all-done.2.stats), channel_id=1, source_target_pairs={{0,8},{1,9},{2,10},{3,11},{4,12},{5,13},{6,14},{7,15},{8,0},{9,1},... | collective-permute-start | bytes 196616 | tf_op jit(solution)/shard_map/ppermute | solution.py:366
  110.5 3.4 %collective-permute-done.14.stats_hi = f32[16,8,128]{2,1,0:T(8,128)S(1)} collective-permute-done((f32[16,8,128]{2,1,0:T(8,128)S(1)}, f32[16,8,128]{2,1,0:T(8,128)S(1)}, u32[]{:S(2)}, u32[]{:S(2)}) %collective-permute-start.14) | collective-permute-done | bytes 65568 | tf_op jit(solution)/shard_map/ppermute | solution.py:366
  113.9 0.3 weigh.1
  114.3 0.6 collective-permute-start.15
  114.9 0.2 collective-permute-start.16
  115.1 2.7 %collective-permute-start.19 = (bf16[4,48,256]{2,1,0:T(8,128)(2,1)S(1)}, bf16[4,48,256]{2,1,0:T(8,128)(2,1)}, u32[]{:S(2)}, u32[]{:S(2)}) collective-permute-start(bf16[4,48,256]{2,1,0:T(8,128)(2,1)S(1)} %get-tuple-element.39.refs_0_), channel_id=1, source_target_pairs={{0,7},{1,0},{2,1},{3,2},{4,3},{5,4},{6,5},{7,6},{8,15},{9,8},{10,9... | collective-permute-start | bytes 294920 | tf_op jit(solution)/shard_map/ppermute | solution.py:370
  117.8 2.7 %collective-permute-start.21 = (bf16[4,48,256]{2,1,0:T(8,128)(2,1)S(1)}, bf16[4,48,256]{2,1,0:T(8,128)(2,1)}, u32[]{:S(2)}, u32[]{:S(2)}) collective-permute-start(bf16[4,48,256]{2,1,0:T(8,128)(2,1)S(1)} %get-tuple-element.39.refs_0_), channel_id=1, source_target_pairs={{0,6},{1,7},{2,0},{3,1},{4,2},{5,3},{6,4},{7,5},{8,14},{9,15},{10,... | collective-permute-start | bytes 294920 | tf_op jit(solution)/shard_map/ppermute | solution.py:370
  120.5 1.4 %collective-permute-done.15.refs_1_ = bf16[4,48,256]{2,1,0:T(8,128)(2,1)S(1)} collective-permute-done((bf16[4,48,256]{2,1,0:T(8,128)(2,1)S(1)}, bf16[4,48,256]{2,1,0:T(8,128)(2,1)S(1)}, u32[]{:S(2)}, u32[]{:S(2)}) %collective-permute-start.15) | collective-permute-done | bytes 98336 | tf_op jit(solution)/shard_map/ppermute | solution.py:370
  122.0 2.1 %collective-permute-done.16.refs_2_ = bf16[4,48,256]{2,1,0:T(8,128)(2,1)S(1)} collective-permute-done((bf16[4,48,256]{2,1,0:T(8,128)(2,1)S(1)}, bf16[4,48,256]{2,1,0:T(8,128)(2,1)S(1)}, u32[]{:S(2)}, u32[]{:S(2)}) %collective-permute-start.16) | collective-permute-done | bytes 98336 | tf_op jit(solution)/shard_map/ppermute | solution.py:370
  124.0 4.1 %collective-permute-start.20 = (bf16[4,48,256]{2,1,0:T(8,128)(2,1)}, bf16[4,48,256]{2,1,0:T(8,128)(2,1)}, u32[]{:S(2)}, u32[]{:S(2)}) collective-permute-start(bf16[4,48,256]{2,1,0:T(8,128)(2,1)} %collective-permute-done.19.refs_7_), channel_id=1, source_target_pairs={{0,6},{1,7},{2,0},{3,1},{4,2},{5,3},{6,4},{7,5},{8,14},{9,15},{10,... | collective-permute-start | bytes 294920 | tf_op jit(solution)/shard_map/ppermute | solution.py:370
  128.3 0.6 reshape.74
  128.8 2.0 %stage.1.refs_8_ = bf16[4,8,8,48,256]{4,3,2,1,0:T(8,128)(2,1)S(1)} custom-call(bf16[8,8,48,256]{3,2,1,0:T(8,128)(2,1)S(1)} %copy-done.1, bf16[8,8,48,256]{3,2,1,0:T(8,128)(2,1)} %collective-permute-done.22.refs_1_, bf16[8,8,48,256]{3,2,1,0:T(8,128)(2,1)S(1)} %collective-permute-done.23.refs_2_, bf16[8,8,48,256]{3,2,1,0:T(8,128)(2,1)} %collective-permute-done.24.refs_3_), custom_call_target="tpu_custom_call" | custom-call | bytes 12582912 | tf_op jit(solution)/shard_map/stage/pallas_call | solution.py:251
  130.9 0.4 collective-permute-done.17.refs_3_
  131.3 1.1 collective-permute-done.18.refs_4_
  132.4 3.8 %project.1 = f32[256,2048]{1,0:T(8,128)} custom-call(s32[2]{0:T(128)S(1)} %pad_add_fusion.place, bf16[4,48,256]{2,1,0:T(8,128)(2,1)S(1)} %get-tuple-element.39.refs_0_, bf16[4,48,256]{2,1,0:T(8,128)(2,1)S(1)} %collective-permute-done.15.refs_1_, bf16[4,48,256]{2,1,0:T(8,128)(2,1)S(1)} %collective-permute-done.16.refs_2_, ...), custom_call_target="tpu_custom_call" | custom-call | tf_op jit(solution)/shard_map/project/pallas_call | solution.py:290
  (36 shorter events, 0.7 us)
Async XLA Ops:
  0.6 26.7 %collective-permute-start.3 = (bf16[256,2048]{1,0:T(8,128)(2,1)}, bf16[256,2048]{1,0:T(8,128)(2,1)S(1)}, u32[]{:S(2)}, u32[]{:S(2)}) collective-permute-start(bf16[256,2048]{1,0:T(8,128)(2,1)} %refs_1_.1), channel_id=1, source_target_pairs={{0,8},{1,9},{2,10},{3,11},{4,12},{5,13},{6,14},{7,15},{8,0},{9,1},... | collective-permute-start | bytes 3145736 | tf_op jit(solution)/shard_map/ppermute | solution.py:318
  4.6 11.9 %copy-start = (bf16[256,2048]{1,0:T(8,128)(2,1)S(1)}, bf16[256,2048]{1,0:T(8,128)(2,1)}, u32[]{:S(2)}) copy-start(bf16[256,2048]{1,0:T(8,128)(2,1)} %refs_1_.1) | copy-start | bytes 3145732
  4.6 26.9 %copy-start.2 = (s32[256]{0:T(256)S(1)}, s32[256]{0:T(256)}, u32[]{:S(2)}) copy-start(s32[256]{0:T(256)} %param.8) | copy-start | bytes 3076
  4.6 26.9 %copy-start.3 = (f32[8]{0:T(128)S(1)}, f32[8]{0:T(128)}, u32[]{:S(2)}) copy-start(f32[8]{0:T(128)} %param.9) | copy-start | bytes 100
  8.0 22.9 %all-to-all-start = ((bf16[8,2,48,256]{3,2,1,0:T(8,128)(2,1)}), bf16[8,2,48,256]{3,2,1,0:T(8,128)(2,1)S(1)}, u32[]{:S(2)}, u32[]{:S(2)}) async-start(bf16[8,2,48,256]{3,2,1,0:T(8,128)(2,1)} %shift.1), calls=%async_computation | async-start | bytes 786432 | tf_op jit(solution)/shard_map/all_to_all | solution.py:329
  16.5 26.6 %collective-permute-start.4 = (bf16[256,2048]{1,0:T(8,128)(2,1)S(1)}, bf16[256,2048]{1,0:T(8,128)(2,1)S(1)}, u32[]{:S(2)}, u32[]{:S(2)}) collective-permute-start(bf16[256,2048]{1,0:T(8,128)(2,1)S(1)} %copy-done), channel_id=1, source_target_pairs={{0,16},{16,0},{32,48},{48,32},{64,80},{80,64},{96,112},{112,96},{1... | collective-permute-start | bytes 3145736 | tf_op jit(solution)/shard_map/ppermute | solution.py:319
  27.3 25.0 %collective-permute-start.5 = (bf16[256,2048]{1,0:T(8,128)(2,1)S(1)}, bf16[256,2048]{1,0:T(8,128)(2,1)}, u32[]{:S(2)}, u32[]{:S(2)}) collective-permute-start(bf16[256,2048]{1,0:T(8,128)(2,1)S(1)} %collective-permute-done.3.refs_8_.refs_9_.refs_10_.refs_11_.refs_6_.refs_7_.refs_2_), channel_id=1, source_target_pairs={{0,16},{16,0},{32,48},{48,32},{64,80},{80,64},{96,112},{112,96},{1... | collective-permute-start | bytes 3145736 | tf_op jit(solution)/shard_map/ppermute | solution.py:320
  30.9 10.8 %collective-permute-start = (bf16[8,2,48,256]{3,2,1,0:T(8,128)(2,1)S(1)}, bf16[8,2,48,256]{3,2,1,0:T(8,128)(2,1)}, u32[]{:S(2)}, u32[]{:S(2)}) collective-permute-start(bf16[8,2,48,256]{3,2,1,0:T(8,128)(2,1)S(1)} %all-to-all-done.refs_0_), channel_id=1, source_target_pairs={{0,96},{16,48},{32,0},{48,80},{64,32},{80,112},{96,64},{112,16},{1... | collective-permute-start | bytes 1179656 | tf_op jit(solution)/shard_map/ppermute | solution.py:331
  31.6 11.4 %collective-permute-start.6 = (bf16[8,2,48,256]{3,2,1,0:T(8,128)(2,1)S(1)}, bf16[8,2,48,256]{3,2,1,0:T(8,128)(2,1)}, u32[]{:S(2)}, u32[]{:S(2)}) collective-permute-start(bf16[8,2,48,256]{3,2,1,0:T(8,128)(2,1)S(1)} %all-to-all-done.refs_0_), channel_id=1, source_target_pairs={{0,32},{16,112},{32,64},{48,16},{64,96},{80,48},{96,0},{112,80},{1... | collective-permute-start | bytes 1179656 | tf_op jit(solution)/shard_map/ppermute | solution.py:331
  33.1 11.6 %collective-permute-start.8 = (bf16[8,2,48,256]{3,2,1,0:T(8,128)(2,1)S(1)}, bf16[8,2,48,256]{3,2,1,0:T(8,128)(2,1)}, u32[]{:S(2)}, u32[]{:S(2)}) collective-permute-start(bf16[8,2,48,256]{3,2,1,0:T(8,128)(2,1)S(1)} %all-to-all-done.refs_0_), channel_id=1, source_target_pairs={{0,128},{16,144},{32,160},{48,176},{64,192},{80,208},{96,224},{112... | collective-permute-start | bytes 1179656 | tf_op jit(solution)/shard_map/ppermute | solution.py:331
  41.6 8.7 %collective-permute-start.1 = (bf16[8,2,48,256]{3,2,1,0:T(8,128)(2,1)}, bf16[8,2,48,256]{3,2,1,0:T(8,128)(2,1)}, u32[]{:S(2)}, u32[]{:S(2)}) collective-permute-start(bf16[8,2,48,256]{3,2,1,0:T(8,128)(2,1)} %collective-permute-done.refs_2_), channel_id=1, source_target_pairs={{0,128},{16,144},{32,160},{48,176},{64,192},{80,208},{96,224},{112... | collective-permute-start | bytes 1179656 | tf_op jit(solution)/shard_map/ppermute | solution.py:331
  43.0 10.9 %collective-permute-start.10 = (f32[256]{0:T(256)S(1)}, f32[256]{0:T(256)S(1)}, u32[]{:S(2)}, u32[]{:S(2)}) collective-permute-start(f32[256]{0:T(256)S(1)} %select_reduce_fusion), channel_id=1, source_target_pairs={{0,16},{16,0},{32,48},{48,32},{64,80},{80,64},{96,112},{112,96},{1... | collective-permute-start | bytes 3080 | tf_op jit(solution)/shard_map/ppermute | solution.py:323
  43.1 14.6 %collective-permute-start.7 = (bf16[8,2,48,256]{3,2,1,0:T(8,128)(2,1)}, bf16[8,2,48,256]{3,2,1,0:T(8,128)(2,1)S(1)}, u32[]{:S(2)}, u32[]{:S(2)}) collective-permute-start(bf16[8,2,48,256]{3,2,1,0:T(8,128)(2,1)} %collective-permute-done.refs_2_), channel_id=1, source_target_pairs={{0,96},{16,48},{32,0},{48,80},{64,32},{80,112},{96,64},{112,16},{1... | collective-permute-start | bytes 1179656 | tf_op jit(solution)/shard_map/ppermute | solution.py:331
  44.6 13.0 %collective-permute-start.9 = (bf16[8,2,48,256]{3,2,1,0:T(8,128)(2,1)}, bf16[8,2,48,256]{3,2,1,0:T(8,128)(2,1)S(1)}, u32[]{:S(2)}, u32[]{:S(2)}) collective-permute-start(bf16[8,2,48,256]{3,2,1,0:T(8,128)(2,1)} %collective-permute-done.8.refs_3_), channel_id=1, source_target_pairs={{0,32},{16,112},{32,64},{48,16},{64,96},{80,48},{96,0},{112,80},{1... | collective-permute-start | bytes 1179656 | tf_op jit(solution)/shard_map/ppermute | solution.py:331
  50.3 10.3 %collective-permute-start.2 = (bf16[8,2,48,256]{3,2,1,0:T(8,128)(2,1)}, bf16[8,2,48,256]{3,2,1,0:T(8,128)(2,1)S(1)}, u32[]{:S(2)}, u32[]{:S(2)}) collective-permute-start(bf16[8,2,48,256]{3,2,1,0:T(8,128)(2,1)} %collective-permute-done.1.refs_1_), channel_id=1, source_target_pairs={{0,96},{16,48},{32,0},{48,80},{64,32},{80,112},{96,64},{112,16},{1... | collective-permute-start | bytes 1179656 | tf_op jit(solution)/shard_map/ppermute | solution.py:331
  63.2 41.7 %copy-start.1 = (bf16[8,8,48,256]{3,2,1,0:T(8,128)(2,1)S(1)}, bf16[8,8,48,256]{3,2,1,0:T(8,128)(2,1)}, u32[]{:S(2)}) copy-start(bf16[8,8,48,256]{3,2,1,0:T(8,128)(2,1)} %get-tuple-element.40.refs_0_) | copy-start | bytes 4718596
  63.2 51.0 %collective-permute-start.23 = (bf16[8,8,48,256]{3,2,1,0:T(8,128)(2,1)}, bf16[8,8,48,256]{3,2,1,0:T(8,128)(2,1)S(1)}, u32[]{:S(2)}, u32[]{:S(2)}) collective-permute-start(bf16[8,8,48,256]{3,2,1,0:T(8,128)(2,1)} %get-tuple-element.41), channel_id=1, source_target_pairs={{0,8},{1,9},{2,10},{3,11},{4,12},{5,13},{6,14},{7,15},{8,0},{9,1},... | collective-permute-start | bytes 4718600 | tf_op jit(solution)/shard_map/ppermute | solution.py:353
  95.3 12.7 %all-to-all-start.2 = ((f32[16,8,128]{2,1,0:T(8,128)}), f32[16,8,128]{2,1,0:T(8,128)S(1)}, u32[]{:S(2)}, u32[]{:S(2)}) async-start(f32[16,8,128]{2,1,0:T(8,128)} %get-tuple-element.31), calls=%async_computation.2 | async-start | bytes 131072 | tf_op jit(solution)/shard_map/all_to_all | solution.py:358
  101.5 3.8 %collective-permute-start.11 = (f32[48,256]{1,0:T(8,128)S(1)}, f32[48,256]{1,0:T(8,128)S(1)}, u32[]{:S(2)}, u32[]{:S(2)}) collective-permute-start(f32[48,256]{1,0:T(8,128)S(1)} %get-tuple-element.33), channel_id=1, source_target_pairs={{0,16},{16,0},{32,48},{48,32},{64,80},{80,64},{96,112},{112,96},{1... | collective-permute-start | bytes 147464 | tf_op jit(solution)/shard_map/ppermute | solution.py:361
  101.6 5.6 %collective-permute-start.12 = (f32[48,256]{1,0:T(8,128)S(1)}, f32[48,256]{1,0:T(8,128)S(1)}, u32[]{:S(2)}, u32[]{:S(2)}) collective-permute-start(f32[48,256]{1,0:T(8,128)S(1)} %get-tuple-element.34.near), channel_id=1, source_target_pairs={{0,8},{1,9},{2,10},{3,11},{4,12},{5,13},{6,14},{7,15},{8,0},{9,1},... | collective-permute-start | bytes 147464 | tf_op jit(solution)/shard_map/ppermute | solution.py:362
  102.8 5.3 %collective-permute-start.13 = (f32[48,256]{1,0:T(8,128)S(1)}, f32[48,256]{1,0:T(8,128)S(1)}, u32[]{:S(2)}, u32[]{:S(2)}) collective-permute-start(f32[48,256]{1,0:T(8,128)S(1)} %get-tuple-element.33), channel_id=1, source_target_pairs={{0,24},{1,25},{2,26},{3,27},{4,28},{5,29},{6,30},{7,31},{8,16},{9,... | collective-permute-start | bytes 147464 | tf_op jit(solution)/shard_map/ppermute | solution.py:363
  104.9 12.9 %collective-permute-start.22 = (bf16[8,8,48,256]{3,2,1,0:T(8,128)(2,1)S(1)}, bf16[8,8,48,256]{3,2,1,0:T(8,128)(2,1)}, u32[]{:S(2)}, u32[]{:S(2)}) collective-permute-start(bf16[8,8,48,256]{3,2,1,0:T(8,128)(2,1)S(1)} %copy-done.1), channel_id=1, source_target_pairs={{0,16},{16,0},{32,48},{48,32},{64,80},{80,64},{96,112},{112,96},{1... | collective-permute-start | bytes 4718600 | tf_op jit(solution)/shard_map/ppermute | solution.py:354
  108.1 5.8 %collective-permute-start.14 = (f32[16,8,128]{2,1,0:T(8,128)S(1)}, f32[16,8,128]{2,1,0:T(8,128)S(1)}, u32[]{:S(2)}, u32[]{:S(2)}) collective-permute-start(f32[16,8,128]{2,1,0:T(8,128)S(1)} %all-to-all-done.2.stats), channel_id=1, source_target_pairs={{0,8},{1,9},{2,10},{3,11},{4,12},{5,13},{6,14},{7,15},{8,0},{9,1},... | collective-permute-start | bytes 196616 | tf_op jit(solution)/shard_map/ppermute | solution.py:366
  114.2 14.7 %collective-permute-start.24 = (bf16[8,8,48,256]{3,2,1,0:T(8,128)(2,1)S(1)}, bf16[8,8,48,256]{3,2,1,0:T(8,128)(2,1)}, u32[]{:S(2)}, u32[]{:S(2)}) collective-permute-start(bf16[8,8,48,256]{3,2,1,0:T(8,128)(2,1)S(1)} %collective-permute-done.23.refs_2_), channel_id=1, source_target_pairs={{0,16},{16,0},{32,48},{48,32},{64,80},{80,64},{96,112},{112,96},{1... | collective-permute-start | bytes 4718600 | tf_op jit(solution)/shard_map/ppermute | solution.py:368
  114.3 7.7 %collective-permute-start.15 = (bf16[4,48,256]{2,1,0:T(8,128)(2,1)S(1)}, bf16[4,48,256]{2,1,0:T(8,128)(2,1)S(1)}, u32[]{:S(2)}, u32[]{:S(2)}) collective-permute-start(bf16[4,48,256]{2,1,0:T(8,128)(2,1)S(1)} %get-tuple-element.39.refs_0_), channel_id=1, source_target_pairs={{0,1},{1,2},{2,3},{3,4},{4,5},{5,6},{6,7},{7,0},{8,9},{9,10},{10,1... | collective-permute-start | bytes 294920 | tf_op jit(solution)/shard_map/ppermute | solution.py:370
  114.9 9.1 %collective-permute-start.16 = (bf16[4,48,256]{2,1,0:T(8,128)(2,1)S(1)}, bf16[4,48,256]{2,1,0:T(8,128)(2,1)S(1)}, u32[]{:S(2)}, u32[]{:S(2)}) collective-permute-start(bf16[4,48,256]{2,1,0:T(8,128)(2,1)S(1)} %get-tuple-element.39.refs_0_), channel_id=1, source_target_pairs={{0,2},{1,3},{2,4},{3,5},{4,6},{5,7},{6,0},{7,1},{8,10},{9,11},{10,... | collective-permute-start | bytes 294920 | tf_op jit(solution)/shard_map/ppermute | solution.py:370
  115.1 8.9 %collective-permute-start.19 = (bf16[4,48,256]{2,1,0:T(8,128)(2,1)S(1)}, bf16[4,48,256]{2,1,0:T(8,128)(2,1)}, u32[]{:S(2)}, u32[]{:S(2)}) collective-permute-start(bf16[4,48,256]{2,1,0:T(8,128)(2,1)S(1)} %get-tuple-element.39.refs_0_), channel_id=1, source_target_pairs={{0,7},{1,0},{2,1},{3,2},{4,3},{5,4},{6,5},{7,6},{8,15},{9,8},{10,9... | collective-permute-start | bytes 294920 | tf_op jit(solution)/shard_map/ppermute | solution.py:370
  117.8 13.1 %collective-permute-start.21 = (bf16[4,48,256]{2,1,0:T(8,128)(2,1)S(1)}, bf16[4,48,256]{2,1,0:T(8,128)(2,1)}, u32[]{:S(2)}, u32[]{:S(2)}) collective-permute-start(bf16[4,48,256]{2,1,0:T(8,128)(2,1)S(1)} %get-tuple-element.39.refs_0_), channel_id=1, source_target_pairs={{0,6},{1,7},{2,0},{3,1},{4,2},{5,3},{6,4},{7,5},{8,14},{9,15},{10,... | collective-permute-start | bytes 294920 | tf_op jit(solution)/shard_map/ppermute | solution.py:370
  122.0 9.4 %collective-permute-start.17 = (bf16[4,48,256]{2,1,0:T(8,128)(2,1)S(1)}, bf16[4,48,256]{2,1,0:T(8,128)(2,1)}, u32[]{:S(2)}, u32[]{:S(2)}) collective-permute-start(bf16[4,48,256]{2,1,0:T(8,128)(2,1)S(1)} %collective-permute-done.15.refs_1_), channel_id=1, source_target_pairs={{0,2},{1,3},{2,4},{3,5},{4,6},{5,7},{6,0},{7,1},{8,10},{9,11},{10,... | collective-permute-start | bytes 294920 | tf_op jit(solution)/shard_map/ppermute | solution.py:370
  124.0 8.3 %collective-permute-start.18 = (bf16[4,48,256]{2,1,0:T(8,128)(2,1)S(1)}, bf16[4,48,256]{2,1,0:T(8,128)(2,1)}, u32[]{:S(2)}, u32[]{:S(2)}) collective-permute-start(bf16[4,48,256]{2,1,0:T(8,128)(2,1)S(1)} %collective-permute-done.16.refs_2_), channel_id=1, source_target_pairs={{0,2},{1,3},{2,4},{3,5},{4,6},{5,7},{6,0},{7,1},{8,10},{9,11},{10,... | collective-permute-start | bytes 294920 | tf_op jit(solution)/shard_map/ppermute | solution.py:370
  124.0 8.3 %collective-permute-start.20 = (bf16[4,48,256]{2,1,0:T(8,128)(2,1)}, bf16[4,48,256]{2,1,0:T(8,128)(2,1)}, u32[]{:S(2)}, u32[]{:S(2)}) collective-permute-start(bf16[4,48,256]{2,1,0:T(8,128)(2,1)} %collective-permute-done.19.refs_7_), channel_id=1, source_target_pairs={{0,6},{1,7},{2,0},{3,1},{4,2},{5,3},{6,4},{7,5},{8,14},{9,15},{10,... | collective-permute-start | bytes 294920 | tf_op jit(solution)/shard_map/ppermute | solution.py:370

commit v6 on v5

--- a/solution.py
+++ b/solution.py
@@ -21,7 +21,6 @@
 CORE = [(i, i ^ 1) for i in range(ORI)]
 Y_LOW = [(i, i ^ 8) for i in range(ORI)]
 Y_HIGH = [(i, i ^ 8) for i in range(DOM)]
-CORE_HIGH = [(i, i ^ (DOM + 8)) for i in range(ORI * DOM)]
 
 
 def along_x(by):
@@ -198,43 +197,39 @@
     )(pieces)
 
 
-def weight_kernel(place, near, came, near_hi, came_hi, stats, stats_hi, weights, log_norm):
+def weight_kernel(place, near, came, stats, weights, log_norm):
     rows = near.shape[0]
     core = place[0]
     used = lax.broadcasted_iota(jnp.int32, (1, LANES), 1) < rows
     peak, total = [], []
-    for hi, given in enumerate((stats, stats_hi)):
-        for c in range(2):
-            peaks = jnp.concatenate([given[p, 0:1, :] for p in range(c, ORI, 2)], axis=0)
-            masses = jnp.concatenate([given[p, 1:2, :] for p in range(c, ORI, 2)], axis=0)
-            top = jnp.max(peaks, axis=0, keepdims=True)
-            mass = jnp.sum(masses * jnp.exp(peaks - top), axis=0, keepdims=True)
-            peak.append(top)
-            total.append(jnp.where(used, mass, 1.0))
-            if hi == 0:
-                log_norm[c : c + 1, :] = top + jnp.log(total[c])
-    for at, part in enumerate((near, came, near_hi, came_hi)):
-        first = (core if at % 2 == 0 else 1 - core) == 0
-        hi = 2 * (at // 2)
-        top = to_column(jnp.where(first, peak[hi], peak[hi + 1]), rows)
-        mass = to_column(jnp.where(first, total[hi], total[hi + 1]), rows)
+    for c in range(2):
+        peaks = jnp.concatenate([stats[p, 0:1, :] for p in range(c, ORI, 2)], axis=0)
+        masses = jnp.concatenate([stats[p, 1:2, :] for p in range(c, ORI, 2)], axis=0)
+        top = jnp.max(peaks, axis=0, keepdims=True)
+        mass = jnp.sum(masses * jnp.exp(peaks - top), axis=0, keepdims=True)
+        peak.append(top)
+        total.append(jnp.where(used, mass, 1.0))
+        log_norm[c : c + 1, :] = top + jnp.log(total[c])
+    for at, (c, part) in enumerate(((core, near), (1 - core, came))):
+        top = to_column(jnp.where(c == 0, peak[0], peak[1]), rows)
+        mass = to_column(jnp.where(c == 0, total[0], total[1]), rows)
         weights[at] = (jnp.exp(part[...] - top) / mass).astype(jnp.bfloat16)
 
 
-def weigh(place, scores, stats, stats_hi):
-    rows, oris = scores[0].shape
+def weigh(place, near, came, stats):
+    rows, oris = near.shape
     vmem = pl.BlockSpec(memory_space=pltpu.VMEM)
     return pl.pallas_call(
         weight_kernel,
         out_shape=(
-            jax.ShapeDtypeStruct((4, rows, oris), jnp.bfloat16),
+            jax.ShapeDtypeStruct((2, rows, oris), jnp.bfloat16),
             jax.ShapeDtypeStruct((2, LANES), jnp.float32),
         ),
-        in_specs=[pl.BlockSpec(memory_space=pltpu.SMEM)] + [vmem] * 6,
+        in_specs=[pl.BlockSpec(memory_space=pltpu.SMEM), vmem, vmem, vmem],
         out_specs=(vmem, vmem),
         compiler_params=pltpu.CompilerParams(vmem_limit_bytes=16 * MIB),
         name="weigh",
-    )(place, *scores, stats, stats_hi)
+    )(place, near, came, stats)
 
 
 def stage_kernel(*refs):
@@ -354,20 +349,14 @@
     from_core = lax.ppermute(keep, "orient", CORE)
     pieces = lax.all_to_all(partial.reshape(HALF, rows, 2 * oris), "dom", 0, 0, axis_index_groups=Z_GROUPS)
     near, other, stats = total_score(pieces)
-    both_axes = ("orient", "dom")
+    came = lax.ppermute(other, "orient", CORE)
     stats = lax.all_to_all(stats, "orient", 0, 0)
-    scores = (
-        near,
-        lax.ppermute(other, "orient", CORE),
-        lax.ppermute(near, "dom", Y_HIGH),
-        lax.ppermute(other, both_axes, CORE_HIGH),
-    )
-    stats, *scores = lax.optimization_barrier((stats, *scores))
-    weights, log_norm = weigh(core.astype(jnp.int32)[None], scores, stats, lax.ppermute(stats, "dom", Y_HIGH))
-    from_hi, _ = lax.optimization_barrier((from_hi, weights))
+    from_hi, stats, came = lax.optimization_barrier((from_hi, stats, came))
     from_both = lax.ppermute(from_hi, "orient", CORE)
-
-    around = lambda by, block: lax.ppermute(block, both_axes, along_z(by))
+    weights, log_norm = weigh(core.astype(jnp.int32)[None], near, came, stats)
+    weights = jnp.concatenate([weights, lax.ppermute(weights, "dom", Y_HIGH)])
+
+    around = lambda by, block: lax.ppermute(block, ("orient", "dom"), along_z(by))
     one, back_one = around(1, weights), around(-1, weights)
     two, back_two = around(2, weights), around(-2, weights)
     three, back_three = around(2, one), around(-2, back_one)

time: 138 us -> 135 us (0.978)
  blocking collectives: 29.2 us -> 0 us
  waiting for transfers between devices: 39.2 us -> 61.4 us
  starting transfers between devices: 43.4 us -> 47 us
    all_to_all x1 -> x0, blocking collectives: 29.2 us -> none  [on_device(): lax.all_to_all(partial.reshape(HALF, rows, 2 * oris), 'dom', 0, 0, axis_i...]
    all_to_all x0 -> x1, waiting for transfers between devices: none -> 20.8 us  [on_device(): lax.all_to_all(partial.reshape(HALF, rows, 2 * oris), 'dom', 0, 0, axis_i...]
    all_to_all x0 -> x1, starting transfers between devices: none -> 8.45 us  [on_device(): lax.all_to_all(partial.reshape(HALF, rows, 2 * oris), 'dom', 0, 0, axis_i...]
    ppermute x11 -> x9, starting transfers between devices: 16.2 us -> 11.6 us  [the longest x7 10.3 us: on_device(): lax.ppermute(block, ('orient', 'dom'), along_z(by))]
    all_to_all x1, waiting for transfers between devices: 0.01 us -> 3.6 us  [on_device(): stats = lax.all_to_all(stats, 'orient', 0, 0)]
    ppermute x11 -> x9, waiting for transfers between devices: 11.1 us -> 8.98 us  [the longest x1 4.54 us: on_device(): weights = jnp.concatenate([weights, lax.ppermute(weights, 'dom', Y_HIGH)])]
  transfers between devices with their start and end apart: 27 -> 26, of which waited for: 12 -> 12; matrix products, arithmetic and copies ran while one was open for 3% -> 3% of each run, Pallas kernels for 10% -> 10%
where the time goes in v6:
time: 135 us; the launch traced here: 133 us
  waiting for transfers between devices  61.4 us (45%)
  starting transfers between devices  47 us (35%)
  Pallas kernels  19.5 us (14%)
  other arithmetic  3.35 us (2%)
    all_to_all x1, waiting for transfers between devices, on_device(): lax.all_to_all(partial.reshape(HALF, rows, 2 * oris), 'dom', 0, 0, axis_i...  20.8 us
    ppermute x7, waiting for transfers between devices, on_device(): send = lambda block, perm: lax.ppermute(block, 'orient', perm)  13.7 us
    ppermute x1, waiting for transfers between devices, on_device(): s_hi = lax.ppermute(slices, 'dom', Y_HIGH)  10.8 us
    ppermute x7, starting transfers between devices, on_device(): lax.ppermute(block, ('orient', 'dom'), along_z(by))  10.3 us
    pallas_call x3, Pallas kernels, add_score(): pl.pallas_call(functools.partial(score_kernel, count), out_shape=(total,...  9.26 us
    all_to_all x1, starting transfers between devices, on_device(): own = lax.all_to_all(own, 'dom', 0, 0, axis_index_groups=Z_GROUPS)  8.48 us
    all_to_all x1, starting transfers between devices, on_device(): lax.all_to_all(partial.reshape(HALF, rows, 2 * oris), 'dom', 0, 0, axis_i...  8.45 us
    ppermute x7, starting transfers between devices, on_device(): send = lambda block, perm: lax.ppermute(block, 'orient', perm)  6.52 us
  transfers between devices with their start and end apart: 26, of which 12 were waited for; matrix products, arithmetic and copies ran while one was open for 3% of the time, Pallas kernels for 10%

profile of v6, /device:TPU:2, one launch (start us, length us, event | category | flops | bytes accessed | tf_op | source)
XLA Modules:
  0.0 132.9 jit_solution(9893528727676204285)
XLA Ops:
  0.6 3.3 %collective-permute-start.3 = (bf16[256,2048]{1,0:T(8,128)(2,1)}, bf16[256,2048]{1,0:T(8,128)(2,1)S(1)}, u32[]{:S(2)}, u32[]{:S(2)}) collective-permute-start(bf16[256,2048]{1,0:T(8,128)(2,1)} %refs_1_.1), channel_id=1, source_target_pairs={{0,8},{1,9},{2,10},{3,11},{4,12},{5,13},{6,14},{7,15},{8,0},{9,1},... | collective-permute-start | bytes 3145736 | tf_op jit(solution)/shard_map/ppermute | solution.py:313
  3.9 0.7 pad_add_fusion.1.place
  4.6 3.4 %shift.1 = bf16[8,2,48,256]{3,2,1,0:T(8,128)(2,1)} custom-call(s32[4]{0:T(128)} %pad_add_fusion.1.place, s32[2,96]{1,0:T(2,128)} %bitcast.24, bf16[96,32768]{1,0:T(8,128)(2,1)} %images.1), custom_call_target="tpu_custom_call" | custom-call | tf_op jit(solution)/shard_map/shift/pallas_call | solution.py:98
  8.0 8.5 %all-to-all-start = ((bf16[8,2,48,256]{3,2,1,0:T(8,128)(2,1)}), bf16[8,2,48,256]{3,2,1,0:T(8,128)(2,1)S(1)}, u32[]{:S(2)}, u32[]{:S(2)}) async-start(bf16[8,2,48,256]{3,2,1,0:T(8,128)(2,1)} %shift.1), calls=%async_computation | async-start | bytes 786432 | tf_op jit(solution)/shard_map/all_to_all | solution.py:324
  16.5 0.1 collective-permute-start.4
  16.6 10.8 %collective-permute-done.3.refs_8_.refs_9_.refs_10_.refs_11_.refs_6_.refs_7_.refs_2_ = bf16[256,2048]{1,0:T(8,128)(2,1)S(1)} collective-permute-done((bf16[256,2048]{1,0:T(8,128)(2,1)}, bf16[256,2048]{1,0:T(8,128)(2,1)S(1)}, u32[]{:S(2)}, u32[]{:S(2)}) %collective-permute-start.3) | collective-permute-done | bytes 1048608 | tf_op jit(solution)/shard_map/ppermute | solution.py:313
  27.3 3.5 %all-to-all-done.refs_0_ = bf16[8,2,48,256]{3,2,1,0:T(8,128)(2,1)S(1)} async-done(((bf16[8,2,48,256]{3,2,1,0:T(8,128)(2,1)}), bf16[8,2,48,256]{3,2,1,0:T(8,128)(2,1)S(1)}, u32[]{:S(2)}, u32[]{:S(2)}) %all-to-all-start) | async-done | bytes 393248 | tf_op jit(solution)/shard_map/all_to_all | solution.py:324
  30.9 0.5 collective-permute-start
  31.5 0.1 select_reduce_fusion
  31.6 1.5 %collective-permute-start.6 = (bf16[8,2,48,256]{3,2,1,0:T(8,128)(2,1)S(1)}, bf16[8,2,48,256]{3,2,1,0:T(8,128)(2,1)}, u32[]{:S(2)}, u32[]{:S(2)}) collective-permute-start(bf16[8,2,48,256]{3,2,1,0:T(8,128)(2,1)S(1)} %all-to-all-done.refs_0_), channel_id=1, source_target_pairs={{0,32},{16,112},{32,64},{48,16},{64,96},{80,48},{96,0},{112,80},{1... | collective-permute-start | bytes 1179656 | tf_op jit(solution)/shard_map/ppermute | solution.py:326
  33.1 0.7 collective-permute-start.8
  33.7 7.9 %collective-permute-done.refs_2_ = bf16[8,2,48,256]{3,2,1,0:T(8,128)(2,1)} collective-permute-done((bf16[8,2,48,256]{3,2,1,0:T(8,128)(2,1)S(1)}, bf16[8,2,48,256]{3,2,1,0:T(8,128)(2,1)}, u32[]{:S(2)}, u32[]{:S(2)}) %collective-permute-start) | collective-permute-done | bytes 393248 | tf_op jit(solution)/shard_map/ppermute | solution.py:326
  41.6 0.7 collective-permute-start.1
  42.4 0.3 multiply_reduce_fusion.3
  42.7 0.3 multiply_reduce_fusion.2
  43.0 0.1 collective-permute-start.10
  43.1 0.6 collective-permute-start.7
  43.7 0.9 collective-permute-done.8.refs_3_
  44.6 0.8 collective-permute-start.9
  45.4 4.9 %collective-permute-done.1.refs_1_ = bf16[8,2,48,256]{3,2,1,0:T(8,128)(2,1)} collective-permute-done((bf16[8,2,48,256]{3,2,1,0:T(8,128)(2,1)}, bf16[8,2,48,256]{3,2,1,0:T(8,128)(2,1)}, u32[]{:S(2)}, u32[]{:S(2)}) %collective-permute-start.1) | collective-permute-done | bytes 393248 | tf_op jit(solution)/shard_map/ppermute | solution.py:326
  50.3 1.7 %collective-permute-start.2 = (bf16[8,2,48,256]{3,2,1,0:T(8,128)(2,1)}, bf16[8,2,48,256]{3,2,1,0:T(8,128)(2,1)S(1)}, u32[]{:S(2)}, u32[]{:S(2)}) collective-permute-start(bf16[8,2,48,256]{3,2,1,0:T(8,128)(2,1)} %collective-permute-done.1.refs_1_), channel_id=1, source_target_pairs={{0,96},{16,48},{32,0},{48,80},{64,32},{80,112},{96,64},{112,16},{1... | collective-permute-start | bytes 1179656 | tf_op jit(solution)/shard_map/ppermute | solution.py:326
  52.0 0.3 multiply_reduce_fusion.1
  52.3 1.5 %multiply_reduce_fusion = f32[256]{0:T(256)S(1)} fusion(bf16[256,2048]{1,0:T(8,128)(2,1)} %collective-permute-done.5.refs_16_.refs_17_.refs_18_.refs_19_.refs_12_.refs_13_.refs_14_.refs_4_), kind=kLoop, calls=%fused_computation | loop fusion | flops 1572608 | bytes 1049600 | tf_op jit(solution)/shard_map/reduce_sum | solution.py:302
  53.9 3.7 %score.3 = (f32[384,512]{1,0:T(8,128)S(1)}, bf16[8,8,48,256]{3,2,1,0:T(8,128)(2,1)}, bf16[8,8,48,256]{3,2,1,0:T(8,128)(2,1)}) custom-call(s32[4]{0:T(128)S(1)} %pad_add_fusion.3.place, bf16[8,2,48,256]{3,2,1,0:T(8,128)(2,1)S(1)} %all-to-all-done.refs_0_, bf16[8,2,48,256]{3,2,1,0:T(8,128)(2,1)} %collective-permute-done.6.refs_1_, ...), custom_call_target="tpu_custom_call" | custom-call | tf_op jit(solution)/shard_map/score/pallas_call | solution.py:143
  57.7 2.9 %score.4 = (f32[384,512]{1,0:T(8,128)S(1)}, bf16[8,8,48,256]{3,2,1,0:T(8,128)(2,1)}, bf16[8,8,48,256]{3,2,1,0:T(8,128)(2,1)}) custom-call(s32[3]{0:T(128)S(1)} %pad_add_fusion.2.place, bf16[8,2,48,256]{3,2,1,0:T(8,128)(2,1)S(1)} %collective-permute-done.7.refs_0_, ...), custom_call_target="tpu_custom_call", output_to_operand_aliasing={{1}: (17, {}), {2}: (18, {})} | custom-call | tf_op jit(solution)/shard_map/score/pallas_call | solution.py:143
  60.6 2.6 %score.5 = (f32[384,512]{1,0:T(8,128)}, bf16[8,8,48,256]{3,2,1,0:T(8,128)(2,1)}, bf16[8,8,48,256]{3,2,1,0:T(8,128)(2,1)}) custom-call(s32[1]{0:T(128)} %bitcast.3.place, bf16[8,2,48,256]{3,2,1,0:T(8,128)(2,1)S(1)} %collective-permute-done.2.refs_0_, bf16[256,2048]{1,0:T(8,128)(2,1)S(1)} %copy-done, ...), custom_call_target="tpu_custom_call", output_to_operand_aliasing={{1}: (7, {}), {2}: (8, {})} | custom-call | tf_op jit(solution)/shard_map/score/pallas_call | solution.py:143
  63.2 2.0 %collective-permute-start.11 = (bf16[8,8,48,256]{3,2,1,0:T(8,128)(2,1)}, bf16[8,8,48,256]{3,2,1,0:T(8,128)(2,1)}, u32[]{:S(2)}, u32[]{:S(2)}) collective-permute-start(bf16[8,8,48,256]{3,2,1,0:T(8,128)(2,1)} %get-tuple-element.29), channel_id=1, source_target_pairs={{0,8},{1,9},{2,10},{3,11},{4,12},{5,13},{6,14},{7,15},{8,0},{9,1},... | collective-permute-start | bytes 4718600 | tf_op jit(solution)/shard_map/ppermute | solution.py:348
  65.2 8.5 %all-to-all-start.1 = ((f32[8,48,512]{2,1,0:T(8,128)}), f32[8,48,512]{2,1,0:T(8,128)S(1)}, u32[]{:S(2)}, u32[]{:S(2)}) async-start(f32[8,48,512]{2,1,0:T(8,128)} %bitcast.20), calls=%async_computation.1 | async-start | bytes 1572864 | tf_op jit(solution)/shard_map/all_to_all | solution.py:350
  73.7 20.8 %all-to-all-done.1.pieces = f32[8,48,512]{2,1,0:T(8,128)S(1)} async-done(((f32[8,48,512]{2,1,0:T(8,128)}), f32[8,48,512]{2,1,0:T(8,128)S(1)}, u32[]{:S(2)}, u32[]{:S(2)}) %all-to-all-start.1) | async-done | bytes 786464 | tf_op jit(solution)/shard_map/all_to_all | solution.py:350
  94.5 0.9 total.1
  95.4 6.3 %all-to-all-start.2 = ((f32[16,8,128]{2,1,0:T(8,128)}), f32[16,8,128]{2,1,0:T(8,128)S(1)}, u32[]{:S(2)}, u32[]{:S(2)}) async-start(f32[16,8,128]{2,1,0:T(8,128)} %get-tuple-element.30), calls=%async_computation.2 | async-start | bytes 131072 | tf_op jit(solution)/shard_map/all_to_all | solution.py:353
  101.7 0.1 collective-permute-start.12
  101.8 1.1 collective-permute-done.12.came
  102.9 3.6 %all-to-all-done.2.stats = f32[16,8,128]{2,1,0:T(8,128)S(1)} async-done(((f32[16,8,128]{2,1,0:T(8,128)}), f32[16,8,128]{2,1,0:T(8,128)S(1)}, u32[]{:S(2)}, u32[]{:S(2)}) %all-to-all-start.2) | async-done | bytes 65568 | tf_op jit(solution)/shard_map/all_to_all | solution.py:353
  106.5 0.1 collective-permute-start.22
  106.6 0.2 weigh.1
  106.9 1.2 collective-permute-start.13
  108.0 4.5 %collective-permute-done.13 = bf16[2,48,256]{2,1,0:T(8,128)(2,1)S(1)} collective-permute-done((bf16[2,48,256]{2,1,0:T(8,128)(2,1)S(1)}, bf16[2,48,256]{2,1,0:T(8,128)(2,1)S(1)}, u32[]{:S(2)}, u32[]{:S(2)}) %collective-permute-start.13) | collective-permute-done | bytes 49184 | tf_op jit(solution)/shard_map/ppermute | solution.py:357
  112.6 0.5 collective-permute-start.14
  113.1 2.8 %collective-permute-start.18 = (bf16[4,48,256]{2,1,0:T(8,128)(2,1)S(1)}, bf16[4,48,256]{2,1,0:T(8,128)(2,1)S(1)}, u32[]{:S(2)}, u32[]{:S(2)}) collective-permute-start(bf16[4,48,256]{2,1,0:T(8,128)(2,1)S(1)} %constant_dynamic-update-slice_fusion.refs_0_), channel_id=1, source_target_pairs={{0,7},{1,0},{2,1},{3,2},{4,3},{5,4},{6,5},{7,6},{8,15},{9,8},{10,9... | collective-permute-start | bytes 294920 | tf_op jit(solution)/shard_map/ppermute | solution.py:359
  115.9 2.9 %collective-permute-start.20 = (bf16[4,48,256]{2,1,0:T(8,128)(2,1)S(1)}, bf16[4,48,256]{2,1,0:T(8,128)(2,1)S(1)}, u32[]{:S(2)}, u32[]{:S(2)}) collective-permute-start(bf16[4,48,256]{2,1,0:T(8,128)(2,1)S(1)} %constant_dynamic-update-slice_fusion.refs_0_), channel_id=1, source_target_pairs={{0,6},{1,7},{2,0},{3,1},{4,2},{5,3},{6,4},{7,5},{8,14},{9,15},{10,... | collective-permute-start | bytes 294920 | tf_op jit(solution)/shard_map/ppermute | solution.py:359
  118.7 1.4 %collective-permute-done.14.refs_1_ = bf16[4,48,256]{2,1,0:T(8,128)(2,1)S(1)} collective-permute-done((bf16[4,48,256]{2,1,0:T(8,128)(2,1)S(1)}, bf16[4,48,256]{2,1,0:T(8,128)(2,1)S(1)}, u32[]{:S(2)}, u32[]{:S(2)}) %collective-permute-start.14) | collective-permute-done | bytes 98336 | tf_op jit(solution)/shard_map/ppermute | solution.py:359
  120.2 1.2 collective-permute-done.15.refs_2_
  121.4 4.1 %collective-permute-start.19 = (bf16[4,48,256]{2,1,0:T(8,128)(2,1)S(1)}, bf16[4,48,256]{2,1,0:T(8,128)(2,1)S(1)}, u32[]{:S(2)}, u32[]{:S(2)}) collective-permute-start(bf16[4,48,256]{2,1,0:T(8,128)(2,1)S(1)} %collective-permute-done.18.refs_7_), channel_id=1, source_target_pairs={{0,6},{1,7},{2,0},{3,1},{4,2},{5,3},{6,4},{7,5},{8,14},{9,15},{10,... | collective-permute-start | bytes 294920 | tf_op jit(solution)/shard_map/ppermute | solution.py:359
  125.6 0.6 reshape.74
  126.2 2.5 %stage.1.refs_8_ = bf16[4,8,8,48,256]{4,3,2,1,0:T(8,128)(2,1)S(1)} custom-call(bf16[8,8,48,256]{3,2,1,0:T(8,128)(2,1)S(1)} %copy-done.1, bf16[8,8,48,256]{3,2,1,0:T(8,128)(2,1)} %collective-permute-done.21.refs_1_, bf16[8,8,48,256]{3,2,1,0:T(8,128)(2,1)} %collective-permute-done.11.refs_2_, bf16[8,8,48,256]{3,2,1,0:T(8,128)(2,1)} %collective-permute-done.22.refs_3_), custom_call_target="tpu_custom_call" | custom-call | bytes 12582912 | tf_op jit(solution)/shard_map/stage/pallas_call | solution.py:246
  128.7 0.7 collective-permute-done.17.refs_4_
  129.4 3.3 %project.1 = f32[256,2048]{1,0:T(8,128)} custom-call(s32[2]{0:T(128)S(1)} %pad_add_fusion.place, bf16[4,48,256]{2,1,0:T(8,128)(2,1)S(1)} %constant_dynamic-update-slice_fusion.refs_0_, bf16[4,48,256]{2,1,0:T(8,128)(2,1)S(1)} %collective-permute-done.14.refs_1_, bf16[4,48,256]{2,1,0:T(8,128)(2,1)S(1)} %collective-permute-done.15.refs_2_, ...), custom_call_target="tpu_custom_call" | custom-call | tf_op jit(solution)/shard_map/project/pallas_call | solution.py:285
  (35 shorter events, 0.3 us)
Async XLA Ops:
  0.6 26.7 %collective-permute-start.3 = (bf16[256,2048]{1,0:T(8,128)(2,1)}, bf16[256,2048]{1,0:T(8,128)(2,1)S(1)}, u32[]{:S(2)}, u32[]{:S(2)}) collective-permute-start(bf16[256,2048]{1,0:T(8,128)(2,1)} %refs_1_.1), channel_id=1, source_target_pairs={{0,8},{1,9},{2,10},{3,11},{4,12},{5,13},{6,14},{7,15},{8,0},{9,1},... | collective-permute-start | bytes 3145736 | tf_op jit(solution)/shard_map/ppermute | solution.py:313
  4.6 11.9 %copy-start = (bf16[256,2048]{1,0:T(8,128)(2,1)S(1)}, bf16[256,2048]{1,0:T(8,128)(2,1)}, u32[]{:S(2)}) copy-start(bf16[256,2048]{1,0:T(8,128)(2,1)} %refs_1_.1) | copy-start | bytes 3145732
  4.6 26.9 %copy-start.2 = (s32[256]{0:T(256)S(1)}, s32[256]{0:T(256)}, u32[]{:S(2)}) copy-start(s32[256]{0:T(256)} %param.8) | copy-start | bytes 3076
  4.6 26.9 %copy-start.3 = (f32[8]{0:T(128)S(1)}, f32[8]{0:T(128)}, u32[]{:S(2)}) copy-start(f32[8]{0:T(128)} %param.9) | copy-start | bytes 100
  8.0 22.9 %all-to-all-start = ((bf16[8,2,48,256]{3,2,1,0:T(8,128)(2,1)}), bf16[8,2,48,256]{3,2,1,0:T(8,128)(2,1)S(1)}, u32[]{:S(2)}, u32[]{:S(2)}) async-start(bf16[8,2,48,256]{3,2,1,0:T(8,128)(2,1)} %shift.1), calls=%async_computation | async-start | bytes 786432 | tf_op jit(solution)/shard_map/all_to_all | solution.py:324
  16.5 26.6 %collective-permute-start.4 = (bf16[256,2048]{1,0:T(8,128)(2,1)S(1)}, bf16[256,2048]{1,0:T(8,128)(2,1)S(1)}, u32[]{:S(2)}, u32[]{:S(2)}) collective-permute-start(bf16[256,2048]{1,0:T(8,128)(2,1)S(1)} %copy-done), channel_id=1, source_target_pairs={{0,16},{16,0},{32,48},{48,32},{64,80},{80,64},{96,112},{112,96},{1... | collective-permute-start | bytes 3145736 | tf_op jit(solution)/shard_map/ppermute | solution.py:314
  27.3 25.0 %collective-permute-start.5 = (bf16[256,2048]{1,0:T(8,128)(2,1)S(1)}, bf16[256,2048]{1,0:T(8,128)(2,1)}, u32[]{:S(2)}, u32[]{:S(2)}) collective-permute-start(bf16[256,2048]{1,0:T(8,128)(2,1)S(1)} %collective-permute-done.3.refs_8_.refs_9_.refs_10_.refs_11_.refs_6_.refs_7_.refs_2_), channel_id=1, source_target_pairs={{0,16},{16,0},{32,48},{48,32},{64,80},{80,64},{96,112},{112,96},{1... | collective-permute-start | bytes 3145736 | tf_op jit(solution)/shard_map/ppermute | solution.py:315
  30.9 10.8 %collective-permute-start = (bf16[8,2,48,256]{3,2,1,0:T(8,128)(2,1)S(1)}, bf16[8,2,48,256]{3,2,1,0:T(8,128)(2,1)}, u32[]{:S(2)}, u32[]{:S(2)}) collective-permute-start(bf16[8,2,48,256]{3,2,1,0:T(8,128)(2,1)S(1)} %all-to-all-done.refs_0_), channel_id=1, source_target_pairs={{0,96},{16,48},{32,0},{48,80},{64,32},{80,112},{96,64},{112,16},{1... | collective-permute-start | bytes 1179656 | tf_op jit(solution)/shard_map/ppermute | solution.py:326
  31.6 11.4 %collective-permute-start.6 = (bf16[8,2,48,256]{3,2,1,0:T(8,128)(2,1)S(1)}, bf16[8,2,48,256]{3,2,1,0:T(8,128)(2,1)}, u32[]{:S(2)}, u32[]{:S(2)}) collective-permute-start(bf16[8,2,48,256]{3,2,1,0:T(8,128)(2,1)S(1)} %all-to-all-done.refs_0_), channel_id=1, source_target_pairs={{0,32},{16,112},{32,64},{48,16},{64,96},{80,48},{96,0},{112,80},{1... | collective-permute-start | bytes 1179656 | tf_op jit(solution)/shard_map/ppermute | solution.py:326
  33.1 11.6 %collective-permute-start.8 = (bf16[8,2,48,256]{3,2,1,0:T(8,128)(2,1)S(1)}, bf16[8,2,48,256]{3,2,1,0:T(8,128)(2,1)}, u32[]{:S(2)}, u32[]{:S(2)}) collective-permute-start(bf16[8,2,48,256]{3,2,1,0:T(8,128)(2,1)S(1)} %all-to-all-done.refs_0_), channel_id=1, source_target_pairs={{0,128},{16,144},{32,160},{48,176},{64,192},{80,208},{96,224},{112... | collective-permute-start | bytes 1179656 | tf_op jit(solution)/shard_map/ppermute | solution.py:326
  41.6 8.7 %collective-permute-start.1 = (bf16[8,2,48,256]{3,2,1,0:T(8,128)(2,1)}, bf16[8,2,48,256]{3,2,1,0:T(8,128)(2,1)}, u32[]{:S(2)}, u32[]{:S(2)}) collective-permute-start(bf16[8,2,48,256]{3,2,1,0:T(8,128)(2,1)} %collective-permute-done.refs_2_), channel_id=1, source_target_pairs={{0,128},{16,144},{32,160},{48,176},{64,192},{80,208},{96,224},{112... | collective-permute-start | bytes 1179656 | tf_op jit(solution)/shard_map/ppermute | solution.py:326
  43.0 10.9 %collective-permute-start.10 = (f32[256]{0:T(256)S(1)}, f32[256]{0:T(256)S(1)}, u32[]{:S(2)}, u32[]{:S(2)}) collective-permute-start(f32[256]{0:T(256)S(1)} %select_reduce_fusion), channel_id=1, source_target_pairs={{0,16},{16,0},{32,48},{48,32},{64,80},{80,64},{96,112},{112,96},{1... | collective-permute-start | bytes 3080 | tf_op jit(solution)/shard_map/ppermute | solution.py:318
  43.1 14.6 %collective-permute-start.7 = (bf16[8,2,48,256]{3,2,1,0:T(8,128)(2,1)}, bf16[8,2,48,256]{3,2,1,0:T(8,128)(2,1)S(1)}, u32[]{:S(2)}, u32[]{:S(2)}) collective-permute-start(bf16[8,2,48,256]{3,2,1,0:T(8,128)(2,1)} %collective-permute-done.refs_2_), channel_id=1, source_target_pairs={{0,96},{16,48},{32,0},{48,80},{64,32},{80,112},{96,64},{112,16},{1... | collective-permute-start | bytes 1179656 | tf_op jit(solution)/shard_map/ppermute | solution.py:326
  44.6 13.0 %collective-permute-start.9 = (bf16[8,2,48,256]{3,2,1,0:T(8,128)(2,1)}, bf16[8,2,48,256]{3,2,1,0:T(8,128)(2,1)S(1)}, u32[]{:S(2)}, u32[]{:S(2)}) collective-permute-start(bf16[8,2,48,256]{3,2,1,0:T(8,128)(2,1)} %collective-permute-done.8.refs_3_), channel_id=1, source_target_pairs={{0,32},{16,112},{32,64},{48,16},{64,96},{80,48},{96,0},{112,80},{1... | collective-permute-start | bytes 1179656 | tf_op jit(solution)/shard_map/ppermute | solution.py:326
  50.3 10.3 %collective-permute-start.2 = (bf16[8,2,48,256]{3,2,1,0:T(8,128)(2,1)}, bf16[8,2,48,256]{3,2,1,0:T(8,128)(2,1)S(1)}, u32[]{:S(2)}, u32[]{:S(2)}) collective-permute-start(bf16[8,2,48,256]{3,2,1,0:T(8,128)(2,1)} %collective-permute-done.1.refs_1_), channel_id=1, source_target_pairs={{0,96},{16,48},{32,0},{48,80},{64,32},{80,112},{96,64},{112,16},{1... | collective-permute-start | bytes 1179656 | tf_op jit(solution)/shard_map/ppermute | solution.py:326
  63.2 63.0 %copy-start.1 = (bf16[8,8,48,256]{3,2,1,0:T(8,128)(2,1)S(1)}, bf16[8,8,48,256]{3,2,1,0:T(8,128)(2,1)}, u32[]{:S(2)}) copy-start(bf16[8,8,48,256]{3,2,1,0:T(8,128)(2,1)} %get-tuple-element.35.refs_0_) | copy-start | bytes 4718596
  63.2 43.3 %collective-permute-start.11 = (bf16[8,8,48,256]{3,2,1,0:T(8,128)(2,1)}, bf16[8,8,48,256]{3,2,1,0:T(8,128)(2,1)}, u32[]{:S(2)}, u32[]{:S(2)}) collective-permute-start(bf16[8,8,48,256]{3,2,1,0:T(8,128)(2,1)} %get-tuple-element.29), channel_id=1, source_target_pairs={{0,8},{1,9},{2,10},{3,11},{4,12},{5,13},{6,14},{7,15},{8,0},{9,1},... | collective-permute-start | bytes 4718600 | tf_op jit(solution)/shard_map/ppermute | solution.py:348
  65.2 29.3 %all-to-all-start.1 = ((f32[8,48,512]{2,1,0:T(8,128)}), f32[8,48,512]{2,1,0:T(8,128)S(1)}, u32[]{:S(2)}, u32[]{:S(2)}) async-start(f32[8,48,512]{2,1,0:T(8,128)} %bitcast.20), calls=%async_computation.1 | async-start | bytes 1572864 | tf_op jit(solution)/shard_map/all_to_all | solution.py:350
  73.7 42.2 %collective-permute-start.21 = (bf16[8,8,48,256]{3,2,1,0:T(8,128)(2,1)}, bf16[8,8,48,256]{3,2,1,0:T(8,128)(2,1)}, u32[]{:S(2)}, u32[]{:S(2)}) collective-permute-start(bf16[8,8,48,256]{3,2,1,0:T(8,128)(2,1)} %get-tuple-element.35.refs_0_), channel_id=1, source_target_pairs={{0,16},{16,0},{32,48},{48,32},{64,80},{80,64},{96,112},{112,96},{1... | collective-permute-start | bytes 4718600 | tf_op jit(solution)/shard_map/ppermute | solution.py:349
  95.4 11.1 %all-to-all-start.2 = ((f32[16,8,128]{2,1,0:T(8,128)}), f32[16,8,128]{2,1,0:T(8,128)S(1)}, u32[]{:S(2)}, u32[]{:S(2)}) async-start(f32[16,8,128]{2,1,0:T(8,128)} %get-tuple-element.30), calls=%async_computation.2 | async-start | bytes 131072 | tf_op jit(solution)/shard_map/all_to_all | solution.py:353
  101.7 1.2 collective-permute-start.12
  106.5 19.7 %collective-permute-start.22 = (bf16[8,8,48,256]{3,2,1,0:T(8,128)(2,1)}, bf16[8,8,48,256]{3,2,1,0:T(8,128)(2,1)}, u32[]{:S(2)}, u32[]{:S(2)}) collective-permute-start(bf16[8,8,48,256]{3,2,1,0:T(8,128)(2,1)} %collective-permute-done.11.refs_2_), channel_id=1, source_target_pairs={{0,16},{16,0},{32,48},{48,32},{64,80},{80,64},{96,112},{112,96},{1... | collective-permute-start | bytes 4718600 | tf_op jit(solution)/shard_map/ppermute | solution.py:355
  106.9 5.7 %collective-permute-start.13 = (bf16[2,48,256]{2,1,0:T(8,128)(2,1)S(1)}, bf16[2,48,256]{2,1,0:T(8,128)(2,1)S(1)}, u32[]{:S(2)}, u32[]{:S(2)}) collective-permute-start(bf16[2,48,256]{2,1,0:T(8,128)(2,1)S(1)} %get-tuple-element.34), channel_id=1, source_target_pairs={{0,8},{1,9},{2,10},{3,11},{4,12},{5,13},{6,14},{7,15},{8,0},{9,1},... | collective-permute-start | bytes 147464 | tf_op jit(solution)/shard_map/ppermute | solution.py:357
  112.6 7.6 %collective-permute-start.14 = (bf16[4,48,256]{2,1,0:T(8,128)(2,1)S(1)}, bf16[4,48,256]{2,1,0:T(8,128)(2,1)S(1)}, u32[]{:S(2)}, u32[]{:S(2)}) collective-permute-start(bf16[4,48,256]{2,1,0:T(8,128)(2,1)S(1)} %constant_dynamic-update-slice_fusion.refs_0_), channel_id=1, source_target_pairs={{0,1},{1,2},{2,3},{3,4},{4,5},{5,6},{6,7},{7,0},{8,9},{9,10},{10,1... | collective-permute-start | bytes 294920 | tf_op jit(solution)/shard_map/ppermute | solution.py:359
  113.1 8.3 %collective-permute-start.15 = (bf16[4,48,256]{2,1,0:T(8,128)(2,1)S(1)}, bf16[4,48,256]{2,1,0:T(8,128)(2,1)S(1)}, u32[]{:S(2)}, u32[]{:S(2)}) collective-permute-start(bf16[4,48,256]{2,1,0:T(8,128)(2,1)S(1)} %constant_dynamic-update-slice_fusion.refs_0_), channel_id=1, source_target_pairs={{0,2},{1,3},{2,4},{3,5},{4,6},{5,7},{6,0},{7,1},{8,10},{9,11},{10,... | collective-permute-start | bytes 294920 | tf_op jit(solution)/shard_map/ppermute | solution.py:359
  113.1 8.3 %collective-permute-start.18 = (bf16[4,48,256]{2,1,0:T(8,128)(2,1)S(1)}, bf16[4,48,256]{2,1,0:T(8,128)(2,1)S(1)}, u32[]{:S(2)}, u32[]{:S(2)}) collective-permute-start(bf16[4,48,256]{2,1,0:T(8,128)(2,1)S(1)} %constant_dynamic-update-slice_fusion.refs_0_), channel_id=1, source_target_pairs={{0,7},{1,0},{2,1},{3,2},{4,3},{5,4},{6,5},{7,6},{8,15},{9,8},{10,9... | collective-permute-start | bytes 294920 | tf_op jit(solution)/shard_map/ppermute | solution.py:359
  115.9 12.8 %collective-permute-start.20 = (bf16[4,48,256]{2,1,0:T(8,128)(2,1)S(1)}, bf16[4,48,256]{2,1,0:T(8,128)(2,1)S(1)}, u32[]{:S(2)}, u32[]{:S(2)}) collective-permute-start(bf16[4,48,256]{2,1,0:T(8,128)(2,1)S(1)} %constant_dynamic-update-slice_fusion.refs_0_), channel_id=1, source_target_pairs={{0,6},{1,7},{2,0},{3,1},{4,2},{5,3},{6,4},{7,5},{8,14},{9,15},{10,... | collective-permute-start | bytes 294920 | tf_op jit(solution)/shard_map/ppermute | solution.py:359
  120.2 8.5 %collective-permute-start.16 = (bf16[4,48,256]{2,1,0:T(8,128)(2,1)S(1)}, bf16[4,48,256]{2,1,0:T(8,128)(2,1)S(1)}, u32[]{:S(2)}, u32[]{:S(2)}) collective-permute-start(bf16[4,48,256]{2,1,0:T(8,128)(2,1)S(1)} %collective-permute-done.14.refs_1_), channel_id=1, source_target_pairs={{0,2},{1,3},{2,4},{3,5},{4,6},{5,7},{6,0},{7,1},{8,10},{9,11},{10,... | collective-permute-start | bytes 294920 | tf_op jit(solution)/shard_map/ppermute | solution.py:359
  121.4 8.1 %collective-permute-start.17 = (bf16[4,48,256]{2,1,0:T(8,128)(2,1)S(1)}, bf16[4,48,256]{2,1,0:T(8,128)(2,1)S(1)}, u32[]{:S(2)}, u32[]{:S(2)}) collective-permute-start(bf16[4,48,256]{2,1,0:T(8,128)(2,1)S(1)} %collective-permute-done.15.refs_2_), channel_id=1, source_target_pairs={{0,2},{1,3},{2,4},{3,5},{4,6},{5,7},{6,0},{7,1},{8,10},{9,11},{10,... | collective-permute-start | bytes 294920 | tf_op jit(solution)/shard_map/ppermute | solution.py:359
  121.4 8.1 %collective-permute-start.19 = (bf16[4,48,256]{2,1,0:T(8,128)(2,1)S(1)}, bf16[4,48,256]{2,1,0:T(8,128)(2,1)S(1)}, u32[]{:S(2)}, u32[]{:S(2)}) collective-permute-start(bf16[4,48,256]{2,1,0:T(8,128)(2,1)S(1)} %collective-permute-done.18.refs_7_), channel_id=1, source_target_pairs={{0,6},{1,7},{2,0},{3,1},{4,2},{5,3},{6,4},{7,5},{8,14},{9,15},{10,... | collective-permute-start | bytes 294920 | tf_op jit(solution)/shard_map/ppermute | solution.py:359

commit v7 on v6

--- a/solution.py
+++ b/solution.py
@@ -327,8 +327,7 @@
     behind = send(own, AHEAD)
     front = send(own, BACK)
     across = send(own, Y_LOW)
-    after, _ = lax.optimization_barrier((front, behind))
-    far = send(after, BACK)
+    far = send(front, BACK)
     across_front = send(front, Y_LOW)
     across_behind = send(across, AHEAD)
     across_far = send(across_front, BACK)

time: 135 us -> 135 us (level)
  waiting for transfers between devices: 61.4 us -> 64 us
  starting transfers between devices: 47 us -> 45.1 us
    all_to_all x1, waiting for transfers between devices: 20.8 us -> 23.1 us  [on_device(): lax.all_to_all(partial.reshape(HALF, rows, 2 * oris), 'dom', 0, 0, axis_i...]
where the time goes in v7:
time: 135 us; the launch traced here: 133 us
  waiting for transfers between devices  64 us (47%)
  starting transfers between devices  45.1 us (33%)
  Pallas kernels  19.3 us (14%)
  other arithmetic  3.35 us (2%)
    all_to_all x1, waiting for transfers between devices, on_device(): lax.all_to_all(partial.reshape(HALF, rows, 2 * oris), 'dom', 0, 0, axis_i...  23.1 us
    ppermute x7, waiting for transfers between devices, on_device(): send = lambda block, perm: lax.ppermute(block, 'orient', perm)  14 us
    ppermute x1, waiting for transfers between devices, on_device(): s_hi = lax.ppermute(slices, 'dom', Y_HIGH)  10.8 us
    ppermute x7, starting transfers between devices, on_device(): lax.ppermute(block, ('orient', 'dom'), along_z(by))  10.3 us
    pallas_call x3, Pallas kernels, add_score(): pl.pallas_call(functools.partial(score_kernel, count), out_shape=(total,...  9.05 us
    all_to_all x1, starting transfers between devices, on_device(): own = lax.all_to_all(own, 'dom', 0, 0, axis_index_groups=Z_GROUPS)  8.48 us
    all_to_all x1, starting transfers between devices, on_device(): lax.all_to_all(partial.reshape(HALF, rows, 2 * oris), 'dom', 0, 0, axis_i...  8.15 us
    ppermute x7, starting transfers between devices, on_device(): send = lambda block, perm: lax.ppermute(block, 'orient', perm)  5.99 us
  transfers between devices with their start and end apart: 26, of which 12 were waited for; matrix products, arithmetic and copies ran while one was open for 3% of the time, Pallas kernels for 10%

profile of v7, /device:TPU:2, one launch (start us, length us, event | category | flops | bytes accessed | tf_op | source)
XLA Modules:
  0.0 133.3 jit_solution(5955192515686637354)
XLA Ops:
  0.6 3.3 %collective-permute-start.3 = (bf16[256,2048]{1,0:T(8,128)(2,1)}, bf16[256,2048]{1,0:T(8,128)(2,1)S(1)}, u32[]{:S(2)}, u32[]{:S(2)}) collective-permute-start(bf16[256,2048]{1,0:T(8,128)(2,1)} %refs_1_.1), channel_id=1, source_target_pairs={{0,8},{1,9},{2,10},{3,11},{4,12},{5,13},{6,14},{7,15},{8,0},{9,1},... | collective-permute-start | bytes 3145736 | tf_op jit(solution)/shard_map/ppermute | solution.py:313
  3.9 0.7 pad_add_fusion.1.place
  4.6 3.4 %shift.1 = bf16[8,2,48,256]{3,2,1,0:T(8,128)(2,1)} custom-call(s32[4]{0:T(128)} %pad_add_fusion.1.place, s32[2,96]{1,0:T(2,128)} %bitcast.24, bf16[96,32768]{1,0:T(8,128)(2,1)} %images.1), custom_call_target="tpu_custom_call" | custom-call | tf_op jit(solution)/shard_map/shift/pallas_call | solution.py:98
  8.0 8.5 %all-to-all-start = ((bf16[8,2,48,256]{3,2,1,0:T(8,128)(2,1)}), bf16[8,2,48,256]{3,2,1,0:T(8,128)(2,1)S(1)}, u32[]{:S(2)}, u32[]{:S(2)}) async-start(bf16[8,2,48,256]{3,2,1,0:T(8,128)(2,1)} %shift.1), calls=%async_computation | async-start | bytes 786432 | tf_op jit(solution)/shard_map/all_to_all | solution.py:324
  16.5 0.1 collective-permute-start.4
  16.6 10.8 %collective-permute-done.3.refs_8_.refs_9_.refs_10_.refs_11_.refs_6_.refs_7_.refs_2_ = bf16[256,2048]{1,0:T(8,128)(2,1)S(1)} collective-permute-done((bf16[256,2048]{1,0:T(8,128)(2,1)}, bf16[256,2048]{1,0:T(8,128)(2,1)S(1)}, u32[]{:S(2)}, u32[]{:S(2)}) %collective-permute-start.3) | collective-permute-done | bytes 1048608 | tf_op jit(solution)/shard_map/ppermute | solution.py:313
  27.3 3.5 %all-to-all-done.refs_0_ = bf16[8,2,48,256]{3,2,1,0:T(8,128)(2,1)S(1)} async-done(((bf16[8,2,48,256]{3,2,1,0:T(8,128)(2,1)}), bf16[8,2,48,256]{3,2,1,0:T(8,128)(2,1)S(1)}, u32[]{:S(2)}, u32[]{:S(2)}) %all-to-all-start) | async-done | bytes 393248 | tf_op jit(solution)/shard_map/all_to_all | solution.py:324
  30.9 0.5 collective-permute-start
  31.5 0.1 select_reduce_fusion
  31.6 0.7 collective-permute-start.7
  32.3 6.5 %collective-permute-done.refs_2_ = bf16[8,2,48,256]{3,2,1,0:T(8,128)(2,1)} collective-permute-done((bf16[8,2,48,256]{3,2,1,0:T(8,128)(2,1)S(1)}, bf16[8,2,48,256]{3,2,1,0:T(8,128)(2,1)}, u32[]{:S(2)}, u32[]{:S(2)}) %collective-permute-start) | collective-permute-done | bytes 393248 | tf_op jit(solution)/shard_map/ppermute | solution.py:326
  38.7 0.7 collective-permute-start.1
  39.5 0.3 multiply_reduce_fusion.3
  39.8 1.6 %collective-permute-start.9 = (bf16[8,2,48,256]{3,2,1,0:T(8,128)(2,1)S(1)}, bf16[8,2,48,256]{3,2,1,0:T(8,128)(2,1)S(1)}, u32[]{:S(2)}, u32[]{:S(2)}) collective-permute-start(bf16[8,2,48,256]{3,2,1,0:T(8,128)(2,1)S(1)} %all-to-all-done.refs_0_), channel_id=1, source_target_pairs={{0,32},{16,112},{32,64},{48,16},{64,96},{80,48},{96,0},{112,80},{1... | collective-permute-start | bytes 1179656 | tf_op jit(solution)/shard_map/ppermute | solution.py:326
  41.3 0.3 multiply_reduce_fusion.2
  41.6 0.6 collective-permute-start.6
  42.3 1.5 %collective-permute-done.7.refs_3_ = bf16[8,2,48,256]{3,2,1,0:T(8,128)(2,1)} collective-permute-done((bf16[8,2,48,256]{3,2,1,0:T(8,128)(2,1)S(1)}, bf16[8,2,48,256]{3,2,1,0:T(8,128)(2,1)}, u32[]{:S(2)}, u32[]{:S(2)}) %collective-permute-start.7) | collective-permute-done | bytes 393248 | tf_op jit(solution)/shard_map/ppermute | solution.py:326
  43.7 1.3 collective-permute-start.8
  45.0 5.0 %collective-permute-done.1.refs_1_ = bf16[8,2,48,256]{3,2,1,0:T(8,128)(2,1)} collective-permute-done((bf16[8,2,48,256]{3,2,1,0:T(8,128)(2,1)}, bf16[8,2,48,256]{3,2,1,0:T(8,128)(2,1)}, u32[]{:S(2)}, u32[]{:S(2)}) %collective-permute-start.1) | collective-permute-done | bytes 393248 | tf_op jit(solution)/shard_map/ppermute | solution.py:326
  50.0 0.6 collective-permute-start.2
  50.6 0.3 multiply_reduce_fusion.1
  50.9 0.1 collective-permute-start.10
  51.0 1.5 %multiply_reduce_fusion = f32[256]{0:T(256)S(1)} fusion(bf16[256,2048]{1,0:T(8,128)(2,1)} %collective-permute-done.5.refs_16_.refs_17_.refs_18_.refs_19_.refs_12_.refs_13_.refs_14_.refs_4_), kind=kLoop, calls=%fused_computation | loop fusion | flops 1572608 | bytes 1049600 | tf_op jit(solution)/shard_map/reduce_sum | solution.py:302
  52.6 3.5 %score.3 = (f32[384,512]{1,0:T(8,128)S(1)}, bf16[8,8,48,256]{3,2,1,0:T(8,128)(2,1)}, bf16[8,8,48,256]{3,2,1,0:T(8,128)(2,1)}) custom-call(s32[4]{0:T(128)S(1)} %pad_add_fusion.3.place, bf16[8,2,48,256]{3,2,1,0:T(8,128)(2,1)S(1)} %all-to-all-done.refs_0_, bf16[8,2,48,256]{3,2,1,0:T(8,128)(2,1)S(1)} %collective-permute-done.9.refs_1_, ...), custom_call_target="tpu_custom_call" | custom-call | tf_op jit(solution)/shard_map/score/pallas_call | solution.py:143
  56.2 1.0 collective-permute-done.8.refs_2_
  57.2 2.9 %score.4 = (f32[384,512]{1,0:T(8,128)S(1)}, bf16[8,8,48,256]{3,2,1,0:T(8,128)(2,1)}, bf16[8,8,48,256]{3,2,1,0:T(8,128)(2,1)}) custom-call(s32[3]{0:T(128)S(1)} %pad_add_fusion.2.place, bf16[8,2,48,256]{3,2,1,0:T(8,128)(2,1)S(1)} %collective-permute-done.6.refs_0_, ...), custom_call_target="tpu_custom_call", output_to_operand_aliasing={{1}: (17, {}), {2}: (18, {})} | custom-call | tf_op jit(solution)/shard_map/score/pallas_call | solution.py:143
  60.1 2.6 %score.5 = (f32[384,512]{1,0:T(8,128)}, bf16[8,8,48,256]{3,2,1,0:T(8,128)(2,1)}, bf16[8,8,48,256]{3,2,1,0:T(8,128)(2,1)}) custom-call(s32[1]{0:T(128)} %bitcast.3.place, bf16[8,2,48,256]{3,2,1,0:T(8,128)(2,1)S(1)} %collective-permute-done.2.refs_0_, bf16[256,2048]{1,0:T(8,128)(2,1)S(1)} %copy-done, ...), custom_call_target="tpu_custom_call", output_to_operand_aliasing={{1}: (7, {}), {2}: (8, {})} | custom-call | tf_op jit(solution)/shard_map/score/pallas_call | solution.py:143
  62.7 1.7 %collective-permute-start.11 = (bf16[8,8,48,256]{3,2,1,0:T(8,128)(2,1)}, bf16[8,8,48,256]{3,2,1,0:T(8,128)(2,1)}, u32[]{:S(2)}, u32[]{:S(2)}) collective-permute-start(bf16[8,8,48,256]{3,2,1,0:T(8,128)(2,1)} %get-tuple-element.27), channel_id=1, source_target_pairs={{0,8},{1,9},{2,10},{3,11},{4,12},{5,13},{6,14},{7,15},{8,0},{9,1},... | collective-permute-start | bytes 4718600 | tf_op jit(solution)/shard_map/ppermute | solution.py:347
  64.4 8.2 %all-to-all-start.1 = ((f32[8,48,512]{2,1,0:T(8,128)}), f32[8,48,512]{2,1,0:T(8,128)S(1)}, u32[]{:S(2)}, u32[]{:S(2)}) async-start(f32[8,48,512]{2,1,0:T(8,128)} %bitcast.20), calls=%async_computation.1 | async-start | bytes 1572864 | tf_op jit(solution)/shard_map/all_to_all | solution.py:349
  72.6 23.1 %all-to-all-done.1.pieces = f32[8,48,512]{2,1,0:T(8,128)S(1)} async-done(((f32[8,48,512]{2,1,0:T(8,128)}), f32[8,48,512]{2,1,0:T(8,128)S(1)}, u32[]{:S(2)}, u32[]{:S(2)}) %all-to-all-start.1) | async-done | bytes 786464 | tf_op jit(solution)/shard_map/all_to_all | solution.py:349
  95.7 0.9 total.1
  96.5 5.2 %all-to-all-start.2 = ((f32[16,8,128]{2,1,0:T(8,128)}), f32[16,8,128]{2,1,0:T(8,128)S(1)}, u32[]{:S(2)}, u32[]{:S(2)}) async-start(f32[16,8,128]{2,1,0:T(8,128)} %get-tuple-element.28), calls=%async_computation.2 | async-start | bytes 131072 | tf_op jit(solution)/shard_map/all_to_all | solution.py:352
  101.8 0.1 collective-permute-start.12
  101.9 1.1 collective-permute-done.12.came
  103.0 3.6 %all-to-all-done.2.stats = f32[16,8,128]{2,1,0:T(8,128)S(1)} async-done(((f32[16,8,128]{2,1,0:T(8,128)}), f32[16,8,128]{2,1,0:T(8,128)S(1)}, u32[]{:S(2)}, u32[]{:S(2)}) %all-to-all-start.2) | async-done | bytes 65568 | tf_op jit(solution)/shard_map/all_to_all | solution.py:352
  106.6 0.1 collective-permute-start.22
  106.7 0.2 weigh.1
  107.0 1.5 %collective-permute-start.13 = (bf16[2,48,256]{2,1,0:T(8,128)(2,1)S(1)}, bf16[2,48,256]{2,1,0:T(8,128)(2,1)S(1)}, u32[]{:S(2)}, u32[]{:S(2)}) collective-permute-start(bf16[2,48,256]{2,1,0:T(8,128)(2,1)S(1)} %get-tuple-element.32), channel_id=1, source_target_pairs={{0,8},{1,9},{2,10},{3,11},{4,12},{5,13},{6,14},{7,15},{8,0},{9,1},... | collective-permute-start | bytes 147464 | tf_op jit(solution)/shard_map/ppermute | solution.py:356
  108.5 4.2 %collective-permute-done.13 = bf16[2,48,256]{2,1,0:T(8,128)(2,1)S(1)} collective-permute-done((bf16[2,48,256]{2,1,0:T(8,128)(2,1)S(1)}, bf16[2,48,256]{2,1,0:T(8,128)(2,1)S(1)}, u32[]{:S(2)}, u32[]{:S(2)}) %collective-permute-start.13) | collective-permute-done | bytes 49184 | tf_op jit(solution)/shard_map/ppermute | solution.py:356
  112.7 0.5 collective-permute-start.14
  113.2 2.8 %collective-permute-start.18 = (bf16[4,48,256]{2,1,0:T(8,128)(2,1)S(1)}, bf16[4,48,256]{2,1,0:T(8,128)(2,1)S(1)}, u32[]{:S(2)}, u32[]{:S(2)}) collective-permute-start(bf16[4,48,256]{2,1,0:T(8,128)(2,1)S(1)} %constant_dynamic-update-slice_fusion.refs_0_), channel_id=1, source_target_pairs={{0,7},{1,0},{2,1},{3,2},{4,3},{5,4},{6,5},{7,6},{8,15},{9,8},{10,9... | collective-permute-start | bytes 294920 | tf_op jit(solution)/shard_map/ppermute | solution.py:358
  116.0 2.9 %collective-permute-start.20 = (bf16[4,48,256]{2,1,0:T(8,128)(2,1)S(1)}, bf16[4,48,256]{2,1,0:T(8,128)(2,1)S(1)}, u32[]{:S(2)}, u32[]{:S(2)}) collective-permute-start(bf16[4,48,256]{2,1,0:T(8,128)(2,1)S(1)} %constant_dynamic-update-slice_fusion.refs_0_), channel_id=1, source_target_pairs={{0,6},{1,7},{2,0},{3,1},{4,2},{5,3},{6,4},{7,5},{8,14},{9,15},{10,... | collective-permute-start | bytes 294920 | tf_op jit(solution)/shard_map/ppermute | solution.py:358
  118.8 1.8 %collective-permute-done.14.refs_1_ = bf16[4,48,256]{2,1,0:T(8,128)(2,1)S(1)} collective-permute-done((bf16[4,48,256]{2,1,0:T(8,128)(2,1)S(1)}, bf16[4,48,256]{2,1,0:T(8,128)(2,1)S(1)}, u32[]{:S(2)}, u32[]{:S(2)}) %collective-permute-start.14) | collective-permute-done | bytes 98336 | tf_op jit(solution)/shard_map/ppermute | solution.py:358
  120.7 1.8 %collective-permute-done.15.refs_2_ = bf16[4,48,256]{2,1,0:T(8,128)(2,1)S(1)} collective-permute-done((bf16[4,48,256]{2,1,0:T(8,128)(2,1)S(1)}, bf16[4,48,256]{2,1,0:T(8,128)(2,1)S(1)}, u32[]{:S(2)}, u32[]{:S(2)}) %collective-permute-start.15) | collective-permute-done | bytes 98336 | tf_op jit(solution)/shard_map/ppermute | solution.py:358
  122.5 4.1 %collective-permute-start.19 = (bf16[4,48,256]{2,1,0:T(8,128)(2,1)S(1)}, bf16[4,48,256]{2,1,0:T(8,128)(2,1)S(1)}, u32[]{:S(2)}, u32[]{:S(2)}) collective-permute-start(bf16[4,48,256]{2,1,0:T(8,128)(2,1)S(1)} %collective-permute-done.18.refs_7_), channel_id=1, source_target_pairs={{0,6},{1,7},{2,0},{3,1},{4,2},{5,3},{6,4},{7,5},{8,14},{9,15},{10,... | collective-permute-start | bytes 294920 | tf_op jit(solution)/shard_map/ppermute | solution.py:358
  126.7 0.6 reshape.74
  127.3 2.5 %stage.1.refs_8_ = bf16[4,8,8,48,256]{4,3,2,1,0:T(8,128)(2,1)S(1)} custom-call(bf16[8,8,48,256]{3,2,1,0:T(8,128)(2,1)S(1)} %copy-done.1, bf16[8,8,48,256]{3,2,1,0:T(8,128)(2,1)} %collective-permute-done.21.refs_1_, bf16[8,8,48,256]{3,2,1,0:T(8,128)(2,1)} %collective-permute-done.11.refs_2_, bf16[8,8,48,256]{3,2,1,0:T(8,128)(2,1)} %collective-permute-done.22.refs_3_), custom_call_target="tpu_custom_call" | custom-call | bytes 12582912 | tf_op jit(solution)/shard_map/stage/pallas_call | solution.py:246
  129.8 3.3 %project.1 = f32[256,2048]{1,0:T(8,128)} custom-call(s32[2]{0:T(128)S(1)} %pad_add_fusion.place, bf16[4,48,256]{2,1,0:T(8,128)(2,1)S(1)} %constant_dynamic-update-slice_fusion.refs_0_, bf16[4,48,256]{2,1,0:T(8,128)(2,1)S(1)} %collective-permute-done.14.refs_1_, bf16[4,48,256]{2,1,0:T(8,128)(2,1)S(1)} %collective-permute-done.15.refs_2_, ...), custom_call_target="tpu_custom_call" | custom-call | tf_op jit(solution)/shard_map/project/pallas_call | solution.py:285
  (35 shorter events, 0.3 us)
Async XLA Ops:
  0.6 26.7 %collective-permute-start.3 = (bf16[256,2048]{1,0:T(8,128)(2,1)}, bf16[256,2048]{1,0:T(8,128)(2,1)S(1)}, u32[]{:S(2)}, u32[]{:S(2)}) collective-permute-start(bf16[256,2048]{1,0:T(8,128)(2,1)} %refs_1_.1), channel_id=1, source_target_pairs={{0,8},{1,9},{2,10},{3,11},{4,12},{5,13},{6,14},{7,15},{8,0},{9,1},... | collective-permute-start | bytes 3145736 | tf_op jit(solution)/shard_map/ppermute | solution.py:313
  4.6 11.9 %copy-start = (bf16[256,2048]{1,0:T(8,128)(2,1)S(1)}, bf16[256,2048]{1,0:T(8,128)(2,1)}, u32[]{:S(2)}) copy-start(bf16[256,2048]{1,0:T(8,128)(2,1)} %refs_1_.1) | copy-start | bytes 3145732
  4.6 26.9 %copy-start.2 = (s32[256]{0:T(256)S(1)}, s32[256]{0:T(256)}, u32[]{:S(2)}) copy-start(s32[256]{0:T(256)} %param.8) | copy-start | bytes 3076
  4.6 26.9 %copy-start.3 = (f32[8]{0:T(128)S(1)}, f32[8]{0:T(128)}, u32[]{:S(2)}) copy-start(f32[8]{0:T(128)} %param.9) | copy-start | bytes 100
  8.0 22.9 %all-to-all-start = ((bf16[8,2,48,256]{3,2,1,0:T(8,128)(2,1)}), bf16[8,2,48,256]{3,2,1,0:T(8,128)(2,1)S(1)}, u32[]{:S(2)}, u32[]{:S(2)}) async-start(bf16[8,2,48,256]{3,2,1,0:T(8,128)(2,1)} %shift.1), calls=%async_computation | async-start | bytes 786432 | tf_op jit(solution)/shard_map/all_to_all | solution.py:324
  16.5 25.2 %collective-permute-start.4 = (bf16[256,2048]{1,0:T(8,128)(2,1)S(1)}, bf16[256,2048]{1,0:T(8,128)(2,1)S(1)}, u32[]{:S(2)}, u32[]{:S(2)}) collective-permute-start(bf16[256,2048]{1,0:T(8,128)(2,1)S(1)} %copy-done), channel_id=1, source_target_pairs={{0,16},{16,0},{32,48},{48,32},{64,80},{80,64},{96,112},{112,96},{1... | collective-permute-start | bytes 3145736 | tf_op jit(solution)/shard_map/ppermute | solution.py:314
  27.3 23.6 %collective-permute-start.5 = (bf16[256,2048]{1,0:T(8,128)(2,1)S(1)}, bf16[256,2048]{1,0:T(8,128)(2,1)}, u32[]{:S(2)}, u32[]{:S(2)}) collective-permute-start(bf16[256,2048]{1,0:T(8,128)(2,1)S(1)} %collective-permute-done.3.refs_8_.refs_9_.refs_10_.refs_11_.refs_6_.refs_7_.refs_2_), channel_id=1, source_target_pairs={{0,16},{16,0},{32,48},{48,32},{64,80},{80,64},{96,112},{112,96},{1... | collective-permute-start | bytes 3145736 | tf_op jit(solution)/shard_map/ppermute | solution.py:315
  30.9 7.9 %collective-permute-start = (bf16[8,2,48,256]{3,2,1,0:T(8,128)(2,1)S(1)}, bf16[8,2,48,256]{3,2,1,0:T(8,128)(2,1)}, u32[]{:S(2)}, u32[]{:S(2)}) collective-permute-start(bf16[8,2,48,256]{3,2,1,0:T(8,128)(2,1)S(1)} %all-to-all-done.refs_0_), channel_id=1, source_target_pairs={{0,96},{16,48},{32,0},{48,80},{64,32},{80,112},{96,64},{112,16},{1... | collective-permute-start | bytes 1179656 | tf_op jit(solution)/shard_map/ppermute | solution.py:326
  31.6 12.2 %collective-permute-start.7 = (bf16[8,2,48,256]{3,2,1,0:T(8,128)(2,1)S(1)}, bf16[8,2,48,256]{3,2,1,0:T(8,128)(2,1)}, u32[]{:S(2)}, u32[]{:S(2)}) collective-permute-start(bf16[8,2,48,256]{3,2,1,0:T(8,128)(2,1)S(1)} %all-to-all-done.refs_0_), channel_id=1, source_target_pairs={{0,128},{16,144},{32,160},{48,176},{64,192},{80,208},{96,224},{112... | collective-permute-start | bytes 1179656 | tf_op jit(solution)/shard_map/ppermute | solution.py:326
  38.7 11.3 %collective-permute-start.1 = (bf16[8,2,48,256]{3,2,1,0:T(8,128)(2,1)}, bf16[8,2,48,256]{3,2,1,0:T(8,128)(2,1)}, u32[]{:S(2)}, u32[]{:S(2)}) collective-permute-start(bf16[8,2,48,256]{3,2,1,0:T(8,128)(2,1)} %collective-permute-done.refs_2_), channel_id=1, source_target_pairs={{0,128},{16,144},{32,160},{48,176},{64,192},{80,208},{96,224},{112... | collective-permute-start | bytes 1179656 | tf_op jit(solution)/shard_map/ppermute | solution.py:326
  39.8 12.8 %collective-permute-start.9 = (bf16[8,2,48,256]{3,2,1,0:T(8,128)(2,1)S(1)}, bf16[8,2,48,256]{3,2,1,0:T(8,128)(2,1)S(1)}, u32[]{:S(2)}, u32[]{:S(2)}) collective-permute-start(bf16[8,2,48,256]{3,2,1,0:T(8,128)(2,1)S(1)} %all-to-all-done.refs_0_), channel_id=1, source_target_pairs={{0,32},{16,112},{32,64},{48,16},{64,96},{80,48},{96,0},{112,80},{1... | collective-permute-start | bytes 1179656 | tf_op jit(solution)/shard_map/ppermute | solution.py:326
  41.6 14.5 %collective-permute-start.6 = (bf16[8,2,48,256]{3,2,1,0:T(8,128)(2,1)}, bf16[8,2,48,256]{3,2,1,0:T(8,128)(2,1)S(1)}, u32[]{:S(2)}, u32[]{:S(2)}) collective-permute-start(bf16[8,2,48,256]{3,2,1,0:T(8,128)(2,1)} %collective-permute-done.refs_2_), channel_id=1, source_target_pairs={{0,96},{16,48},{32,0},{48,80},{64,32},{80,112},{96,64},{112,16},{1... | collective-permute-start | bytes 1179656 | tf_op jit(solution)/shard_map/ppermute | solution.py:326
  43.7 13.5 %collective-permute-start.8 = (bf16[8,2,48,256]{3,2,1,0:T(8,128)(2,1)}, bf16[8,2,48,256]{3,2,1,0:T(8,128)(2,1)S(1)}, u32[]{:S(2)}, u32[]{:S(2)}) collective-permute-start(bf16[8,2,48,256]{3,2,1,0:T(8,128)(2,1)} %collective-permute-done.7.refs_3_), channel_id=1, source_target_pairs={{0,32},{16,112},{32,64},{48,16},{64,96},{80,48},{96,0},{112,80},{1... | collective-permute-start | bytes 1179656 | tf_op jit(solution)/shard_map/ppermute | solution.py:326
  50.0 10.0 %collective-permute-start.2 = (bf16[8,2,48,256]{3,2,1,0:T(8,128)(2,1)}, bf16[8,2,48,256]{3,2,1,0:T(8,128)(2,1)S(1)}, u32[]{:S(2)}, u32[]{:S(2)}) collective-permute-start(bf16[8,2,48,256]{3,2,1,0:T(8,128)(2,1)} %collective-permute-done.1.refs_1_), channel_id=1, source_target_pairs={{0,96},{16,48},{32,0},{48,80},{64,32},{80,112},{96,64},{112,16},{1... | collective-permute-start | bytes 1179656 | tf_op jit(solution)/shard_map/ppermute | solution.py:326
  50.9 1.6 %collective-permute-start.10 = (f32[256]{0:T(256)S(1)}, f32[256]{0:T(256)S(1)}, u32[]{:S(2)}, u32[]{:S(2)}) collective-permute-start(f32[256]{0:T(256)S(1)} %select_reduce_fusion), channel_id=1, source_target_pairs={{0,16},{16,0},{32,48},{48,32},{64,80},{80,64},{96,112},{112,96},{1... | collective-permute-start | bytes 3080 | tf_op jit(solution)/shard_map/ppermute | solution.py:318
  62.7 64.6 %copy-start.1 = (bf16[8,8,48,256]{3,2,1,0:T(8,128)(2,1)S(1)}, bf16[8,8,48,256]{3,2,1,0:T(8,128)(2,1)}, u32[]{:S(2)}) copy-start(bf16[8,8,48,256]{3,2,1,0:T(8,128)(2,1)} %get-tuple-element.33.refs_0_) | copy-start | bytes 4718596
  62.7 43.9 %collective-permute-start.11 = (bf16[8,8,48,256]{3,2,1,0:T(8,128)(2,1)}, bf16[8,8,48,256]{3,2,1,0:T(8,128)(2,1)}, u32[]{:S(2)}, u32[]{:S(2)}) collective-permute-start(bf16[8,8,48,256]{3,2,1,0:T(8,128)(2,1)} %get-tuple-element.27), channel_id=1, source_target_pairs={{0,8},{1,9},{2,10},{3,11},{4,12},{5,13},{6,14},{7,15},{8,0},{9,1},... | collective-permute-start | bytes 4718600 | tf_op jit(solution)/shard_map/ppermute | solution.py:347
  64.4 31.2 %all-to-all-start.1 = ((f32[8,48,512]{2,1,0:T(8,128)}), f32[8,48,512]{2,1,0:T(8,128)S(1)}, u32[]{:S(2)}, u32[]{:S(2)}) async-start(f32[8,48,512]{2,1,0:T(8,128)} %bitcast.20), calls=%async_computation.1 | async-start | bytes 1572864 | tf_op jit(solution)/shard_map/all_to_all | solution.py:349
  72.6 43.4 %collective-permute-start.21 = (bf16[8,8,48,256]{3,2,1,0:T(8,128)(2,1)}, bf16[8,8,48,256]{3,2,1,0:T(8,128)(2,1)}, u32[]{:S(2)}, u32[]{:S(2)}) collective-permute-start(bf16[8,8,48,256]{3,2,1,0:T(8,128)(2,1)} %get-tuple-element.33.refs_0_), channel_id=1, source_target_pairs={{0,16},{16,0},{32,48},{48,32},{64,80},{80,64},{96,112},{112,96},{1... | collective-permute-start | bytes 4718600 | tf_op jit(solution)/shard_map/ppermute | solution.py:348
  96.5 10.1 %all-to-all-start.2 = ((f32[16,8,128]{2,1,0:T(8,128)}), f32[16,8,128]{2,1,0:T(8,128)S(1)}, u32[]{:S(2)}, u32[]{:S(2)}) async-start(f32[16,8,128]{2,1,0:T(8,128)} %get-tuple-element.28), calls=%async_computation.2 | async-start | bytes 131072 | tf_op jit(solution)/shard_map/all_to_all | solution.py:352
  101.8 1.2 collective-permute-start.12
  106.6 20.7 %collective-permute-start.22 = (bf16[8,8,48,256]{3,2,1,0:T(8,128)(2,1)}, bf16[8,8,48,256]{3,2,1,0:T(8,128)(2,1)}, u32[]{:S(2)}, u32[]{:S(2)}) collective-permute-start(bf16[8,8,48,256]{3,2,1,0:T(8,128)(2,1)} %collective-permute-done.11.refs_2_), channel_id=1, source_target_pairs={{0,16},{16,0},{32,48},{48,32},{64,80},{80,64},{96,112},{112,96},{1... | collective-permute-start | bytes 4718600 | tf_op jit(solution)/shard_map/ppermute | solution.py:354
  107.0 5.7 %collective-permute-start.13 = (bf16[2,48,256]{2,1,0:T(8,128)(2,1)S(1)}, bf16[2,48,256]{2,1,0:T(8,128)(2,1)S(1)}, u32[]{:S(2)}, u32[]{:S(2)}) collective-permute-start(bf16[2,48,256]{2,1,0:T(8,128)(2,1)S(1)} %get-tuple-element.32), channel_id=1, source_target_pairs={{0,8},{1,9},{2,10},{3,11},{4,12},{5,13},{6,14},{7,15},{8,0},{9,1},... | collective-permute-start | bytes 147464 | tf_op jit(solution)/shard_map/ppermute | solution.py:356
  112.7 8.0 %collective-permute-start.14 = (bf16[4,48,256]{2,1,0:T(8,128)(2,1)S(1)}, bf16[4,48,256]{2,1,0:T(8,128)(2,1)S(1)}, u32[]{:S(2)}, u32[]{:S(2)}) collective-permute-start(bf16[4,48,256]{2,1,0:T(8,128)(2,1)S(1)} %constant_dynamic-update-slice_fusion.refs_0_), channel_id=1, source_target_pairs={{0,1},{1,2},{2,3},{3,4},{4,5},{5,6},{6,7},{7,0},{8,9},{9,10},{10,1... | collective-permute-start | bytes 294920 | tf_op jit(solution)/shard_map/ppermute | solution.py:358
  113.2 9.3 %collective-permute-start.15 = (bf16[4,48,256]{2,1,0:T(8,128)(2,1)S(1)}, bf16[4,48,256]{2,1,0:T(8,128)(2,1)S(1)}, u32[]{:S(2)}, u32[]{:S(2)}) collective-permute-start(bf16[4,48,256]{2,1,0:T(8,128)(2,1)S(1)} %constant_dynamic-update-slice_fusion.refs_0_), channel_id=1, source_target_pairs={{0,2},{1,3},{2,4},{3,5},{4,6},{5,7},{6,0},{7,1},{8,10},{9,11},{10,... | collective-permute-start | bytes 294920 | tf_op jit(solution)/shard_map/ppermute | solution.py:358
  113.2 9.3 %collective-permute-start.18 = (bf16[4,48,256]{2,1,0:T(8,128)(2,1)S(1)}, bf16[4,48,256]{2,1,0:T(8,128)(2,1)S(1)}, u32[]{:S(2)}, u32[]{:S(2)}) collective-permute-start(bf16[4,48,256]{2,1,0:T(8,128)(2,1)S(1)} %constant_dynamic-update-slice_fusion.refs_0_), channel_id=1, source_target_pairs={{0,7},{1,0},{2,1},{3,2},{4,3},{5,4},{6,5},{7,6},{8,15},{9,8},{10,9... | collective-permute-start | bytes 294920 | tf_op jit(solution)/shard_map/ppermute | solution.py:358
  116.0 13.8 %collective-permute-start.20 = (bf16[4,48,256]{2,1,0:T(8,128)(2,1)S(1)}, bf16[4,48,256]{2,1,0:T(8,128)(2,1)S(1)}, u32[]{:S(2)}, u32[]{:S(2)}) collective-permute-start(bf16[4,48,256]{2,1,0:T(8,128)(2,1)S(1)} %constant_dynamic-update-slice_fusion.refs_0_), channel_id=1, source_target_pairs={{0,6},{1,7},{2,0},{3,1},{4,2},{5,3},{6,4},{7,5},{8,14},{9,15},{10,... | collective-permute-start | bytes 294920 | tf_op jit(solution)/shard_map/ppermute | solution.py:358
  120.7 9.2 %collective-permute-start.16 = (bf16[4,48,256]{2,1,0:T(8,128)(2,1)S(1)}, bf16[4,48,256]{2,1,0:T(8,128)(2,1)S(1)}, u32[]{:S(2)}, u32[]{:S(2)}) collective-permute-start(bf16[4,48,256]{2,1,0:T(8,128)(2,1)S(1)} %collective-permute-done.14.refs_1_), channel_id=1, source_target_pairs={{0,2},{1,3},{2,4},{3,5},{4,6},{5,7},{6,0},{7,1},{8,10},{9,11},{10,... | collective-permute-start | bytes 294920 | tf_op jit(solution)/shard_map/ppermute | solution.py:358
  122.5 7.3 %collective-permute-start.17 = (bf16[4,48,256]{2,1,0:T(8,128)(2,1)S(1)}, bf16[4,48,256]{2,1,0:T(8,128)(2,1)S(1)}, u32[]{:S(2)}, u32[]{:S(2)}) collective-permute-start(bf16[4,48,256]{2,1,0:T(8,128)(2,1)S(1)} %collective-permute-done.15.refs_2_), channel_id=1, source_target_pairs={{0,2},{1,3},{2,4},{3,5},{4,6},{5,7},{6,0},{7,1},{8,10},{9,11},{10,... | collective-permute-start | bytes 294920 | tf_op jit(solution)/shard_map/ppermute | solution.py:358
  122.5 7.3 %collective-permute-start.19 = (bf16[4,48,256]{2,1,0:T(8,128)(2,1)S(1)}, bf16[4,48,256]{2,1,0:T(8,128)(2,1)S(1)}, u32[]{:S(2)}, u32[]{:S(2)}) collective-permute-start(bf16[4,48,256]{2,1,0:T(8,128)(2,1)S(1)} %collective-permute-done.18.refs_7_), channel_id=1, source_target_pairs={{0,6},{1,7},{2,0},{3,1},{4,2},{5,3},{6,4},{7,5},{8,14},{9,15},{10,... | collective-permute-start | bytes 294920 | tf_op jit(solution)/shard_map/ppermute | solution.py:358

commit v8 on v7

--- a/solution.py
+++ b/solution.py
@@ -312,16 +312,17 @@
 
     s_hi = lax.ppermute(slices, "dom", Y_HIGH)
     s_core = lax.ppermute(slices, "orient", CORE)
+    share = y_lo * RING + x
+    own = shift_part(images, shifts.T, share, core, hi)
+    own = lax.all_to_all(own, "dom", 0, 0, axis_index_groups=Z_GROUPS)
+
+    s_hi, _ = lax.optimization_barrier((s_hi, own))
     s_both = lax.ppermute(s_hi, "orient", CORE)
     onehot = class_of[:, None] == jnp.arange(log_prior.shape[0], dtype=jnp.int32)[None, :]
     prior = jnp.sum(jnp.where(onehot, log_prior[None, :], 0.0), axis=1)
     prior = jnp.concatenate([prior, lax.ppermute(prior, "orient", CORE)])
     norms = jnp.concatenate([squares(slices) + squares(s_hi), squares(s_core) + squares(s_both)])
     bias = jnp.where(z == 0, prior, 0.0) - 0.5 * norms
-
-    share = y_lo * RING + x
-    own = shift_part(images, shifts.T, share, core, hi)
-    own = lax.all_to_all(own, "dom", 0, 0, axis_index_groups=Z_GROUPS)
 
     send = lambda block, perm: lax.ppermute(block, "orient", perm)
     behind = send(own, AHEAD)

time: 135 us -> 135 us (level)
    all_to_all x1, waiting for transfers between devices: 3.52 us -> 14.3 us  [on_device(): own = lax.all_to_all(own, 'dom', 0, 0, axis_index_groups=Z_GROUPS)]
    ppermute x1, waiting for transfers between devices: 10.8 us -> 0.01 us  [on_device(): s_hi = lax.ppermute(slices, 'dom', Y_HIGH)]
    all_to_all x1, starting transfers between devices: 8.15 us -> 6.61 us  [on_device(): lax.all_to_all(partial.reshape(HALF, rows, 2 * oris), 'dom', 0, 0, axis_i...]
  transfers between devices with their start and end apart: 26 -> 26, of which waited for: 12 -> 10; matrix products, arithmetic and copies ran while one was open for 3% -> 3% of each run, Pallas kernels for 10% -> 10%
where the time goes in v8:
time: 135 us; the launch traced here: 133 us
  waiting for transfers between devices  64.4 us (48%)
  starting transfers between devices  44.6 us (33%)
  Pallas kernels  19.3 us (14%)
  other arithmetic  3.35 us (2%)
    all_to_all x1, waiting for transfers between devices, on_device(): lax.all_to_all(partial.reshape(HALF, rows, 2 * oris), 'dom', 0, 0, axis_i...  23.1 us
    ppermute x7, waiting for transfers between devices, on_device(): send = lambda block, perm: lax.ppermute(block, 'orient', perm)  14.4 us
    all_to_all x1, waiting for transfers between devices, on_device(): own = lax.all_to_all(own, 'dom', 0, 0, axis_index_groups=Z_GROUPS)  14.3 us
    ppermute x7, starting transfers between devices, on_device(): lax.ppermute(block, ('orient', 'dom'), along_z(by))  10.3 us
    pallas_call x3, Pallas kernels, add_score(): pl.pallas_call(functools.partial(score_kernel, count), out_shape=(total,...  9.06 us
    all_to_all x1, starting transfers between devices, on_device(): own = lax.all_to_all(own, 'dom', 0, 0, axis_index_groups=Z_GROUPS)  8.48 us
    ppermute x7, starting transfers between devices, on_device(): send = lambda block, perm: lax.ppermute(block, 'orient', perm)  6.75 us
    all_to_all x1, starting transfers between devices, on_device(): lax.all_to_all(partial.reshape(HALF, rows, 2 * oris), 'dom', 0, 0, axis_i...  6.61 us
  transfers between devices with their start and end apart: 26, of which 10 were waited for; matrix products, arithmetic and copies ran while one was open for 3% of the time, Pallas kernels for 10%

profile of v8, /device:TPU:2, one launch (start us, length us, event | category | flops | bytes accessed | tf_op | source)
XLA Modules:
  0.0 133.3 jit_solution(6844046687919988269)
XLA Ops:
  0.6 3.3 %collective-permute-start.3 = (bf16[256,2048]{1,0:T(8,128)(2,1)}, bf16[256,2048]{1,0:T(8,128)(2,1)S(1)}, u32[]{:S(2)}, u32[]{:S(2)}) collective-permute-start(bf16[256,2048]{1,0:T(8,128)(2,1)} %refs_1_.1), channel_id=1, source_target_pairs={{0,8},{1,9},{2,10},{3,11},{4,12},{5,13},{6,14},{7,15},{8,0},{9,1},... | collective-permute-start | bytes 3145736 | tf_op jit(solution)/shard_map/ppermute | solution.py:313
  3.9 0.7 pad_add_fusion.1.place
  4.6 3.4 %shift.1 = bf16[8,2,48,256]{3,2,1,0:T(8,128)(2,1)} custom-call(s32[4]{0:T(128)} %pad_add_fusion.1.place, s32[2,96]{1,0:T(2,128)} %bitcast.24, bf16[96,32768]{1,0:T(8,128)(2,1)} %images.1), custom_call_target="tpu_custom_call" | custom-call | tf_op jit(solution)/shard_map/shift/pallas_call | solution.py:98
  8.0 8.5 %all-to-all-start = ((bf16[8,2,48,256]{3,2,1,0:T(8,128)(2,1)}), bf16[8,2,48,256]{3,2,1,0:T(8,128)(2,1)S(1)}, u32[]{:S(2)}, u32[]{:S(2)}) async-start(bf16[8,2,48,256]{3,2,1,0:T(8,128)(2,1)} %shift.1), calls=%async_computation | async-start | bytes 786432 | tf_op jit(solution)/shard_map/all_to_all | solution.py:317
  16.5 0.1 collective-permute-start.4
  16.6 14.3 %all-to-all-done.refs_0_ = bf16[8,2,48,256]{3,2,1,0:T(8,128)(2,1)S(1)} async-done(((bf16[8,2,48,256]{3,2,1,0:T(8,128)(2,1)}), bf16[8,2,48,256]{3,2,1,0:T(8,128)(2,1)S(1)}, u32[]{:S(2)}, u32[]{:S(2)}) %all-to-all-start) | async-done | bytes 393248 | tf_op jit(solution)/shard_map/all_to_all | solution.py:317
  30.9 0.5 collective-permute-start
  31.4 0.1 pad_add_fusion.3.place
  31.5 0.1 select_reduce_fusion
  31.6 0.7 collective-permute-start.7
  32.3 6.5 %collective-permute-done.refs_2_ = bf16[8,2,48,256]{3,2,1,0:T(8,128)(2,1)} collective-permute-done((bf16[8,2,48,256]{3,2,1,0:T(8,128)(2,1)S(1)}, bf16[8,2,48,256]{3,2,1,0:T(8,128)(2,1)}, u32[]{:S(2)}, u32[]{:S(2)}) %collective-permute-start) | collective-permute-done | bytes 393248 | tf_op jit(solution)/shard_map/ppermute | solution.py:327
  38.7 0.7 collective-permute-start.1
  39.4 0.1 pad_add_fusion.2.place
  39.5 0.3 multiply_reduce_fusion.3
  39.8 1.6 %collective-permute-start.9 = (bf16[8,2,48,256]{3,2,1,0:T(8,128)(2,1)S(1)}, bf16[8,2,48,256]{3,2,1,0:T(8,128)(2,1)S(1)}, u32[]{:S(2)}, u32[]{:S(2)}) collective-permute-start(bf16[8,2,48,256]{3,2,1,0:T(8,128)(2,1)S(1)} %all-to-all-done.refs_0_), channel_id=1, source_target_pairs={{0,32},{16,112},{32,64},{48,16},{64,96},{80,48},{96,0},{112,80},{1... | collective-permute-start | bytes 1179656 | tf_op jit(solution)/shard_map/ppermute | solution.py:327
  41.4 0.3 multiply_reduce_fusion.2
  41.7 0.6 collective-permute-start.6
  42.3 1.2 collective-permute-done.7.refs_3_
  43.5 1.7 %collective-permute-start.8 = (bf16[8,2,48,256]{3,2,1,0:T(8,128)(2,1)}, bf16[8,2,48,256]{3,2,1,0:T(8,128)(2,1)S(1)}, u32[]{:S(2)}, u32[]{:S(2)}) collective-permute-start(bf16[8,2,48,256]{3,2,1,0:T(8,128)(2,1)} %collective-permute-done.7.refs_3_), channel_id=1, source_target_pairs={{0,32},{16,112},{32,64},{48,16},{64,96},{80,48},{96,0},{112,80},{1... | collective-permute-start | bytes 1179656 | tf_op jit(solution)/shard_map/ppermute | solution.py:327
  45.2 6.7 %collective-permute-done.1.refs_1_ = bf16[8,2,48,256]{3,2,1,0:T(8,128)(2,1)} collective-permute-done((bf16[8,2,48,256]{3,2,1,0:T(8,128)(2,1)}, bf16[8,2,48,256]{3,2,1,0:T(8,128)(2,1)}, u32[]{:S(2)}, u32[]{:S(2)}) %collective-permute-start.1) | collective-permute-done | bytes 393248 | tf_op jit(solution)/shard_map/ppermute | solution.py:327
  51.9 1.0 collective-permute-start.2
  52.9 0.3 multiply_reduce_fusion.1
  53.1 0.5 collective-permute-start.10
  53.6 1.5 %multiply_reduce_fusion = f32[256]{0:T(256)S(1)} fusion(bf16[256,2048]{1,0:T(8,128)(2,1)} %collective-permute-done.5.refs_16_.refs_17_.refs_18_.refs_19_.refs_12_.refs_13_.refs_14_.refs_4_), kind=kLoop, calls=%fused_computation | loop fusion | flops 1572608 | bytes 1049600 | tf_op jit(solution)/shard_map/reduce_sum | solution.py:302
  55.2 3.6 %score.3 = (f32[384,512]{1,0:T(8,128)S(1)}, bf16[8,8,48,256]{3,2,1,0:T(8,128)(2,1)}, bf16[8,8,48,256]{3,2,1,0:T(8,128)(2,1)}) custom-call(s32[4]{0:T(128)S(1)} %pad_add_fusion.3.place, bf16[8,2,48,256]{3,2,1,0:T(8,128)(2,1)S(1)} %all-to-all-done.refs_0_, bf16[8,2,48,256]{3,2,1,0:T(8,128)(2,1)S(1)} %collective-permute-done.9.refs_1_, ...), custom_call_target="tpu_custom_call" | custom-call | tf_op jit(solution)/shard_map/score/pallas_call | solution.py:143
  58.8 2.9 %score.4 = (f32[384,512]{1,0:T(8,128)S(1)}, bf16[8,8,48,256]{3,2,1,0:T(8,128)(2,1)}, bf16[8,8,48,256]{3,2,1,0:T(8,128)(2,1)}) custom-call(s32[3]{0:T(128)S(1)} %pad_add_fusion.2.place, bf16[8,2,48,256]{3,2,1,0:T(8,128)(2,1)S(1)} %collective-permute-done.6.refs_0_, ...), custom_call_target="tpu_custom_call", output_to_operand_aliasing={{1}: (17, {}), {2}: (18, {})} | custom-call | tf_op jit(solution)/shard_map/score/pallas_call | solution.py:143
  61.7 2.6 %score.5 = (f32[384,512]{1,0:T(8,128)}, bf16[8,8,48,256]{3,2,1,0:T(8,128)(2,1)}, bf16[8,8,48,256]{3,2,1,0:T(8,128)(2,1)}) custom-call(s32[1]{0:T(128)} %bitcast.3.place, bf16[8,2,48,256]{3,2,1,0:T(8,128)(2,1)S(1)} %collective-permute-done.2.refs_0_, bf16[256,2048]{1,0:T(8,128)(2,1)S(1)} %copy-done, ...), custom_call_target="tpu_custom_call", output_to_operand_aliasing={{1}: (7, {}), {2}: (8, {})} | custom-call | tf_op jit(solution)/shard_map/score/pallas_call | solution.py:143
  64.3 1.6 %collective-permute-start.11 = (bf16[8,8,48,256]{3,2,1,0:T(8,128)(2,1)}, bf16[8,8,48,256]{3,2,1,0:T(8,128)(2,1)}, u32[]{:S(2)}, u32[]{:S(2)}) collective-permute-start(bf16[8,8,48,256]{3,2,1,0:T(8,128)(2,1)} %get-tuple-element.29), channel_id=1, source_target_pairs={{0,8},{1,9},{2,10},{3,11},{4,12},{5,13},{6,14},{7,15},{8,0},{9,1},... | collective-permute-start | bytes 4718600 | tf_op jit(solution)/shard_map/ppermute | solution.py:348
  66.0 6.6 %all-to-all-start.1 = ((f32[8,48,512]{2,1,0:T(8,128)}), f32[8,48,512]{2,1,0:T(8,128)S(1)}, u32[]{:S(2)}, u32[]{:S(2)}) async-start(f32[8,48,512]{2,1,0:T(8,128)} %bitcast.20), calls=%async_computation.1 | async-start | bytes 1572864 | tf_op jit(solution)/shard_map/all_to_all | solution.py:350
  72.6 23.1 %all-to-all-done.1.pieces = f32[8,48,512]{2,1,0:T(8,128)S(1)} async-done(((f32[8,48,512]{2,1,0:T(8,128)}), f32[8,48,512]{2,1,0:T(8,128)S(1)}, u32[]{:S(2)}, u32[]{:S(2)}) %all-to-all-start.1) | async-done | bytes 786464 | tf_op jit(solution)/shard_map/all_to_all | solution.py:350
  95.7 0.9 total.1
  96.5 5.2 %all-to-all-start.2 = ((f32[16,8,128]{2,1,0:T(8,128)}), f32[16,8,128]{2,1,0:T(8,128)S(1)}, u32[]{:S(2)}, u32[]{:S(2)}) async-start(f32[16,8,128]{2,1,0:T(8,128)} %get-tuple-element.30), calls=%async_computation.2 | async-start | bytes 131072 | tf_op jit(solution)/shard_map/all_to_all | solution.py:353
  101.8 0.1 collective-permute-start.12
  101.9 1.1 collective-permute-done.12.came
  103.0 3.6 %all-to-all-done.2.stats = f32[16,8,128]{2,1,0:T(8,128)S(1)} async-done(((f32[16,8,128]{2,1,0:T(8,128)}), f32[16,8,128]{2,1,0:T(8,128)S(1)}, u32[]{:S(2)}, u32[]{:S(2)}) %all-to-all-start.2) | async-done | bytes 65568 | tf_op jit(solution)/shard_map/all_to_all | solution.py:353
  106.6 0.1 collective-permute-start.22
  106.7 0.2 weigh.1
  107.0 1.5 %collective-permute-start.13 = (bf16[2,48,256]{2,1,0:T(8,128)(2,1)S(1)}, bf16[2,48,256]{2,1,0:T(8,128)(2,1)S(1)}, u32[]{:S(2)}, u32[]{:S(2)}) collective-permute-start(bf16[2,48,256]{2,1,0:T(8,128)(2,1)S(1)} %get-tuple-element.34), channel_id=1, source_target_pairs={{0,8},{1,9},{2,10},{3,11},{4,12},{5,13},{6,14},{7,15},{8,0},{9,1},... | collective-permute-start | bytes 147464 | tf_op jit(solution)/shard_map/ppermute | solution.py:357
  108.5 4.2 %collective-permute-done.13 = bf16[2,48,256]{2,1,0:T(8,128)(2,1)S(1)} collective-permute-done((bf16[2,48,256]{2,1,0:T(8,128)(2,1)S(1)}, bf16[2,48,256]{2,1,0:T(8,128)(2,1)S(1)}, u32[]{:S(2)}, u32[]{:S(2)}) %collective-permute-start.13) | collective-permute-done | bytes 49184 | tf_op jit(solution)/shard_map/ppermute | solution.py:357
  112.7 0.5 collective-permute-start.14
  113.2 2.8 %collective-permute-start.18 = (bf16[4,48,256]{2,1,0:T(8,128)(2,1)S(1)}, bf16[4,48,256]{2,1,0:T(8,128)(2,1)S(1)}, u32[]{:S(2)}, u32[]{:S(2)}) collective-permute-start(bf16[4,48,256]{2,1,0:T(8,128)(2,1)S(1)} %constant_dynamic-update-slice_fusion.refs_0_), channel_id=1, source_target_pairs={{0,7},{1,0},{2,1},{3,2},{4,3},{5,4},{6,5},{7,6},{8,15},{9,8},{10,9... | collective-permute-start | bytes 294920 | tf_op jit(solution)/shard_map/ppermute | solution.py:359
  116.0 2.9 %collective-permute-start.20 = (bf16[4,48,256]{2,1,0:T(8,128)(2,1)S(1)}, bf16[4,48,256]{2,1,0:T(8,128)(2,1)S(1)}, u32[]{:S(2)}, u32[]{:S(2)}) collective-permute-start(bf16[4,48,256]{2,1,0:T(8,128)(2,1)S(1)} %constant_dynamic-update-slice_fusion.refs_0_), channel_id=1, source_target_pairs={{0,6},{1,7},{2,0},{3,1},{4,2},{5,3},{6,4},{7,5},{8,14},{9,15},{10,... | collective-permute-start | bytes 294920 | tf_op jit(solution)/shard_map/ppermute | solution.py:359
  118.8 1.8 %collective-permute-done.14.refs_1_ = bf16[4,48,256]{2,1,0:T(8,128)(2,1)S(1)} collective-permute-done((bf16[4,48,256]{2,1,0:T(8,128)(2,1)S(1)}, bf16[4,48,256]{2,1,0:T(8,128)(2,1)S(1)}, u32[]{:S(2)}, u32[]{:S(2)}) %collective-permute-start.14) | collective-permute-done | bytes 98336 | tf_op jit(solution)/shard_map/ppermute | solution.py:359
  120.7 1.8 %collective-permute-done.15.refs_2_ = bf16[4,48,256]{2,1,0:T(8,128)(2,1)S(1)} collective-permute-done((bf16[4,48,256]{2,1,0:T(8,128)(2,1)S(1)}, bf16[4,48,256]{2,1,0:T(8,128)(2,1)S(1)}, u32[]{:S(2)}, u32[]{:S(2)}) %collective-permute-start.15) | collective-permute-done | bytes 98336 | tf_op jit(solution)/shard_map/ppermute | solution.py:359
  122.5 4.1 %collective-permute-start.19 = (bf16[4,48,256]{2,1,0:T(8,128)(2,1)S(1)}, bf16[4,48,256]{2,1,0:T(8,128)(2,1)S(1)}, u32[]{:S(2)}, u32[]{:S(2)}) collective-permute-start(bf16[4,48,256]{2,1,0:T(8,128)(2,1)S(1)} %collective-permute-done.18.refs_7_), channel_id=1, source_target_pairs={{0,6},{1,7},{2,0},{3,1},{4,2},{5,3},{6,4},{7,5},{8,14},{9,15},{10,... | collective-permute-start | bytes 294920 | tf_op jit(solution)/shard_map/ppermute | solution.py:359
  126.7 0.6 reshape.74
  127.3 2.5 %stage.1.refs_8_ = bf16[4,8,8,48,256]{4,3,2,1,0:T(8,128)(2,1)S(1)} custom-call(bf16[8,8,48,256]{3,2,1,0:T(8,128)(2,1)S(1)} %copy-done.1, bf16[8,8,48,256]{3,2,1,0:T(8,128)(2,1)} %collective-permute-done.21.refs_1_, bf16[8,8,48,256]{3,2,1,0:T(8,128)(2,1)} %collective-permute-done.11.refs_2_, bf16[8,8,48,256]{3,2,1,0:T(8,128)(2,1)} %collective-permute-done.22.refs_3_), custom_call_target="tpu_custom_call" | custom-call | bytes 12582912 | tf_op jit(solution)/shard_map/stage/pallas_call | solution.py:246
  129.8 3.3 %project.1 = f32[256,2048]{1,0:T(8,128)} custom-call(s32[2]{0:T(128)S(1)} %pad_add_fusion.place, bf16[4,48,256]{2,1,0:T(8,128)(2,1)S(1)} %constant_dynamic-update-slice_fusion.refs_0_, bf16[4,48,256]{2,1,0:T(8,128)(2,1)S(1)} %collective-permute-done.14.refs_1_, bf16[4,48,256]{2,1,0:T(8,128)(2,1)S(1)} %collective-permute-done.15.refs_2_, ...), custom_call_target="tpu_custom_call" | custom-call | tf_op jit(solution)/shard_map/project/pallas_call | solution.py:285
  (35 shorter events, 0.2 us)
Async XLA Ops:
  0.6 30.2 %collective-permute-start.3 = (bf16[256,2048]{1,0:T(8,128)(2,1)}, bf16[256,2048]{1,0:T(8,128)(2,1)S(1)}, u32[]{:S(2)}, u32[]{:S(2)}) collective-permute-start(bf16[256,2048]{1,0:T(8,128)(2,1)} %refs_1_.1), channel_id=1, source_target_pairs={{0,8},{1,9},{2,10},{3,11},{4,12},{5,13},{6,14},{7,15},{8,0},{9,1},... | collective-permute-start | bytes 3145736 | tf_op jit(solution)/shard_map/ppermute | solution.py:313
  4.6 11.9 %copy-start = (bf16[256,2048]{1,0:T(8,128)(2,1)S(1)}, bf16[256,2048]{1,0:T(8,128)(2,1)}, u32[]{:S(2)}) copy-start(bf16[256,2048]{1,0:T(8,128)(2,1)} %refs_1_.1) | copy-start | bytes 3145732
  4.6 26.9 %copy-start.2 = (s32[256]{0:T(256)S(1)}, s32[256]{0:T(256)}, u32[]{:S(2)}) copy-start(s32[256]{0:T(256)} %param.8) | copy-start | bytes 3076
  4.6 26.9 %copy-start.3 = (f32[8]{0:T(128)S(1)}, f32[8]{0:T(128)}, u32[]{:S(2)}) copy-start(f32[8]{0:T(128)} %param.9) | copy-start | bytes 100
  8.0 22.9 %all-to-all-start = ((bf16[8,2,48,256]{3,2,1,0:T(8,128)(2,1)}), bf16[8,2,48,256]{3,2,1,0:T(8,128)(2,1)S(1)}, u32[]{:S(2)}, u32[]{:S(2)}) async-start(bf16[8,2,48,256]{3,2,1,0:T(8,128)(2,1)} %shift.1), calls=%async_computation | async-start | bytes 786432 | tf_op jit(solution)/shard_map/all_to_all | solution.py:317
  16.5 25.2 %collective-permute-start.4 = (bf16[256,2048]{1,0:T(8,128)(2,1)S(1)}, bf16[256,2048]{1,0:T(8,128)(2,1)S(1)}, u32[]{:S(2)}, u32[]{:S(2)}) collective-permute-start(bf16[256,2048]{1,0:T(8,128)(2,1)S(1)} %copy-done), channel_id=1, source_target_pairs={{0,16},{16,0},{32,48},{48,32},{64,80},{80,64},{96,112},{112,96},{1... | collective-permute-start | bytes 3145736 | tf_op jit(solution)/shard_map/ppermute | solution.py:314
  30.9 22.3 %collective-permute-start.5 = (bf16[256,2048]{1,0:T(8,128)(2,1)S(1)}, bf16[256,2048]{1,0:T(8,128)(2,1)}, u32[]{:S(2)}, u32[]{:S(2)}) collective-permute-start(bf16[256,2048]{1,0:T(8,128)(2,1)S(1)} %collective-permute-done.3.refs_8_.refs_9_.refs_10_.refs_11_.refs_6_.refs_7_.refs_2_), channel_id=1, source_target_pairs={{0,16},{16,0},{32,48},{48,32},{64,80},{80,64},{96,112},{112,96},{1... | collective-permute-start | bytes 3145736 | tf_op jit(solution)/shard_map/ppermute | solution.py:320
  30.9 7.9 %collective-permute-start = (bf16[8,2,48,256]{3,2,1,0:T(8,128)(2,1)S(1)}, bf16[8,2,48,256]{3,2,1,0:T(8,128)(2,1)}, u32[]{:S(2)}, u32[]{:S(2)}) collective-permute-start(bf16[8,2,48,256]{3,2,1,0:T(8,128)(2,1)S(1)} %all-to-all-done.refs_0_), channel_id=1, source_target_pairs={{0,96},{16,48},{32,0},{48,80},{64,32},{80,112},{96,64},{112,16},{1... | collective-permute-start | bytes 1179656 | tf_op jit(solution)/shard_map/ppermute | solution.py:327
  31.6 11.9 %collective-permute-start.7 = (bf16[8,2,48,256]{3,2,1,0:T(8,128)(2,1)S(1)}, bf16[8,2,48,256]{3,2,1,0:T(8,128)(2,1)}, u32[]{:S(2)}, u32[]{:S(2)}) collective-permute-start(bf16[8,2,48,256]{3,2,1,0:T(8,128)(2,1)S(1)} %all-to-all-done.refs_0_), channel_id=1, source_target_pairs={{0,128},{16,144},{32,160},{48,176},{64,192},{80,208},{96,224},{112... | collective-permute-start | bytes 1179656 | tf_op jit(solution)/shard_map/ppermute | solution.py:327
  38.7 13.1 %collective-permute-start.1 = (bf16[8,2,48,256]{3,2,1,0:T(8,128)(2,1)}, bf16[8,2,48,256]{3,2,1,0:T(8,128)(2,1)}, u32[]{:S(2)}, u32[]{:S(2)}) collective-permute-start(bf16[8,2,48,256]{3,2,1,0:T(8,128)(2,1)} %collective-permute-done.refs_2_), channel_id=1, source_target_pairs={{0,128},{16,144},{32,160},{48,176},{64,192},{80,208},{96,224},{112... | collective-permute-start | bytes 1179656 | tf_op jit(solution)/shard_map/ppermute | solution.py:327
  39.8 15.4 %collective-permute-start.9 = (bf16[8,2,48,256]{3,2,1,0:T(8,128)(2,1)S(1)}, bf16[8,2,48,256]{3,2,1,0:T(8,128)(2,1)S(1)}, u32[]{:S(2)}, u32[]{:S(2)}) collective-permute-start(bf16[8,2,48,256]{3,2,1,0:T(8,128)(2,1)S(1)} %all-to-all-done.refs_0_), channel_id=1, source_target_pairs={{0,32},{16,112},{32,64},{48,16},{64,96},{80,48},{96,0},{112,80},{1... | collective-permute-start | bytes 1179656 | tf_op jit(solution)/shard_map/ppermute | solution.py:327
  41.7 17.1 %collective-permute-start.6 = (bf16[8,2,48,256]{3,2,1,0:T(8,128)(2,1)}, bf16[8,2,48,256]{3,2,1,0:T(8,128)(2,1)S(1)}, u32[]{:S(2)}, u32[]{:S(2)}) collective-permute-start(bf16[8,2,48,256]{3,2,1,0:T(8,128)(2,1)} %collective-permute-done.refs_2_), channel_id=1, source_target_pairs={{0,96},{16,48},{32,0},{48,80},{64,32},{80,112},{96,64},{112,16},{1... | collective-permute-start | bytes 1179656 | tf_op jit(solution)/shard_map/ppermute | solution.py:327
  43.5 15.3 %collective-permute-start.8 = (bf16[8,2,48,256]{3,2,1,0:T(8,128)(2,1)}, bf16[8,2,48,256]{3,2,1,0:T(8,128)(2,1)S(1)}, u32[]{:S(2)}, u32[]{:S(2)}) collective-permute-start(bf16[8,2,48,256]{3,2,1,0:T(8,128)(2,1)} %collective-permute-done.7.refs_3_), channel_id=1, source_target_pairs={{0,32},{16,112},{32,64},{48,16},{64,96},{80,48},{96,0},{112,80},{1... | collective-permute-start | bytes 1179656 | tf_op jit(solution)/shard_map/ppermute | solution.py:327
  51.9 9.8 %collective-permute-start.2 = (bf16[8,2,48,256]{3,2,1,0:T(8,128)(2,1)}, bf16[8,2,48,256]{3,2,1,0:T(8,128)(2,1)S(1)}, u32[]{:S(2)}, u32[]{:S(2)}) collective-permute-start(bf16[8,2,48,256]{3,2,1,0:T(8,128)(2,1)} %collective-permute-done.1.refs_1_), channel_id=1, source_target_pairs={{0,96},{16,48},{32,0},{48,80},{64,32},{80,112},{96,64},{112,16},{1... | collective-permute-start | bytes 1179656 | tf_op jit(solution)/shard_map/ppermute | solution.py:327
  53.1 2.0 %collective-permute-start.10 = (f32[256]{0:T(256)S(1)}, f32[256]{0:T(256)S(1)}, u32[]{:S(2)}, u32[]{:S(2)}) collective-permute-start(f32[256]{0:T(256)S(1)} %select_reduce_fusion), channel_id=1, source_target_pairs={{0,16},{16,0},{32,48},{48,32},{64,80},{80,64},{96,112},{112,96},{1... | collective-permute-start | bytes 3080 | tf_op jit(solution)/shard_map/ppermute | solution.py:323
  64.3 63.0 %copy-start.1 = (bf16[8,8,48,256]{3,2,1,0:T(8,128)(2,1)S(1)}, bf16[8,8,48,256]{3,2,1,0:T(8,128)(2,1)}, u32[]{:S(2)}) copy-start(bf16[8,8,48,256]{3,2,1,0:T(8,128)(2,1)} %get-tuple-element.35.refs_0_) | copy-start | bytes 4718596
  64.3 42.3 %collective-permute-start.11 = (bf16[8,8,48,256]{3,2,1,0:T(8,128)(2,1)}, bf16[8,8,48,256]{3,2,1,0:T(8,128)(2,1)}, u32[]{:S(2)}, u32[]{:S(2)}) collective-permute-start(bf16[8,8,48,256]{3,2,1,0:T(8,128)(2,1)} %get-tuple-element.29), channel_id=1, source_target_pairs={{0,8},{1,9},{2,10},{3,11},{4,12},{5,13},{6,14},{7,15},{8,0},{9,1},... | collective-permute-start | bytes 4718600 | tf_op jit(solution)/shard_map/ppermute | solution.py:348
  66.0 29.7 %all-to-all-start.1 = ((f32[8,48,512]{2,1,0:T(8,128)}), f32[8,48,512]{2,1,0:T(8,128)S(1)}, u32[]{:S(2)}, u32[]{:S(2)}) async-start(f32[8,48,512]{2,1,0:T(8,128)} %bitcast.20), calls=%async_computation.1 | async-start | bytes 1572864 | tf_op jit(solution)/shard_map/all_to_all | solution.py:350
  72.6 43.4 %collective-permute-start.21 = (bf16[8,8,48,256]{3,2,1,0:T(8,128)(2,1)}, bf16[8,8,48,256]{3,2,1,0:T(8,128)(2,1)}, u32[]{:S(2)}, u32[]{:S(2)}) collective-permute-start(bf16[8,8,48,256]{3,2,1,0:T(8,128)(2,1)} %get-tuple-element.35.refs_0_), channel_id=1, source_target_pairs={{0,16},{16,0},{32,48},{48,32},{64,80},{80,64},{96,112},{112,96},{1... | collective-permute-start | bytes 4718600 | tf_op jit(solution)/shard_map/ppermute | solution.py:349
  96.5 10.1 %all-to-all-start.2 = ((f32[16,8,128]{2,1,0:T(8,128)}), f32[16,8,128]{2,1,0:T(8,128)S(1)}, u32[]{:S(2)}, u32[]{:S(2)}) async-start(f32[16,8,128]{2,1,0:T(8,128)} %get-tuple-element.30), calls=%async_computation.2 | async-start | bytes 131072 | tf_op jit(solution)/shard_map/all_to_all | solution.py:353
  101.8 1.2 collective-permute-start.12
  106.6 20.7 %collective-permute-start.22 = (bf16[8,8,48,256]{3,2,1,0:T(8,128)(2,1)}, bf16[8,8,48,256]{3,2,1,0:T(8,128)(2,1)}, u32[]{:S(2)}, u32[]{:S(2)}) collective-permute-start(bf16[8,8,48,256]{3,2,1,0:T(8,128)(2,1)} %collective-permute-done.11.refs_2_), channel_id=1, source_target_pairs={{0,16},{16,0},{32,48},{48,32},{64,80},{80,64},{96,112},{112,96},{1... | collective-permute-start | bytes 4718600 | tf_op jit(solution)/shard_map/ppermute | solution.py:355
  107.0 5.7 %collective-permute-start.13 = (bf16[2,48,256]{2,1,0:T(8,128)(2,1)S(1)}, bf16[2,48,256]{2,1,0:T(8,128)(2,1)S(1)}, u32[]{:S(2)}, u32[]{:S(2)}) collective-permute-start(bf16[2,48,256]{2,1,0:T(8,128)(2,1)S(1)} %get-tuple-element.34), channel_id=1, source_target_pairs={{0,8},{1,9},{2,10},{3,11},{4,12},{5,13},{6,14},{7,15},{8,0},{9,1},... | collective-permute-start | bytes 147464 | tf_op jit(solution)/shard_map/ppermute | solution.py:357
  112.7 8.0 %collective-permute-start.14 = (bf16[4,48,256]{2,1,0:T(8,128)(2,1)S(1)}, bf16[4,48,256]{2,1,0:T(8,128)(2,1)S(1)}, u32[]{:S(2)}, u32[]{:S(2)}) collective-permute-start(bf16[4,48,256]{2,1,0:T(8,128)(2,1)S(1)} %constant_dynamic-update-slice_fusion.refs_0_), channel_id=1, source_target_pairs={{0,1},{1,2},{2,3},{3,4},{4,5},{5,6},{6,7},{7,0},{8,9},{9,10},{10,1... | collective-permute-start | bytes 294920 | tf_op jit(solution)/shard_map/ppermute | solution.py:359
  113.2 9.3 %collective-permute-start.15 = (bf16[4,48,256]{2,1,0:T(8,128)(2,1)S(1)}, bf16[4,48,256]{2,1,0:T(8,128)(2,1)S(1)}, u32[]{:S(2)}, u32[]{:S(2)}) collective-permute-start(bf16[4,48,256]{2,1,0:T(8,128)(2,1)S(1)} %constant_dynamic-update-slice_fusion.refs_0_), channel_id=1, source_target_pairs={{0,2},{1,3},{2,4},{3,5},{4,6},{5,7},{6,0},{7,1},{8,10},{9,11},{10,... | collective-permute-start | bytes 294920 | tf_op jit(solution)/shard_map/ppermute | solution.py:359
  113.2 9.3 %collective-permute-start.18 = (bf16[4,48,256]{2,1,0:T(8,128)(2,1)S(1)}, bf16[4,48,256]{2,1,0:T(8,128)(2,1)S(1)}, u32[]{:S(2)}, u32[]{:S(2)}) collective-permute-start(bf16[4,48,256]{2,1,0:T(8,128)(2,1)S(1)} %constant_dynamic-update-slice_fusion.refs_0_), channel_id=1, source_target_pairs={{0,7},{1,0},{2,1},{3,2},{4,3},{5,4},{6,5},{7,6},{8,15},{9,8},{10,9... | collective-permute-start | bytes 294920 | tf_op jit(solution)/shard_map/ppermute | solution.py:359
  116.0 13.8 %collective-permute-start.20 = (bf16[4,48,256]{2,1,0:T(8,128)(2,1)S(1)}, bf16[4,48,256]{2,1,0:T(8,128)(2,1)S(1)}, u32[]{:S(2)}, u32[]{:S(2)}) collective-permute-start(bf16[4,48,256]{2,1,0:T(8,128)(2,1)S(1)} %constant_dynamic-update-slice_fusion.refs_0_), channel_id=1, source_target_pairs={{0,6},{1,7},{2,0},{3,1},{4,2},{5,3},{6,4},{7,5},{8,14},{9,15},{10,... | collective-permute-start | bytes 294920 | tf_op jit(solution)/shard_map/ppermute | solution.py:359
  120.7 9.1 %collective-permute-start.16 = (bf16[4,48,256]{2,1,0:T(8,128)(2,1)S(1)}, bf16[4,48,256]{2,1,0:T(8,128)(2,1)S(1)}, u32[]{:S(2)}, u32[]{:S(2)}) collective-permute-start(bf16[4,48,256]{2,1,0:T(8,128)(2,1)S(1)} %collective-permute-done.14.refs_1_), channel_id=1, source_target_pairs={{0,2},{1,3},{2,4},{3,5},{4,6},{5,7},{6,0},{7,1},{8,10},{9,11},{10,... | collective-permute-start | bytes 294920 | tf_op jit(solution)/shard_map/ppermute | solution.py:359
  122.5 7.3 %collective-permute-start.17 = (bf16[4,48,256]{2,1,0:T(8,128)(2,1)S(1)}, bf16[4,48,256]{2,1,0:T(8,128)(2,1)S(1)}, u32[]{:S(2)}, u32[]{:S(2)}) collective-permute-start(bf16[4,48,256]{2,1,0:T(8,128)(2,1)S(1)} %collective-permute-done.15.refs_2_), channel_id=1, source_target_pairs={{0,2},{1,3},{2,4},{3,5},{4,6},{5,7},{6,0},{7,1},{8,10},{9,11},{10,... | collective-permute-start | bytes 294920 | tf_op jit(solution)/shard_map/ppermute | solution.py:359
  122.5 7.3 %collective-permute-start.19 = (bf16[4,48,256]{2,1,0:T(8,128)(2,1)S(1)}, bf16[4,48,256]{2,1,0:T(8,128)(2,1)S(1)}, u32[]{:S(2)}, u32[]{:S(2)}) collective-permute-start(bf16[4,48,256]{2,1,0:T(8,128)(2,1)S(1)} %collective-permute-done.18.refs_7_), channel_id=1, source_target_pairs={{0,6},{1,7},{2,0},{3,1},{4,2},{5,3},{6,4},{7,5},{8,14},{9,15},{10,... | collective-permute-start | bytes 294920 | tf_op jit(solution)/shard_map/ppermute | solution.py:359
